TPU v7x, 32 devices: a whole 2x2x4 slice. The times are simulated.
32 devices in a mesh: tm: 16 (over z, x, core), head: 2 (over y).
Axes of the slice: x: 2, y: 2, z: 4, core: 2. Of those that a mesh axis runs over, the one named last changes fastest.
Arguments:
- query_states: bfloat16 [24576, 1024], P('tm', 'head'), may hold values from -30 to 30
- key_states: bfloat16 [24576, 1024], P('tm', 'head'), may hold values from -30 to 30
- value_states: bfloat16 [24576, 1024], P('tm', 'head'), may hold values from -6 to 6
- win_start: int32 [32], P('tm'), may hold values from 0 to 30, as said below
- group_end: int32 [32], P('tm'), may hold values from 0 to 31, as said below
- out_weight: bfloat16 [1024, 1536], replicated, may hold values from -0.1875 to 0.1875
Outputs:
- projected: bfloat16 [24576, 1536], P(('tm', 'head'))
Inputs may be any that keep to these rules, and one draw needn't show every extreme that they name: For every frame f, win_start[f] = max(f - lag, 0) with a lag of 1 to 3; frame 32 - 2 has a lag of 3 in every draw, and the last frame has a lag of 1. `group_end`: frames 2p and 2p + 1 form one group (both end at 2p + 1) or two groups of one frame (each ends at itself); both kinds occur in every draw.
All inputs are finite; a program needn't handle non-finite values.
Results may differ from a plain program's by a relative error of at most 0.0051.
Values may be sent and summed in bfloat16 or wider, within the bound.
No kernel may reach another device: no remote copies, remote signals or barrier semaphores. Data moves between devices by JAX's collectives and lax.ppermute only.
A program may use at most 384 MiB of HBM per device.

v0:
```python
import functools

import jax
import jax.numpy as jnp
from jax import lax
from jax.experimental import pallas as pl
from jax.experimental.pallas import tpu as pltpu
from jax.sharding import PartitionSpec as P

HD = 128
FT = 768
BK = 256
LOG2E = 1.4426950408889634
SCALE = HD ** -0.5 * LOG2E
LIMIT = 1e30
HIDDEN = 1e30
PARAMS = pltpu.CompilerParams(vmem_limit_bytes=24 * 1024 * 1024)
ANY_SPEC = pl.BlockSpec(memory_space=pl.ANY)
COST = pl.CostEstimate(flops=1000, bytes_accessed=1000, transcendentals=0)
TOKEN = jax.ShapeDtypeStruct((8, 128), jnp.float32)


def dot(a, b):
    return jnp.dot(a, b, preferred_element_type=jnp.float32)


def span(start, size):
    return pl.ds(pl.multiple_of(start, size), size)


def rows_of(slot):
    return slice(slot * FT, (slot + 1) * FT)


def extended_scores(q, kt, j):
    return dot(q, kt[:, j * BK : (j + 1) * BK])


def add_frame(lanes, kt, values):
    units = [(n, j) for n in range(len(lanes)) for j in range(FT // BK)]

    def fetch(unit):
        n, j = unit
        return extended_scores(lanes[n][0], kt, j)

    ahead = fetch(units[0])
    weights = []
    for at, (n, j) in enumerate(units):
        s = ahead
        if at + 1 < len(units):
            ahead = fetch(units[at + 1])
        _, shift, add = lanes[n]
        for c in range(0, BK, HD):
            weights.append(jnp.exp2(s[:, c : c + HD] * SCALE - shift).astype(jnp.bfloat16))
        if j == FT // BK - 1:
            add(dot(jnp.concatenate(weights, axis=1), values[...]))
            weights = []


def visible(info, slot, frame):
    return (frame >= 1) & (frame >= info[2 + slot]) & (frame <= info[4 + slot])


def lanes_of(h, heads):
    share = HD // heads
    lane = lax.broadcasted_iota(jnp.int32, (1, HD), 1)
    return (lane >= h * share) & (lane < (h + 1) * share)


def spread(packed, h, heads):
    row = lax.broadcasted_iota(jnp.int32, (HD, HD), 0)
    chosen = jnp.where(row == h * (HD // heads), 1.0, 0.0).astype(jnp.bfloat16)
    return dot(packed, chosen)


def spread_sum(packed, h, heads):
    high = packed.astype(jnp.bfloat16)
    low = (packed - high.astype(jnp.float32)).astype(jnp.bfloat16)
    return spread(high, h, heads) + spread(low, h, heads)


def sums_into(acc_from, acc, sums, rows, column, h, heads):
    def add(added):
        new = added[:, :HD]
        acc[rows, column] = new if acc_from is None else acc_from[rows, column] + new
        old = sums[rows, :]
        sums[rows, :] = jnp.where(lanes_of(h, heads), old + added[:, HD:], old)

    return add


def load_frame(kt, values, k, v, column):
    kt[...] = k[:, column].T
    values[:, :HD] = v[:, column]


def each_head(group, turn):
    offset, count = group

    def body(h, carry):
        turn(h, span(h * HD, HD), span((h + offset) * HD, HD))
        return carry

    lax.fori_loop(0, count, body, 0)


def own_kernel(group, info, q, k, v, *refs):
    m, acc, sums, token, kt, values = refs[-6:]
    if len(refs) > 6:
        refs[0][...] = v[...]
    heads = group[1]
    first = info[0]
    token[...] = jnp.zeros_like(token)
    values[:, HD:] = jnp.ones((FT, HD), jnp.bfloat16)
    ones = jnp.ones((HD, HD), jnp.bfloat16)
    m[...] = jnp.zeros_like(m)
    sums[...] = jnp.zeros_like(sums)

    def turn(h, column, wide):
        here = lanes_of(h, heads)
        for slot in (0, 1):
            rows = rows_of(slot)
            product = q[rows, wide].astype(jnp.float32) * k[rows, wide].astype(jnp.float32)
            own = (dot(product.astype(jnp.bfloat16), ones) * SCALE).astype(jnp.bfloat16)
            m[rows, :] = jnp.where(here, own, m[rows, :])
        for frame in (0, 1):
            load_frame(kt, values, k.at[rows_of(frame)], v.at[rows_of(frame)], wide)
            lanes = []
            for slot in (0, 1):
                rows = rows_of(slot)
                shift = spread(m[rows, :], h, heads)
                shift = jnp.where(visible(info, slot, first + frame), shift, HIDDEN)
                acc_from = acc if frame else None
                add = sums_into(acc_from, acc, sums, rows, column, h, heads)
                lanes.append((q[rows, wide], shift, add))
            add_frame(lanes, kt, values)

    each_head(group, turn)


def near_kernel(group, info, q, m, acc_in, sums_in, near_k, near_v, *refs):
    acc, sums, kt, values, k_buf, v_buf, sem = refs
    offset, heads = group
    first = info[0]
    order = (1, 0)
    copies = {
        frame: [
            pltpu.make_async_copy(
                source.at[pl.ds(frame * FT, FT), pl.ds(offset * HD, heads * HD)],
                buf.at[frame],
                sem.at[frame, n],
            )
            for n, (source, buf) in enumerate(((near_k, k_buf), (near_v, v_buf)))
        ]
        for frame in order
    }
    for frame in order:
        for copy in copies[frame]:
            copy.start()
    values[:, HD:] = jnp.ones((FT, HD), jnp.bfloat16)
    sums[...] = sums_in[...]
    for frame in order:
        for copy in copies[frame]:
            copy.wait()

        def turn(h, column, wide):
            load_frame(kt, values, k_buf.at[frame], v_buf.at[frame], column)
            acc_from = acc_in if frame == order[0] else acc
            lanes = []
            for slot in (0, 1):
                rows = rows_of(slot)
                shift = spread(m[rows, :], h, heads)
                shift = jnp.where(visible(info, slot, first - 2 + frame), shift, HIDDEN)
                add = sums_into(acc_from, acc, sums, rows, column, h, heads)
                lanes.append((q[rows, wide], shift, add))
            add_frame(lanes, kt, values)

        each_head(group, turn)


def final_kernel(
    group, info, q, m, acc_in, sums_in,
    sink_a, sink_b, far, relay_k, relay_v, key_any, value_any, near_k, near_v, *refs,
):
    outs = refs[:-8]
    kt, values, k_buf, v_buf, acc, shift, largest, sem = refs[-8:]
    first = info[0]
    core = info[6]
    far_seen = visible(info, 0, first - 3)
    offset, heads = group
    group_columns = pl.ds(offset * HD, heads * HD)
    values[:, HD:] = jnp.ones((FT, HD), jnp.bfloat16)

    def copies(frame, k, k_row, v, v_row, columns):
        return [
            pltpu.make_async_copy(
                source.at[pl.ds(row, FT), columns], buf.at[frame], sem.at[frame, n]
            )
            for n, (source, row, buf) in enumerate(((k, k_row, k_buf), (v, v_row, v_buf)))
        ]

    arriving = {
        0: [
            (0, sink_a, 0, sink_b, 0, group_columns),
            (1, far, 0, far, FT, group_columns),
        ],
        1: [
            (0, sink_b, 0, sink_a, 0, group_columns),
            (1, relay_k, FT, relay_v, FT, group_columns),
        ],
    }
    for which, listed in arriving.items():

        @pl.when(core == which)
        def _():
            started = [copies(*entry) for entry in listed]
            for act in (lambda copy: copy.start(), lambda copy: copy.wait()):
                for pair in started:
                    for copy in pair:
                        act(copy)

    def write(slot, h, acc, total):
        attended = (acc / total).astype(jnp.bfloat16)
        column = span(h * HD, HD)
        if len(outs) == 1:
            outs[0][rows_of(slot), column] = attended
        else:

            @pl.when(info[1] == slot)
            def _():
                outs[0][:, column] = attended

            @pl.when(info[1] != slot)
            def _():
                outs[1][:, column] = attended

    def turn(h, column, wide):
        results = {}

        def keep(slot):
            def add(added):
                results[slot] = results[slot] + added if slot in results else added

            return add

        shifts = [spread(m[rows_of(slot), :], h, heads) for slot in (0, 1)]
        load_frame(kt, values, k_buf.at[0], v_buf.at[0], column)
        add_frame(
            [(q[rows_of(slot), wide], shifts[slot], keep(slot)) for slot in (1, 0)], kt, values
        )
        load_frame(kt, values, k_buf.at[1], v_buf.at[1], column)
        shown = jnp.where(far_seen, shifts[0], HIDDEN)
        add_frame([(q[rows_of(0), wide], shown, keep(0))], kt, values)
        for slot in (0, 1):
            rows = rows_of(slot)
            total = spread_sum(sums_in[rows, :], h, heads) + results[slot][:, HD:]
            write(slot, h, acc_in[rows, column] + results[slot][:, :HD], total)
            largest[h, slot] = jnp.max(total)

    each_head(group, turn)

    def again(slot, h, wide):
        here, there = core == 0, core == 1
        sources = [(here, sink_a, 0, sink_b, 0), (there, sink_b, 0, sink_a, 0)]
        if slot == 0:
            sources += [
                (far_seen & here, far, 0, far, FT), (far_seen & there, relay_k, FT, relay_v, FT)
            ]
        for frame in (0, 1):
            row = frame * FT
            own = visible(info, slot, first + frame)
            sources.append((own, key_any, row, value_any, row))
            behind = visible(info, slot, first - 2 + frame)
            sources.append((behind, near_k, row, near_v, row))
        one = (k_buf.at[0, :, :HD], v_buf.at[0, :, :HD])

        def sweep(step):
            def visit(t, carry):
                seen = False
                for n, (shown, k, k_row, v, v_row) in enumerate(sources):
                    chosen = (t == n) & shown
                    seen = seen | chosen

                    @pl.when(chosen)
                    def _():
                        for n, (ref, row) in enumerate(((k, k_row), (v, v_row))):
                            copy = pltpu.make_async_copy(
                                ref.at[pl.ds(row, FT), wide], one[n], sem.at[0, n]
                            )
                            copy.start()
                            copy.wait()

                @pl.when(seen)
                def _():
                    load_frame(kt, values, k_buf.at[0], v_buf.at[0], slice(0, HD))
                    step()

                return carry

            lax.fori_loop(0, len(sources), visit, 0)

        queries = q[rows_of(slot), wide]

        def peak():
            for j in range(FT // BK):
                most = jnp.max(extended_scores(queries, kt, j), axis=1, keepdims=True) * SCALE
                shift[...] = jnp.maximum(shift[...], most)

        def more(added):
            acc[...] = acc[...] + added

        shift[...] = jnp.full((FT, HD), -jnp.inf, jnp.float32)
        acc[...] = jnp.zeros((FT, 2 * HD), jnp.float32)
        sweep(peak)
        sweep(lambda: add_frame([(queries, shift[...], more)], kt, values))
        write(slot, h, acc[:, :HD], acc[:, HD:])

    def check(h, column, wide):
        for slot in (0, 1):
            in_range = largest[h, slot] < LIMIT
            pl.when(jnp.logical_not(in_range))(lambda slot=slot: again(slot, h, wide))

    each_head(group, check)


VMEM_SPEC = pl.BlockSpec(memory_space=pltpu.VMEM)
SMEM_SPEC = pl.BlockSpec(memory_space=pltpu.SMEM)


def stage(kernel, arrays, in_any, outs, scratch):
    return pl.pallas_call(
        kernel,
        in_specs=[SMEM_SPEC] + [VMEM_SPEC] * (len(arrays) - in_any - 1) + [ANY_SPEC] * in_any,
        out_specs=[VMEM_SPEC] * len(outs),
        scratch_shapes=[
            pltpu.VMEM((HD, FT), jnp.bfloat16), pltpu.VMEM((FT, 2 * HD), jnp.bfloat16)
        ] + list(scratch),
        out_shape=outs,
        compiler_params=PARAMS,
        cost_estimate=COST,
    )(*arrays)


def last_frames(keys, values):
    return jnp.concatenate([keys[FT:], values[FT:]], axis=0)


def sink_steps(size):
    bits = [1 << b for b in range(1, size.bit_length() - 1)]
    orders = (bits[::-1], [bits[0]] + bits[:0:-1])
    done = [0, 0]
    steps = []
    for step in range(len(bits)):
        pairs = []
        for which in (0, 1):
            bit = orders[which][step]
            holders = [i for i in range(0, size, 2) if i & ~done[which] == 0]
            pairs += [(i + which, (i | bit) + which) for i in holders]
            done[which] |= bit
        steps.append(pairs)
    return steps


def project(info, parts, weight):
    columns = weight.shape[1]
    turns = 6
    block = columns // turns
    rows, depth = parts[0][0].shape
    n = len(parts)

    def kernel(info, *refs):
        weight, out = refs[n:]
        column = span(pl.program_id(0) * block, block)
        total = None
        for a, (_, place, received) in zip(refs[:n], parts):
            owner = 1 - info[1] if received else info[1]
            first = owner * (weight.shape[0] // 2) + place * depth
            product = dot(a[...], weight[span(first, depth), column])
            total = product if total is None else total + product
        out[...] = total.astype(jnp.bfloat16)

    return pl.pallas_call(
        kernel,
        grid=(turns,),
        in_specs=[SMEM_SPEC] + [VMEM_SPEC] * (n + 1),
        out_specs=pl.BlockSpec((rows, block), lambda i: (0, i)),
        out_shape=jax.ShapeDtypeStruct((rows, columns), jnp.bfloat16),
        compiler_params=PARAMS,
        cost_estimate=COST,
    )(info, *[a for a, _, _ in parts], weight)


def local(query_states, key_states, value_states, win_start, group_end, out_weight):
    axis = "tm"
    size = lax.axis_size(axis)
    paired = lax.axis_size("head") == 2
    me = lax.axis_index(axis)
    core = me % 2
    heads = query_states.shape[1] // HD
    info = jnp.concatenate(
        [
            jnp.stack([me * 2, lax.axis_index("head")]).astype(jnp.int32),
            win_start.astype(jnp.int32),
            group_end.astype(jnp.int32),
            jnp.stack([core]).astype(jnp.int32),
        ]
    )
    groups = [(0, heads // 2), (heads // 2, heads // 2)] if heads % 2 == 0 else [(0, heads)]
    rows, width = query_states.shape
    q_like = jax.ShapeDtypeStruct((rows, width), jnp.bfloat16)
    group_width = groups[0][1] * HD
    m_like = jax.ShapeDtypeStruct((rows, HD), jnp.bfloat16)
    acc_like = jax.ShapeDtypeStruct((rows, group_width), jnp.float32)
    sums_like = jax.ShapeDtypeStruct((rows, HD), jnp.float32)
    frame_buffers = [pltpu.VMEM((2, FT, group_width), jnp.bfloat16)] * 2
    dma_sems = pltpu.SemaphoreType.DMA((2, 2))

    onward = [(i, i + 1) for i in range(size - 1)]
    near_k = lax.ppermute(key_states, axis, onward)
    moved = lax.ppermute(value_states, axis, [(0, 1)])
    held = jnp.where(core == 0, key_states[:FT], moved[:FT])
    own_last = last_frames(key_states, value_states)
    far = lax.ppermute(own_last, axis, [(i, i + 2) for i in range(0, size - 2, 2)])

    states = []
    for step, pairs in enumerate(sink_steps(size)):
        moved = lax.ppermute(held, axis, pairs)
        takes = jnp.zeros((), bool)
        for _, target in pairs:
            takes = takes | (me == target)
        if step < len(groups):
            *passed, m, acc, sums, token = stage(
                functools.partial(own_kernel, groups[step]),
                [info, query_states, key_states, value_states], 0,
                [q_like] * (step == 0) + [m_like, acc_like, sums_like, TOKEN], [],
            )
            states.append((m, acc, sums))
            takes = takes & (token[0, 0] == 0)
            if step == 0:
                near_v = lax.ppermute(passed[0], axis, onward)
        held = jnp.where(takes, moved, held)
    other = lax.ppermute(held, axis, [(i, i ^ 1) for i in range(size)])
    on_chip = [(i, i + 1) for i in range(0, size, 2)]
    relay_k = lax.ppermute(near_k, axis, on_chip)
    relay_v = lax.ppermute(near_v, axis, on_chip)

    for g, group in enumerate(groups):
        m, acc, sums = states[g]
        acc, sums = stage(
            functools.partial(near_kernel, group),
            [info, query_states, m, acc, sums, near_k, near_v], 2, [acc_like, sums_like],
            frame_buffers + [dma_sems],
        )
        states[g] = m, acc, sums
    mine, theirs = [], []
    for g, group in enumerate(groups):
        part = jax.ShapeDtypeStruct((FT if paired else rows, group_width), jnp.bfloat16)
        results = stage(
            functools.partial(final_kernel, group),
            [info, query_states, *states[g], held, other, far, relay_k, relay_v,
             key_states, value_states, near_k, near_v], 9,
            [part] * (2 if paired else 1),
            frame_buffers + [
                pltpu.VMEM((FT, 2 * HD), jnp.float32),
                pltpu.VMEM((FT, HD), jnp.float32),
                pltpu.SMEM((group[1], 2), jnp.float32),
                dma_sems,
            ],
        )
        mine.append(results[0])
        if paired:
            theirs.append(lax.ppermute(results[1], "head", [(0, 1), (1, 0)]))
    if not paired:
        attended = jnp.concatenate(mine, axis=1)
        token_rows = lax.all_to_all(attended, "head", split_axis=0, concat_axis=1, tiled=True)
        return dot(token_rows, out_weight).astype(jnp.bfloat16)
    parts = [(array, g, False) for g, array in enumerate(mine)]
    parts += [(array, g, True) for g, array in enumerate(theirs)]
    return project(info, parts, out_weight)


def solution(mesh):
    in_specs = (P("tm", "head"), P("tm", "head"), P("tm", "head"), P("tm"), P("tm"), P())
    out_specs = P(("tm", "head"), None)
    return jax.shard_map(local, mesh=mesh, in_specs=in_specs, out_specs=out_specs, check_vma=False)
```

profile of v0, /device:TPU:18, one launch (start us, length us, event | category | flops | bytes accessed | tf_op | source)
XLA Modules:
  0.0 128.7 jit_solution(686045245870273293)
XLA Ops:
  0.0 1.9 %collective-permute-start.2 = (bf16[1536,512]{1,0:T(8,128)(2,1)}, bf16[1536,512]{1,0:T(8,128)(2,1)}, u32[]{:S(2)}, u32[]{:S(2)}) collective-permute-start(bf16[1536,512]{1,0:T(8,128)(2,1)} %value_any.3), channel_id=1, source_target_pairs={{0,2},{1,3}} | collective-permute-start | bytes 4718600 | tf_op jit(solution)/shard_map/ppermute | solution.py:420
  1.9 3.1 %fusion = (bf16[768,512]{1,0:T(8,128)(2,1)}, bf16[768,512]{1,0:T(8,128)(2,1)}) fusion(bf16[1536,512]{1,0:T(8,128)(2,1)} %key_any.3, bf16[1536,512]{1,0:T(8,128)(2,1)} %collective-permute-done.2, pred[]{:T(512)S(6)} %eq.77), kind=kLoop, calls=%fused_computation.5 | loop fusion | flops 393216 | bytes 3932161 | tf_op jit(solution)/shard_map/slice | solution.py:345
  4.9 1.6 %collective-permute-start.3 = (bf16[768,512]{1,0:T(8,128)(2,1)}, bf16[768,512]{1,0:T(8,128)(2,1)}, u32[]{:S(2)}, u32[]{:S(2)}) collective-permute-start(bf16[768,512]{1,0:T(8,128)(2,1)} %get-tuple-element.40), channel_id=1, source_target_pairs={{0,16},{2,6},{1,17},{3,7}} | collective-permute-start | bytes 2359304 | tf_op jit(solution)/shard_map/ppermute | solution.py:427
  6.5 1.9 %collective-permute-start = (bf16[1536,512]{1,0:T(8,128)(2,1)S(1)}, bf16[1536,512]{1,0:T(8,128)(2,1)}, u32[]{:S(2)}, u32[]{:S(2)}) collective-permute-start(bf16[1536,512]{1,0:T(8,128)(2,1)S(1)} %copy-done.1), channel_id=1, source_target_pairs={{0,2},{2,4},{4,6},{6,8},{8,10},{10,12},{12,14},{14,16},{16,18},{18... | collective-permute-start | bytes 4718600 | tf_op jit(solution)/shard_map/ppermute | solution.py:419
  8.5 1.4 %copy-done.2 = bf16[1536,512]{1,0:T(8,128)(2,1)S(1)} copy-done((bf16[1536,512]{1,0:T(8,128)(2,1)S(1)}, bf16[1536,512]{1,0:T(8,128)(2,1)}, u32[]{:S(2)}) %copy-start.2) | copy-done | bytes 1572888
  10.0 7.2 %shard_map.64 = (bf16[1536,512]{1,0:T(8,128)(2,1)}, bf16[1536,128]{1,0:T(8,128)(2,1)S(1)}, f32[1536,256]{1,0:T(8,128)S(1)}, f32[1536,128]{1,0:T(8,128)S(1)}, f32[8,128]{1,0:T(8,128)S(1)}) custom-call(s32[7]{0:T(128)S(1)} %concatenate.6.info, bf16[1536,512]{1,0:T(8,128)(2,1)S(1)} %copy-done, bf16[1536,512]{1,0:T(8,128)(2,1)S(1)} %copy-done.1, ...), custom_call_target="tpu_custom_call" | custom-call | flops 1000 | bytes 1000 | tf_op jit(solution)/shard_map/pallas_call | solution.py:331
  19.2 3.5 %collective-permute-start.1 = (bf16[1536,512]{1,0:T(8,128)(2,1)}, bf16[1536,512]{1,0:T(8,128)(2,1)}, u32[]{:S(2)}, u32[]{:S(2)}) collective-permute-start(bf16[1536,512]{1,0:T(8,128)(2,1)} %get-tuple-element.25), channel_id=1, source_target_pairs={{0,2},{2,4},{4,6},{6,8},{8,10},{10,12},{12,14},{14,16},{16,18},{18... | collective-permute-start | bytes 4718600 | tf_op jit(solution)/shard_map/ppermute | solution.py:440
  24.0 2.2 %broadcast_select_fusion = bf16[768,512]{1,0:T(8,128)(2,1)} fusion(bf16[768,512]{1,0:T(8,128)(2,1)} %collective-permute-done.3, bf16[768,512]{1,0:T(8,128)(2,1)} %get-tuple-element.40, pred[]{:T(512)S(6)} %and.15), kind=kLoop, calls=%fused_computation.2 | loop fusion | flops 393216 | bytes 2359297 | tf_op jit(solution)/shard_map/jit(_where)/select_n | solution.py:441
  26.3 1.6 %collective-permute-start.4 = (bf16[768,512]{1,0:T(8,128)(2,1)}, bf16[768,512]{1,0:T(8,128)(2,1)}, u32[]{:S(2)}, u32[]{:S(2)}) collective-permute-start(bf16[768,512]{1,0:T(8,128)(2,1)} %broadcast_select_fusion), channel_id=1, source_target_pairs={{0,8},{16,24},{2,18},{6,22},{1,9},{17,25},{3,19},{7,23}} | collective-permute-start | bytes 2359304 | tf_op jit(solution)/shard_map/ppermute | solution.py:427
  27.9 7.1 %shard_map.66 = (bf16[1536,128]{1,0:T(8,128)(2,1)S(1)}, f32[1536,256]{1,0:T(8,128)S(1)}, f32[1536,128]{1,0:T(8,128)S(1)}, f32[8,128]{1,0:T(8,128)S(1)}) custom-call(s32[7]{0:T(128)S(1)} %concatenate.6.info, bf16[1536,512]{1,0:T(8,128)(2,1)S(1)} %copy-done, bf16[1536,512]{1,0:T(8,128)(2,1)S(1)} %copy-done.1, bf16[1536,512]{1,0:T(8,128)(2,1)S(1)} %copy-done.3), custom_call_target="tpu_custom_call" | custom-call | flops 1000 | bytes 1000 | tf_op jit(solution)/shard_map/pallas_call | solution.py:331
  39.0 2.3 %broadcast_select_fusion.1 = bf16[768,512]{1,0:T(8,128)(2,1)} fusion(bf16[768,512]{1,0:T(8,128)(2,1)} %collective-permute-done.4, bf16[768,512]{1,0:T(8,128)(2,1)} %broadcast_select_fusion, pred[]{:T(512)S(6)} %and.14), kind=kLoop, calls=%fused_computation.3 | loop fusion | flops 393216 | bytes 2359297 | tf_op jit(solution)/shard_map/jit(_where)/select_n | solution.py:441
  42.6 1.3 %pad_maximum_fusion = bf16[1536,512]{1,0:T(8,128)(2,1)} fusion(bf16[768,512]{1,0:T(8,128)(2,1)S(1)} %slice.23, bf16[768,512]{1,0:T(8,128)(2,1)S(1)} %copy-done.17), kind=kLoop, calls=%fused_computation | loop fusion | flops 3145728 | bytes 3145728 | tf_op jit(solution)/shard_map/concatenate | solution.py:345
  43.9 5.5 %collective-permute-start.7 = (bf16[1536,512]{1,0:T(8,128)(2,1)}, bf16[1536,512]{1,0:T(8,128)(2,1)}, u32[]{:S(2)}, u32[]{:S(2)}) collective-permute-start(bf16[1536,512]{1,0:T(8,128)(2,1)} %pad_maximum_fusion), channel_id=1, source_target_pairs={{0,4},{4,8},{8,12},{12,16},{16,20},{20,24},{24,28},{1,5},{5,9},{9,... | collective-permute-start | bytes 4718600 | tf_op jit(solution)/shard_map/ppermute | solution.py:423
  49.5 14.4 %collective-permute-start.8 = (bf16[1536,512]{1,0:T(8,128)(2,1)}, bf16[1536,512]{1,0:T(8,128)(2,1)}, u32[]{:S(2)}, u32[]{:S(2)}) collective-permute-start(bf16[1536,512]{1,0:T(8,128)(2,1)} %collective-permute-done.near_k), channel_id=1, source_target_pairs={{0,2},{4,6},{8,10},{12,14},{16,18},{20,22},{24,26},{28,30},{1,3},{... | collective-permute-start | bytes 4718600 | tf_op jit(solution)/shard_map/ppermute | solution.py:444
  63.9 2.4 %collective-permute-start.9 = (bf16[1536,512]{1,0:T(8,128)(2,1)}, bf16[1536,512]{1,0:T(8,128)(2,1)}, u32[]{:S(2)}, u32[]{:S(2)}) collective-permute-start(bf16[1536,512]{1,0:T(8,128)(2,1)} %collective-permute-done.1.near_v), channel_id=1, source_target_pairs={{0,2},{4,6},{8,10},{12,14},{16,18},{20,22},{24,26},{28,30},{1,3},{... | collective-permute-start | bytes 4718600 | tf_op jit(solution)/shard_map/ppermute | solution.py:445
  66.3 1.4 %broadcast_select_fusion.2.sink_a = bf16[768,512]{1,0:T(8,128)(2,1)S(1)} fusion(bf16[768,512]{1,0:T(8,128)(2,1)} %collective-permute-done.5, bf16[768,512]{1,0:T(8,128)(2,1)} %broadcast_select_fusion.1, pred[]{:T(512)S(6)} %or.39), kind=kLoop, calls=%fused_computation.4 | loop fusion | flops 393216 | bytes 2359297 | tf_op jit(solution)/shard_map/jit(_where)/select_n | solution.py:441
  67.7 8.0 %collective-permute-start.6 = (bf16[768,512]{1,0:T(8,128)(2,1)S(1)}, bf16[768,512]{1,0:T(8,128)(2,1)S(1)}, u32[]{:S(2)}, u32[]{:S(2)}) collective-permute-start(bf16[768,512]{1,0:T(8,128)(2,1)S(1)} %broadcast_select_fusion.2.sink_a), channel_id=1, source_target_pairs={{0,2},{2,0},{4,6},{6,4},{8,10},{10,8},{12,14},{14,12},{16,18},{18,... | collective-permute-start | bytes 2359304 | tf_op jit(solution)/shard_map/ppermute | solution.py:442
  76.9 8.2 %shard_map.68 = (f32[1536,256]{1,0:T(8,128)S(1)}, f32[1536,128]{1,0:T(8,128)S(1)}) custom-call(s32[7]{0:T(128)S(1)} %concatenate.6.info, bf16[1536,512]{1,0:T(8,128)(2,1)S(1)} %copy-done, bf16[1536,128]{1,0:T(8,128)(2,1)S(1)} %copy-done.12, f32[1536,256]{1,0:T(8,128)S(1)} %copy-done.10, f32[1536,128]{1,0:T(8,128)S(1)} %copy-done.16, ...), custom_call_target="tpu_custom_call" | custom-call | flops 1000 | bytes 1000 | tf_op jit(solution)/shard_map/pallas_call | solution.py:331
  85.1 8.1 %shard_map.65 = (f32[1536,256]{1,0:T(8,128)S(1)}, f32[1536,128]{1,0:T(8,128)S(1)}) custom-call(s32[7]{0:T(128)S(1)} %concatenate.6.info, bf16[1536,512]{1,0:T(8,128)(2,1)S(1)} %copy-done, bf16[1536,128]{1,0:T(8,128)(2,1)S(1)} %get-tuple-element.22.m, f32[1536,256]{1,0:T(8,128)S(1)} %copy-done.8, f32[1536,128]{1,0:T(8,128)S(1)} %copy-done.14, ...), custom_call_target="tpu_custom_call" | custom-call | flops 1000 | bytes 1000 | tf_op jit(solution)/shard_map/pallas_call | solution.py:331
  93.2 8.8 %shard_map.69 = (bf16[768,256]{1,0:T(8,128)(2,1)S(1)}, bf16[768,256]{1,0:T(8,128)(2,1)S(1)}) custom-call(s32[7]{0:T(128)S(1)} %concatenate.6.info, bf16[1536,512]{1,0:T(8,128)(2,1)S(1)} %copy-done, bf16[1536,128]{1,0:T(8,128)(2,1)S(1)} %copy-done.12, f32[1536,256]{1,0:T(8,128)S(1)} %get-tuple-element.34.acc_in, f32[1536,128]{1,0:T(8,128)S(1)} %get-tuple-element.35.sums_in, ...), custom_call_target="tpu_custom_call" | custom-call | flops 1000 | bytes 1000 | tf_op jit(solution)/shard_map/pallas_call | solution.py:331
  102.0 1.6 %collective-permute-start.11 = (bf16[768,256]{1,0:T(8,128)(2,1)S(1)}, bf16[768,256]{1,0:T(8,128)(2,1)S(1)}, u32[]{:S(2)}, u32[]{:S(2)}) collective-permute-start(bf16[768,256]{1,0:T(8,128)(2,1)S(1)} %get-tuple-element.38), channel_id=1, source_target_pairs={{0,1},{1,0},{2,3},{3,2},{4,5},{5,4},{6,7},{7,6},{8,9},{9,8},{10,11... | collective-permute-start | bytes 1179656 | tf_op jit(solution)/shard_map/ppermute | solution.py:472
  103.6 9.0 %shard_map.67 = (bf16[768,256]{1,0:T(8,128)(2,1)S(1)}, bf16[768,256]{1,0:T(8,128)(2,1)S(1)}) custom-call(s32[7]{0:T(128)S(1)} %concatenate.6.info, bf16[1536,512]{1,0:T(8,128)(2,1)S(1)} %copy-done, bf16[1536,128]{1,0:T(8,128)(2,1)S(1)} %get-tuple-element.22.m, f32[1536,256]{1,0:T(8,128)S(1)} %get-tuple-element.26.acc_in, ...), custom_call_target="tpu_custom_call" | custom-call | flops 1000 | bytes 1000 | tf_op jit(solution)/shard_map/pallas_call | solution.py:331
  113.2 10.3 %collective-permute-done.10.refs_2_ = bf16[768,256]{1,0:T(8,128)(2,1)S(1)} collective-permute-done((bf16[768,256]{1,0:T(8,128)(2,1)S(1)}, bf16[768,256]{1,0:T(8,128)(2,1)S(1)}, u32[]{:S(2)}, u32[]{:S(2)}) %collective-permute-start.10) | collective-permute-done | bytes 393248 | tf_op jit(solution)/shard_map/ppermute | solution.py:472
  123.5 5.2 %shard_map.70 = bf16[768,1536]{1,0:T(8,128)(2,1)} custom-call(s32[7]{0:T(128)S(1)} %concatenate.6.info, bf16[768,256]{1,0:T(8,128)(2,1)S(1)} %get-tuple-element.30.refs_0_, bf16[768,256]{1,0:T(8,128)(2,1)S(1)} %get-tuple-element.36.refs_1_, bf16[768,256]{1,0:T(8,128)(2,1)S(1)} %collective-permute-done.10.refs_2_, ...), custom_call_target="tpu_custom_call" | custom-call | flops 1000 | bytes 1000 | tf_op jit(solution)/shard_map/pallas_call | solution.py:382
  (56 shorter events, 9.2 us)
Async XLA Ops:
  0.0 1.9 %collective-permute-start.2 = (bf16[1536,512]{1,0:T(8,128)(2,1)}, bf16[1536,512]{1,0:T(8,128)(2,1)}, u32[]{:S(2)}, u32[]{:S(2)}) collective-permute-start(bf16[1536,512]{1,0:T(8,128)(2,1)} %value_any.3), channel_id=1, source_target_pairs={{0,2},{1,3}} | collective-permute-start | bytes 4718600 | tf_op jit(solution)/shard_map/ppermute | solution.py:420
  1.9 4.6 %copy-start.1 = (bf16[1536,512]{1,0:T(8,128)(2,1)S(1)}, bf16[1536,512]{1,0:T(8,128)(2,1)}, u32[]{:S(2)}) copy-start(bf16[1536,512]{1,0:T(8,128)(2,1)} %key_any.3) | copy-start | bytes 4718596
  1.9 6.6 %copy-start.18 = (s32[2]{0:T(128)S(1)}, s32[2]{0:T(128)}, u32[]{:S(2)}) copy-start(s32[2]{0:T(128)} %param.9) | copy-start | bytes 28
  1.9 6.6 %copy-start.19 = (s32[2]{0:T(128)S(1)}, s32[2]{0:T(128)}, u32[]{:S(2)}) copy-start(s32[2]{0:T(128)} %param.10) | copy-start | bytes 28
  1.9 6.7 %copy-start = (bf16[1536,512]{1,0:T(8,128)(2,1)S(1)}, bf16[1536,512]{1,0:T(8,128)(2,1)}, u32[]{:S(2)}) copy-start(bf16[1536,512]{1,0:T(8,128)(2,1)} %q.11) | copy-start | bytes 4718596
  4.9 19.1 %collective-permute-start.3 = (bf16[768,512]{1,0:T(8,128)(2,1)}, bf16[768,512]{1,0:T(8,128)(2,1)}, u32[]{:S(2)}, u32[]{:S(2)}) collective-permute-start(bf16[768,512]{1,0:T(8,128)(2,1)} %get-tuple-element.40), channel_id=1, source_target_pairs={{0,16},{2,6},{1,17},{3,7}} | collective-permute-start | bytes 2359304 | tf_op jit(solution)/shard_map/ppermute | solution.py:427
  6.5 43.0 %collective-permute-start = (bf16[1536,512]{1,0:T(8,128)(2,1)S(1)}, bf16[1536,512]{1,0:T(8,128)(2,1)}, u32[]{:S(2)}, u32[]{:S(2)}) collective-permute-start(bf16[1536,512]{1,0:T(8,128)(2,1)S(1)} %copy-done.1), channel_id=1, source_target_pairs={{0,2},{2,4},{4,6},{6,8},{8,10},{10,12},{12,14},{14,16},{16,18},{18... | collective-permute-start | bytes 4718600 | tf_op jit(solution)/shard_map/ppermute | solution.py:419
  19.2 44.7 %collective-permute-start.1 = (bf16[1536,512]{1,0:T(8,128)(2,1)}, bf16[1536,512]{1,0:T(8,128)(2,1)}, u32[]{:S(2)}, u32[]{:S(2)}) collective-permute-start(bf16[1536,512]{1,0:T(8,128)(2,1)} %get-tuple-element.25), channel_id=1, source_target_pairs={{0,2},{2,4},{4,6},{6,8},{8,10},{10,12},{12,14},{14,16},{16,18},{18... | collective-permute-start | bytes 4718600 | tf_op jit(solution)/shard_map/ppermute | solution.py:440
  24.0 3.8 %copy-start.3 = (bf16[1536,512]{1,0:T(8,128)(2,1)S(1)}, bf16[1536,512]{1,0:T(8,128)(2,1)}, u32[]{:S(2)}) copy-start(bf16[1536,512]{1,0:T(8,128)(2,1)} %value_any.3) | copy-start | bytes 4718596
  26.3 12.7 %collective-permute-start.4 = (bf16[768,512]{1,0:T(8,128)(2,1)}, bf16[768,512]{1,0:T(8,128)(2,1)}, u32[]{:S(2)}, u32[]{:S(2)}) collective-permute-start(bf16[768,512]{1,0:T(8,128)(2,1)} %broadcast_select_fusion), channel_id=1, source_target_pairs={{0,8},{16,24},{2,18},{6,22},{1,9},{17,25},{3,19},{7,23}} | collective-permute-start | bytes 2359304 | tf_op jit(solution)/shard_map/ppermute | solution.py:427
  39.0 3.6 %copy-start.17 = (bf16[768,512]{1,0:T(8,128)(2,1)S(1)}, bf16[768,512]{1,0:T(8,128)(2,1)}, u32[]{:S(2)}) copy-start(bf16[768,512]{1,0:T(8,128)(2,1)} %get-tuple-element.39) | copy-start | bytes 2359300
  41.3 25.1 %collective-permute-start.5 = (bf16[768,512]{1,0:T(8,128)(2,1)}, bf16[768,512]{1,0:T(8,128)(2,1)}, u32[]{:S(2)}, u32[]{:S(2)}) collective-permute-start(bf16[768,512]{1,0:T(8,128)(2,1)} %broadcast_select_fusion.1), channel_id=1, source_target_pairs={{0,4},{8,12},{16,20},{24,28},{2,10},{6,14},{18,26},{22,30},{1,5},{... | collective-permute-start | bytes 2359304 | tf_op jit(solution)/shard_map/ppermute | solution.py:427
  43.9 49.3 %collective-permute-start.7 = (bf16[1536,512]{1,0:T(8,128)(2,1)}, bf16[1536,512]{1,0:T(8,128)(2,1)}, u32[]{:S(2)}, u32[]{:S(2)}) collective-permute-start(bf16[1536,512]{1,0:T(8,128)(2,1)} %pad_maximum_fusion), channel_id=1, source_target_pairs={{0,4},{4,8},{8,12},{12,16},{16,20},{20,24},{24,28},{1,5},{5,9},{9,... | collective-permute-start | bytes 4718600 | tf_op jit(solution)/shard_map/ppermute | solution.py:423
  49.5 43.7 %collective-permute-start.8 = (bf16[1536,512]{1,0:T(8,128)(2,1)}, bf16[1536,512]{1,0:T(8,128)(2,1)}, u32[]{:S(2)}, u32[]{:S(2)}) collective-permute-start(bf16[1536,512]{1,0:T(8,128)(2,1)} %collective-permute-done.near_k), channel_id=1, source_target_pairs={{0,2},{4,6},{8,10},{12,14},{16,18},{20,22},{24,26},{28,30},{1,3},{... | collective-permute-start | bytes 4718600 | tf_op jit(solution)/shard_map/ppermute | solution.py:444
  63.9 29.3 %collective-permute-start.9 = (bf16[1536,512]{1,0:T(8,128)(2,1)}, bf16[1536,512]{1,0:T(8,128)(2,1)}, u32[]{:S(2)}, u32[]{:S(2)}) collective-permute-start(bf16[1536,512]{1,0:T(8,128)(2,1)} %collective-permute-done.1.near_v), channel_id=1, source_target_pairs={{0,2},{4,6},{8,10},{12,14},{16,18},{20,22},{24,26},{28,30},{1,3},{... | collective-permute-start | bytes 4718600 | tf_op jit(solution)/shard_map/ppermute | solution.py:445
  66.3 9.4 %copy-start.10 = (f32[1536,256]{1,0:T(8,128)S(1)}, f32[1536,256]{1,0:T(8,128)}, u32[]{:S(2)}) copy-start(f32[1536,256]{1,0:T(8,128)} %copy-done.9) | copy-start | bytes 4718596
  66.3 9.4 %copy-start.12 = (bf16[1536,128]{1,0:T(8,128)(2,1)S(1)}, bf16[1536,128]{1,0:T(8,128)(2,1)}, u32[]{:S(2)}) copy-start(bf16[1536,128]{1,0:T(8,128)(2,1)} %copy-done.11) | copy-start | bytes 1179652
  67.7 25.5 %collective-permute-start.6 = (bf16[768,512]{1,0:T(8,128)(2,1)S(1)}, bf16[768,512]{1,0:T(8,128)(2,1)S(1)}, u32[]{:S(2)}, u32[]{:S(2)}) collective-permute-start(bf16[768,512]{1,0:T(8,128)(2,1)S(1)} %broadcast_select_fusion.2.sink_a), channel_id=1, source_target_pairs={{0,2},{2,0},{4,6},{6,4},{8,10},{10,8},{12,14},{14,12},{16,18},{18,... | collective-permute-start | bytes 2359304 | tf_op jit(solution)/shard_map/ppermute | solution.py:442
  76.8 8.2 %copy-start.8 = (f32[1536,256]{1,0:T(8,128)S(1)}, f32[1536,256]{1,0:T(8,128)}, u32[]{:S(2)}) copy-start(f32[1536,256]{1,0:T(8,128)} %copy-done.7) | copy-start | bytes 4718596
  76.9 8.3 %copy-start.14 = (f32[1536,128]{1,0:T(8,128)S(1)}, f32[1536,128]{1,0:T(8,128)}, u32[]{:S(2)}) copy-start(f32[1536,128]{1,0:T(8,128)} %copy-done.13) | copy-start | bytes 2359300
  85.1 8.1 %copy-start.5 = (bf16[1536,512]{1,0:T(8,128)(2,1)S(1)}, bf16[1536,512]{1,0:T(8,128)(2,1)}, u32[]{:S(2)}) copy-start(bf16[1536,512]{1,0:T(8,128)(2,1)} %value_any.3) | copy-start | bytes 4718596
  102.0 11.2 %collective-permute-start.11 = (bf16[768,256]{1,0:T(8,128)(2,1)S(1)}, bf16[768,256]{1,0:T(8,128)(2,1)S(1)}, u32[]{:S(2)}, u32[]{:S(2)}) collective-permute-start(bf16[768,256]{1,0:T(8,128)(2,1)S(1)} %get-tuple-element.38), channel_id=1, source_target_pairs={{0,1},{1,0},{2,3},{3,2},{4,5},{5,4},{6,7},{7,6},{8,9},{9,8},{10,11... | collective-permute-start | bytes 1179656 | tf_op jit(solution)/shard_map/ppermute | solution.py:472
  103.6 19.9 %copy-start.6 = (bf16[1024,1536]{1,0:T(8,128)(2,1)S(1)}, bf16[1024,1536]{1,0:T(8,128)(2,1)}, u32[]{:S(2)}) copy-start(bf16[1024,1536]{1,0:T(8,128)(2,1)} %refs_4_.1) | copy-start | bytes 9437188
  112.7 10.9 %collective-permute-start.10 = (bf16[768,256]{1,0:T(8,128)(2,1)S(1)}, bf16[768,256]{1,0:T(8,128)(2,1)S(1)}, u32[]{:S(2)}, u32[]{:S(2)}) collective-permute-start(bf16[768,256]{1,0:T(8,128)(2,1)S(1)} %get-tuple-element.37), channel_id=1, source_target_pairs={{0,1},{1,0},{2,3},{3,2},{4,5},{5,4},{6,7},{7,6},{8,9},{9,8},{10,11... | collective-permute-start | bytes 1179656 | tf_op jit(solution)/shard_map/ppermute | solution.py:472
  (8 other events, 11.1 us)
where the time goes:
time: 130 us; the launch traced here: 129 us
  Pallas kernels  53.5 us (41%)
  starting transfers between devices  44.3 us (34%)
  waiting for transfers between devices  10.3 us (8%)
  other arithmetic  10.2 us (8%)
  local copies, waits for them, and re-layouts  8.74 us (7%)
  between operations  1.63 us (1%)
    pallas_call x6, Pallas kernels, stage(): pl.pallas_call(kernel, in_specs=[SMEM_SPEC] + [VMEM_SPEC] * (len(arrays)...  48.4 us
    ppermute x1, starting transfers between devices, local(): relay_k = lax.ppermute(near_k, axis, on_chip)  14.4 us
    ppermute x2, waiting for transfers between devices, local(): theirs.append(lax.ppermute(results[1], 'head', [(0, 1), (1, 0)]))  10.3 us
    ppermute x1, starting transfers between devices, local(): other = lax.ppermute(held, axis, [(i, i ^ 1) for i in range(size)])  8 us
    unnamed x40, local copies, waits for them, and re-layouts  7.51 us
    select_n x3, other arithmetic, local(): held = jnp.where(takes, moved, held)  5.84 us
    ppermute x1, starting transfers between devices, local(): lax.ppermute(own_last, axis, [(i, i + 2) for i in range(0, size - 2, 2)])  5.55 us
    pallas_call x1, Pallas kernels, project(): pl.pallas_call(kernel, grid=(turns,), in_specs=[SMEM_SPEC] + [VMEM_SPEC]...  5.15 us
  transfers between devices with their start and end apart: 12, of which 1 were waited for; matrix products, arithmetic and copies ran while one was open for 6% of the time, Pallas kernels for 31%

commit v1 on v0

--- a/solution.py
+++ b/solution.py
@@ -14,8 +14,9 @@
 SCALE = HD ** -0.5 * LOG2E
 LIMIT = 1e30
 HIDDEN = 1e30
-PARAMS = pltpu.CompilerParams(vmem_limit_bytes=24 * 1024 * 1024)
+PARAMS = pltpu.CompilerParams(vmem_limit_bytes=12 * 1024 * 1024)
 ANY_SPEC = pl.BlockSpec(memory_space=pl.ANY)
+NEAR_COST = pl.CostEstimate(flops=8_000_000_000, bytes_accessed=1000, transcendentals=0)
 COST = pl.CostEstimate(flops=1000, bytes_accessed=1000, transcendentals=0)
 TOKEN = jax.ShapeDtypeStruct((8, 128), jnp.float32)
 
@@ -139,8 +140,9 @@
 
 
 def near_kernel(group, info, q, m, acc_in, sums_in, near_k, near_v, *refs):
-    acc, sums, kt, values, k_buf, v_buf, sem = refs
+    acc, sums, token, kt, values, k_buf, v_buf, sem = refs
     offset, heads = group
+    token[...] = jnp.zeros_like(token)
     first = info[0]
     order = (1, 0)
     copies = {
@@ -183,7 +185,7 @@
     sink_a, sink_b, far, relay_k, relay_v, key_any, value_any, near_k, near_v, *refs,
 ):
     outs = refs[:-8]
-    kt, values, k_buf, v_buf, acc, shift, largest, sem = refs[-8:]
+    kt, values, k_buf, v_buf, acc, shift, too_large, sem = refs[-8:]
     first = info[0]
     core = info[6]
     far_seen = visible(info, 0, first - 3)
@@ -255,7 +257,7 @@
             rows = rows_of(slot)
             total = spread_sum(sums_in[rows, :], h, heads) + results[slot][:, HD:]
             write(slot, h, acc_in[rows, column] + results[slot][:, :HD], total)
-            largest[h, slot] = jnp.max(total)
+            too_large[h, slot] = jnp.max(jnp.where(total < LIMIT, 0.0, 1.0))
 
     each_head(group, turn)
 
@@ -317,8 +319,7 @@
 
     def check(h, column, wide):
         for slot in (0, 1):
-            in_range = largest[h, slot] < LIMIT
-            pl.when(jnp.logical_not(in_range))(lambda slot=slot: again(slot, h, wide))
+            pl.when(too_large[h, slot] > 0.0)(lambda slot=slot: again(slot, h, wide))
 
     each_head(group, check)
 
@@ -327,7 +328,7 @@
 SMEM_SPEC = pl.BlockSpec(memory_space=pltpu.SMEM)
 
 
-def stage(kernel, arrays, in_any, outs, scratch):
+def stage(kernel, arrays, in_any, outs, scratch, cost=None):
     return pl.pallas_call(
         kernel,
         in_specs=[SMEM_SPEC] + [VMEM_SPEC] * (len(arrays) - in_any - 1) + [ANY_SPEC] * in_any,
@@ -337,7 +338,7 @@
         ] + list(scratch),
         out_shape=outs,
         compiler_params=PARAMS,
-        cost_estimate=COST,
+        cost_estimate=cost or COST,
     )(*arrays)
 
 
@@ -347,7 +348,7 @@
 
 def sink_steps(size):
     bits = [1 << b for b in range(1, size.bit_length() - 1)]
-    orders = (bits[::-1], [bits[0]] + bits[:0:-1])
+    orders = (bits[::-1], bits[::-1])
     done = [0, 0]
     steps = []
     for step in range(len(bits)):
@@ -419,11 +420,20 @@
     near_k = lax.ppermute(key_states, axis, onward)
     moved = lax.ppermute(value_states, axis, [(0, 1)])
     held = jnp.where(core == 0, key_states[:FT], moved[:FT])
-    own_last = last_frames(key_states, value_states)
-    far = lax.ppermute(own_last, axis, [(i, i + 2) for i in range(0, size - 2, 2)])
+
+    def arrived(array):
+        return array[0, 0] == array[0, 0]
+
+    def near_stage(group, state):
+        return stage(
+            functools.partial(near_kernel, group),
+            [info, query_states, *state, near_k, near_v], 2, [acc_like, sums_like, TOKEN],
+            frame_buffers + [dma_sems], NEAR_COST,
+        )
 
     states = []
-    for step, pairs in enumerate(sink_steps(size)):
+    steps = sink_steps(size)
+    for step, pairs in enumerate(steps):
         moved = lax.ppermute(held, axis, pairs)
         takes = jnp.zeros((), bool)
         for _, target in pairs:
@@ -438,20 +448,23 @@
             takes = takes & (token[0, 0] == 0)
             if step == 0:
                 near_v = lax.ppermute(passed[0], axis, onward)
+                takes = takes & arrived(near_k)
+            if step == len(groups) - 1:
+                own_last = jnp.where(token[0, 0] == 0, last_frames(key_states, value_states), 0)
+                far = lax.ppermute(own_last, axis, [(i, i + 2) for i in range(0, size - 2, 2)])
+        if step == len(steps) - 1:
+            *sums_now, token = near_stage(groups[0], states[0])
+            states[0] = states[0][0], *sums_now
+            takes = takes & (token[0, 0] == 0) & arrived(far)
         held = jnp.where(takes, moved, held)
     other = lax.ppermute(held, axis, [(i, i ^ 1) for i in range(size)])
     on_chip = [(i, i + 1) for i in range(0, size, 2)]
     relay_k = lax.ppermute(near_k, axis, on_chip)
     relay_v = lax.ppermute(near_v, axis, on_chip)
 
-    for g, group in enumerate(groups):
-        m, acc, sums = states[g]
-        acc, sums = stage(
-            functools.partial(near_kernel, group),
-            [info, query_states, m, acc, sums, near_k, near_v], 2, [acc_like, sums_like],
-            frame_buffers + [dma_sems],
-        )
-        states[g] = m, acc, sums
+    for g, group in enumerate(groups[1:], 1):
+        *sums_now, _ = near_stage(group, states[g])
+        states[g] = states[g][0], *sums_now
     mine, theirs = [], []
     for g, group in enumerate(groups):
         part = jax.ShapeDtypeStruct((FT if paired else rows, group_width), jnp.bfloat16)

time: 130 us -> 136 us (1.046)
  starting transfers between devices: 44.3 us -> 22.8 us
  waiting for transfers between devices: 10.3 us -> 22.6 us
  local copies, waits for them, and re-layouts: 8.74 us -> 19.1 us
  between operations: 1.63 us -> 4.72 us
    ppermute x1, starting transfers between devices: 14.4 us -> 2.49 us  [local(): relay_k = lax.ppermute(near_k, axis, on_chip)]
    ppermute x1, starting transfers between devices: 8 us -> 0.07 us  [local(): other = lax.ppermute(held, axis, [(i, i ^ 1) for i in range(size)])]
    unnamed x40 -> x48, local copies, waits for them, and re-layouts: 7.51 us -> 14.8 us
    ppermute x3, waiting for transfers between devices: 0.01 us -> 6.06 us  [local(): moved = lax.ppermute(held, axis, pairs)]
    ppermute x1, waiting for transfers between devices: 0.01 us -> 5.82 us  [local(): lax.ppermute(own_last, axis, [(i, i + 2) for i in range(0, size - 2, 2)])]
    slice x0 -> x4, local copies, waits for them, and re-layouts: none -> 3.52 us  [the longest x2 2.43 us: arrived(): return array[0, 0] == array[0, 0]]
    ppermute x1, starting transfers between devices: 5.55 us -> 4 us  [local(): lax.ppermute(own_last, axis, [(i, i + 2) for i in range(0, size - 2, 2)])]
    select_n x0 -> x1, other arithmetic: none -> 1.51 us  [local(): jnp.where(token[0, 0] == 0, last_frames(key_states, value_states), 0)]
  transfers between devices with their start and end apart: 12 -> 12, of which waited for: 1 -> 4; matrix products, arithmetic and copies ran while one was open for 6% -> 11% of each run, Pallas kernels for 31% -> 30%
where the time goes in v1:
time: 136 us; the launch traced here: 134 us
  Pallas kernels  54.3 us (40%)
  starting transfers between devices  22.8 us (17%)
  waiting for transfers between devices  22.6 us (17%)
  local copies, waits for them, and re-layouts  19.1 us (14%)
  other arithmetic  10.2 us (7%)
  between operations  4.72 us (3%)
    pallas_call x6, Pallas kernels, stage(): pl.pallas_call(kernel, in_specs=[SMEM_SPEC] + [VMEM_SPEC] * (len(arrays)...  49.2 us
    unnamed x48, local copies, waits for them, and re-layouts  14.8 us
    ppermute x2, waiting for transfers between devices, local(): theirs.append(lax.ppermute(results[1], 'head', [(0, 1), (1, 0)]))  10.7 us
    ppermute x3, waiting for transfers between devices, local(): moved = lax.ppermute(held, axis, pairs)  6.06 us
    ppermute x1, waiting for transfers between devices, local(): lax.ppermute(own_last, axis, [(i, i + 2) for i in range(0, size - 2, 2)])  5.82 us
    select_n x3, other arithmetic, local(): held = jnp.where(takes, moved, held)  5.61 us
    pallas_call x1, Pallas kernels, project(): pl.pallas_call(kernel, grid=(turns,), in_specs=[SMEM_SPEC] + [VMEM_SPEC]...  5.15 us
    ppermute x3, starting transfers between devices, local(): moved = lax.ppermute(held, axis, pairs)  4.36 us
  transfers between devices with their start and end apart: 12, of which 4 were waited for; matrix products, arithmetic and copies ran while one was open for 11% of the time, Pallas kernels for 30%

profile of v1, /device:TPU:18, one launch (start us, length us, event | category | flops | bytes accessed | tf_op | source)
XLA Modules:
  0.0 133.7 jit_solution(18261195811047691052)
XLA Ops:
  0.0 1.8 %collective-permute-start.3 = (bf16[1536,512]{1,0:T(8,128)(2,1)}, bf16[1536,512]{1,0:T(8,128)(2,1)}, u32[]{:S(2)}, u32[]{:S(2)}) collective-permute-start(bf16[1536,512]{1,0:T(8,128)(2,1)} %value_any.3), channel_id=1, source_target_pairs={{0,2},{1,3}} | collective-permute-start | bytes 4718600 | tf_op jit(solution)/shard_map/ppermute | solution.py:421
  1.8 1.9 %collective-permute-start = (bf16[1536,512]{1,0:T(8,128)(2,1)}, bf16[1536,512]{1,0:T(8,128)(2,1)}, u32[]{:S(2)}, u32[]{:S(2)}) collective-permute-start(bf16[1536,512]{1,0:T(8,128)(2,1)} %key_any.3), channel_id=1, source_target_pairs={{0,2},{2,4},{4,6},{6,8},{8,10},{10,12},{12,14},{14,16},{16,18},{18... | collective-permute-start | bytes 4718600 | tf_op jit(solution)/shard_map/ppermute | solution.py:420
  3.8 3.1 %fusion = (bf16[768,512]{1,0:T(8,128)(2,1)}, bf16[768,512]{1,0:T(8,128)(2,1)}) fusion(bf16[1536,512]{1,0:T(8,128)(2,1)} %key_any.3, bf16[1536,512]{1,0:T(8,128)(2,1)} %collective-permute-done.3, pred[]{:T(512)S(6)} %eq.102), kind=kLoop, calls=%fused_computation.5 | loop fusion | flops 393216 | bytes 3932161 | tf_op jit(solution)/shard_map/slice | solution.py:346
  6.9 1.5 %collective-permute-start.4 = (bf16[768,512]{1,0:T(8,128)(2,1)}, bf16[768,512]{1,0:T(8,128)(2,1)}, u32[]{:S(2)}, u32[]{:S(2)}) collective-permute-start(bf16[768,512]{1,0:T(8,128)(2,1)} %get-tuple-element.42), channel_id=1, source_target_pairs={{0,16},{2,18},{1,17},{3,19}} | collective-permute-start | bytes 2359304 | tf_op jit(solution)/shard_map/ppermute | solution.py:437
  9.9 7.2 %shard_map.64 = (bf16[1536,512]{1,0:T(8,128)(2,1)}, bf16[1536,128]{1,0:T(8,128)(2,1)S(1)}, f32[1536,256]{1,0:T(8,128)S(1)}, f32[1536,128]{1,0:T(8,128)S(1)}, f32[8,128]{1,0:T(8,128)S(1)}) custom-call(s32[7]{0:T(128)S(1)} %concatenate.6.info, bf16[1536,512]{1,0:T(8,128)(2,1)S(1)} %copy-done.2, bf16[1536,512]{1,0:T(8,128)(2,1)S(1)} %copy-done, ...), custom_call_target="tpu_custom_call" | custom-call | flops 1000 | bytes 1000 | tf_op jit(solution)/shard_map/pallas_call | solution.py:332
  19.2 3.5 %collective-permute-start.1 = (bf16[1536,512]{1,0:T(8,128)(2,1)}, bf16[1536,512]{1,0:T(8,128)(2,1)}, u32[]{:S(2)}, u32[]{:S(2)}) collective-permute-start(bf16[1536,512]{1,0:T(8,128)(2,1)} %get-tuple-element.26), channel_id=1, source_target_pairs={{0,2},{2,4},{4,6},{6,8},{8,10},{10,12},{12,14},{14,16},{16,18},{18... | collective-permute-start | bytes 4718600 | tf_op jit(solution)/shard_map/ppermute | solution.py:450
  26.5 2.3 %broadcast_select_fusion = bf16[768,512]{1,0:T(8,128)(2,1)} fusion(bf16[768,512]{1,0:T(8,128)(2,1)} %collective-permute-done.4, bf16[768,512]{1,0:T(8,128)(2,1)} %get-tuple-element.42, pred[]{:T(512)S(6)} %and.27), kind=kLoop, calls=%fused_computation.2 | loop fusion | flops 393216 | bytes 2359297 | tf_op jit(solution)/shard_map/jit(_where)/select_n | solution.py:459
  28.8 1.5 %collective-permute-start.5 = (bf16[768,512]{1,0:T(8,128)(2,1)}, bf16[768,512]{1,0:T(8,128)(2,1)}, u32[]{:S(2)}, u32[]{:S(2)}) collective-permute-start(bf16[768,512]{1,0:T(8,128)(2,1)} %broadcast_select_fusion), channel_id=1, source_target_pairs={{0,8},{16,24},{2,10},{18,26},{1,9},{17,25},{3,11},{19,27}} | collective-permute-start | bytes 2359304 | tf_op jit(solution)/shard_map/ppermute | solution.py:437
  30.3 7.1 %shard_map.66 = (bf16[1536,128]{1,0:T(8,128)(2,1)S(1)}, f32[1536,256]{1,0:T(8,128)S(1)}, f32[1536,128]{1,0:T(8,128)S(1)}, f32[8,128]{1,0:T(8,128)S(1)}) custom-call(s32[7]{0:T(128)S(1)} %concatenate.6.info, bf16[1536,512]{1,0:T(8,128)(2,1)S(1)} %copy-done.3, bf16[1536,512]{1,0:T(8,128)(2,1)S(1)} %copy-done, bf16[1536,512]{1,0:T(8,128)(2,1)S(1)} %copy-done.1), custom_call_target="tpu_custom_call" | custom-call | flops 1000 | bytes 1000 | tf_op jit(solution)/shard_map/pallas_call | solution.py:332
  41.6 1.5 %maximum_select_fusion = bf16[1536,512]{1,0:T(8,128)(2,1)} fusion(bf16[768,512]{1,0:T(8,128)(2,1)S(1)} %slice.33, bf16[768,512]{1,0:T(8,128)(2,1)S(1)} %copy-done.21, pred[]{:T(512)} %bitcast.4), kind=kLoop, calls=%fused_computation | loop fusion | flops 3932160 | bytes 3145729 | tf_op jit(solution)/shard_map/jit(_where)/select_n | solution.py:453
  43.1 4.0 %collective-permute-start.2 = (bf16[1536,512]{1,0:T(8,128)(2,1)}, bf16[1536,512]{1,0:T(8,128)(2,1)}, u32[]{:S(2)}, u32[]{:S(2)}) collective-permute-start(bf16[1536,512]{1,0:T(8,128)(2,1)} %maximum_select_fusion), channel_id=1, source_target_pairs={{0,4},{4,8},{8,12},{12,16},{16,20},{20,24},{24,28},{1,5},{5,9},{9,... | collective-permute-start | bytes 4718600 | tf_op jit(solution)/shard_map/ppermute | solution.py:454
  47.1 2.1 %broadcast_select_fusion.1 = bf16[768,512]{1,0:T(8,128)(2,1)} fusion(bf16[768,512]{1,0:T(8,128)(2,1)} %collective-permute-done.5, bf16[768,512]{1,0:T(8,128)(2,1)} %broadcast_select_fusion, pred[]{:T(512)S(6)} %and.25), kind=kLoop, calls=%fused_computation.3 | loop fusion | flops 393216 | bytes 2359297 | tf_op jit(solution)/shard_map/jit(_where)/select_n | solution.py:459
  50.6 2.5 %collective-permute-start.8 = (bf16[1536,512]{1,0:T(8,128)(2,1)}, bf16[1536,512]{1,0:T(8,128)(2,1)}, u32[]{:S(2)}, u32[]{:S(2)}) collective-permute-start(bf16[1536,512]{1,0:T(8,128)(2,1)} %collective-permute-done.near_k), channel_id=1, source_target_pairs={{0,2},{4,6},{8,10},{12,14},{16,18},{20,22},{24,26},{28,30},{1,3},{... | collective-permute-start | bytes 4718600 | tf_op jit(solution)/shard_map/ppermute | solution.py:462
  53.1 2.4 %collective-permute-start.9 = (bf16[1536,512]{1,0:T(8,128)(2,1)}, bf16[1536,512]{1,0:T(8,128)(2,1)}, u32[]{:S(2)}, u32[]{:S(2)}) collective-permute-start(bf16[1536,512]{1,0:T(8,128)(2,1)} %collective-permute-done.1.near_v), channel_id=1, source_target_pairs={{0,2},{4,6},{8,10},{12,14},{16,18},{20,22},{24,26},{28,30},{1,3},{... | collective-permute-start | bytes 4718600 | tf_op jit(solution)/shard_map/ppermute | solution.py:463
  55.5 1.4 %copy-done.4 = bf16[1536,512]{1,0:T(8,128)(2,1)S(1)} copy-done((bf16[1536,512]{1,0:T(8,128)(2,1)S(1)}, bf16[1536,512]{1,0:T(8,128)(2,1)}, u32[]{:S(2)}) %copy-start.4) | copy-done | bytes 1572888
  59.5 8.1 %shard_map.65 = (f32[1536,256]{1,0:T(8,128)S(1)}, f32[1536,128]{1,0:T(8,128)S(1)}, f32[8,128]{1,0:T(8,128)S(1)}) custom-call(s32[7]{0:T(128)S(1)} %concatenate.6.info, bf16[1536,512]{1,0:T(8,128)(2,1)S(1)} %copy-done.4, bf16[1536,128]{1,0:T(8,128)(2,1)S(1)} %get-tuple-element.23.m, f32[1536,256]{1,0:T(8,128)S(1)} %copy-done.14, f32[1536,128]{1,0:T(8,128)S(1)} %copy-done.18, ...), custom_call_target="tpu_custom_call" | custom-call | flops 8000000000 | bytes 1000 | tf_op jit(solution)/shard_map/pallas_call | solution.py:332
  70.7 5.8 %collective-permute-done.2.far = bf16[1536,512]{1,0:T(8,128)(2,1)} collective-permute-done((bf16[1536,512]{1,0:T(8,128)(2,1)}, bf16[1536,512]{1,0:T(8,128)(2,1)}, u32[]{:S(2)}, u32[]{:S(2)}) %collective-permute-start.2) | collective-permute-done | bytes 1572896 | tf_op jit(solution)/shard_map/ppermute | solution.py:454
  78.9 6.1 %collective-permute-done.6 = bf16[768,512]{1,0:T(8,128)(2,1)} collective-permute-done((bf16[768,512]{1,0:T(8,128)(2,1)}, bf16[768,512]{1,0:T(8,128)(2,1)}, u32[]{:S(2)}, u32[]{:S(2)}) %collective-permute-start.6) | collective-permute-done | bytes 786464 | tf_op jit(solution)/shard_map/ppermute | solution.py:437
  88.8 8.7 %shard_map.68 = (f32[1536,256]{1,0:T(8,128)S(1)}, f32[1536,128]{1,0:T(8,128)S(1)}, f32[8,128]{1,0:T(8,128)}) custom-call(s32[7]{0:T(128)S(1)} %concatenate.6.info, bf16[1536,512]{1,0:T(8,128)(2,1)S(1)} %copy-done.5, bf16[1536,128]{1,0:T(8,128)(2,1)S(1)} %copy-done.12, f32[1536,256]{1,0:T(8,128)S(1)} %copy-done.16, f32[1536,128]{1,0:T(8,128)S(1)} %copy-done.20, ...), custom_call_target="tpu_custom_call" | custom-call | flops 8000000000 | bytes 1000 | tf_op jit(solution)/shard_map/pallas_call | solution.py:332
  97.5 9.0 %shard_map.69 = (bf16[768,256]{1,0:T(8,128)(2,1)S(1)}, bf16[768,256]{1,0:T(8,128)(2,1)S(1)}) custom-call(s32[7]{0:T(128)S(1)} %concatenate.6.info, bf16[1536,512]{1,0:T(8,128)(2,1)S(1)} %copy-done.5, bf16[1536,128]{1,0:T(8,128)(2,1)S(1)} %copy-done.12, f32[1536,256]{1,0:T(8,128)S(1)} %get-tuple-element.36.acc_in, f32[1536,128]{1,0:T(8,128)S(1)} %get-tuple-element.37.sums_in, ...), custom_call_target="tpu_custom_call" | custom-call | flops 1000 | bytes 1000 | tf_op jit(solution)/shard_map/pallas_call | solution.py:332
  106.5 1.6 %collective-permute-start.11 = (bf16[768,256]{1,0:T(8,128)(2,1)S(1)}, bf16[768,256]{1,0:T(8,128)(2,1)S(1)}, u32[]{:S(2)}, u32[]{:S(2)}) collective-permute-start(bf16[768,256]{1,0:T(8,128)(2,1)S(1)} %get-tuple-element.40), channel_id=1, source_target_pairs={{0,1},{1,0},{2,3},{3,2},{4,5},{5,4},{6,7},{7,6},{8,9},{9,8},{10,11... | collective-permute-start | bytes 1179656 | tf_op jit(solution)/shard_map/ppermute | solution.py:485
  108.1 9.2 %shard_map.67 = (bf16[768,256]{1,0:T(8,128)(2,1)S(1)}, bf16[768,256]{1,0:T(8,128)(2,1)S(1)}) custom-call(s32[7]{0:T(128)S(1)} %concatenate.6.info, bf16[1536,512]{1,0:T(8,128)(2,1)S(1)} %copy-done.5, bf16[1536,128]{1,0:T(8,128)(2,1)S(1)} %get-tuple-element.23.m, f32[1536,256]{1,0:T(8,128)S(1)} %copy-done.8, f32[1536,128]{1,0:T(8,128)S(1)} %copy-done.10, ...), custom_call_target="tpu_custom_call" | custom-call | flops 1000 | bytes 1000 | tf_op jit(solution)/shard_map/pallas_call | solution.py:332
  118.0 10.5 %collective-permute-done.10.refs_2_ = bf16[768,256]{1,0:T(8,128)(2,1)S(1)} collective-permute-done((bf16[768,256]{1,0:T(8,128)(2,1)S(1)}, bf16[768,256]{1,0:T(8,128)(2,1)S(1)}, u32[]{:S(2)}, u32[]{:S(2)}) %collective-permute-start.10) | collective-permute-done | bytes 393248 | tf_op jit(solution)/shard_map/ppermute | solution.py:485
  128.6 5.1 %shard_map.70 = bf16[768,1536]{1,0:T(8,128)(2,1)} custom-call(s32[7]{0:T(128)S(1)} %concatenate.6.info, bf16[768,256]{1,0:T(8,128)(2,1)S(1)} %get-tuple-element.32.refs_0_, bf16[768,256]{1,0:T(8,128)(2,1)S(1)} %get-tuple-element.38.refs_1_, bf16[768,256]{1,0:T(8,128)(2,1)S(1)} %collective-permute-done.10.refs_2_, ...), custom_call_target="tpu_custom_call" | custom-call | flops 1000 | bytes 1000 | tf_op jit(solution)/shard_map/pallas_call | solution.py:383
  (67 shorter events, 21.0 us)
Async XLA Ops:
  0.0 3.8 %collective-permute-start.3 = (bf16[1536,512]{1,0:T(8,128)(2,1)}, bf16[1536,512]{1,0:T(8,128)(2,1)}, u32[]{:S(2)}, u32[]{:S(2)}) collective-permute-start(bf16[1536,512]{1,0:T(8,128)(2,1)} %value_any.3), channel_id=1, source_target_pairs={{0,2},{1,3}} | collective-permute-start | bytes 4718600 | tf_op jit(solution)/shard_map/ppermute | solution.py:421
  1.8 22.1 %collective-permute-start = (bf16[1536,512]{1,0:T(8,128)(2,1)}, bf16[1536,512]{1,0:T(8,128)(2,1)}, u32[]{:S(2)}, u32[]{:S(2)}) collective-permute-start(bf16[1536,512]{1,0:T(8,128)(2,1)} %key_any.3), channel_id=1, source_target_pairs={{0,2},{2,4},{4,6},{6,8},{8,10},{10,12},{12,14},{14,16},{16,18},{18... | collective-permute-start | bytes 4718600 | tf_op jit(solution)/shard_map/ppermute | solution.py:420
  3.8 4.7 %copy-start.22 = (s32[2]{0:T(128)S(1)}, s32[2]{0:T(128)}, u32[]{:S(2)}) copy-start(s32[2]{0:T(128)} %param.9) | copy-start | bytes 28
  3.8 4.7 %copy-start.23 = (s32[2]{0:T(128)S(1)}, s32[2]{0:T(128)}, u32[]{:S(2)}) copy-start(s32[2]{0:T(128)} %param.10) | copy-start | bytes 28
  3.8 4.7 %copy-start = (bf16[1536,512]{1,0:T(8,128)(2,1)S(1)}, bf16[1536,512]{1,0:T(8,128)(2,1)}, u32[]{:S(2)}) copy-start(bf16[1536,512]{1,0:T(8,128)(2,1)} %key_any.3) | copy-start | bytes 4718596
  3.8 4.7 %copy-start.1 = (bf16[1536,512]{1,0:T(8,128)(2,1)S(1)}, bf16[1536,512]{1,0:T(8,128)(2,1)}, u32[]{:S(2)}) copy-start(bf16[1536,512]{1,0:T(8,128)(2,1)} %value_any.3) | copy-start | bytes 4718596
  6.9 19.6 %collective-permute-start.4 = (bf16[768,512]{1,0:T(8,128)(2,1)}, bf16[768,512]{1,0:T(8,128)(2,1)}, u32[]{:S(2)}, u32[]{:S(2)}) collective-permute-start(bf16[768,512]{1,0:T(8,128)(2,1)} %get-tuple-element.42), channel_id=1, source_target_pairs={{0,16},{2,18},{1,17},{3,19}} | collective-permute-start | bytes 2359304 | tf_op jit(solution)/shard_map/ppermute | solution.py:437
  8.5 1.4 %copy-start.2 = (bf16[1536,512]{1,0:T(8,128)(2,1)S(1)}, bf16[1536,512]{1,0:T(8,128)(2,1)}, u32[]{:S(2)}) copy-start(bf16[1536,512]{1,0:T(8,128)(2,1)} %q.11) | copy-start | bytes 4718596
  19.2 33.9 %collective-permute-start.1 = (bf16[1536,512]{1,0:T(8,128)(2,1)}, bf16[1536,512]{1,0:T(8,128)(2,1)}, u32[]{:S(2)}, u32[]{:S(2)}) collective-permute-start(bf16[1536,512]{1,0:T(8,128)(2,1)} %get-tuple-element.26), channel_id=1, source_target_pairs={{0,2},{2,4},{4,6},{6,8},{8,10},{10,12},{12,14},{14,16},{16,18},{18... | collective-permute-start | bytes 4718600 | tf_op jit(solution)/shard_map/ppermute | solution.py:450
  26.5 3.8 %copy-start.3 = (bf16[1536,512]{1,0:T(8,128)(2,1)S(1)}, bf16[1536,512]{1,0:T(8,128)(2,1)}, u32[]{:S(2)}) copy-start(bf16[1536,512]{1,0:T(8,128)(2,1)} %q.11) | copy-start | bytes 4718596
  28.8 18.4 %collective-permute-start.5 = (bf16[768,512]{1,0:T(8,128)(2,1)}, bf16[768,512]{1,0:T(8,128)(2,1)}, u32[]{:S(2)}, u32[]{:S(2)}) collective-permute-start(bf16[768,512]{1,0:T(8,128)(2,1)} %broadcast_select_fusion), channel_id=1, source_target_pairs={{0,8},{16,24},{2,10},{18,26},{1,9},{17,25},{3,11},{19,27}} | collective-permute-start | bytes 2359304 | tf_op jit(solution)/shard_map/ppermute | solution.py:437
  43.1 33.4 %collective-permute-start.2 = (bf16[1536,512]{1,0:T(8,128)(2,1)}, bf16[1536,512]{1,0:T(8,128)(2,1)}, u32[]{:S(2)}, u32[]{:S(2)}) collective-permute-start(bf16[1536,512]{1,0:T(8,128)(2,1)} %maximum_select_fusion), channel_id=1, source_target_pairs={{0,4},{4,8},{8,12},{12,16},{16,20},{20,24},{24,28},{1,5},{5,9},{9,... | collective-permute-start | bytes 4718600 | tf_op jit(solution)/shard_map/ppermute | solution.py:454
  49.3 35.7 %collective-permute-start.6 = (bf16[768,512]{1,0:T(8,128)(2,1)}, bf16[768,512]{1,0:T(8,128)(2,1)}, u32[]{:S(2)}, u32[]{:S(2)}) collective-permute-start(bf16[768,512]{1,0:T(8,128)(2,1)} %broadcast_select_fusion.1), channel_id=1, source_target_pairs={{0,4},{8,12},{16,20},{24,28},{2,6},{10,14},{18,22},{26,30},{1,5},{... | collective-permute-start | bytes 2359304 | tf_op jit(solution)/shard_map/ppermute | solution.py:437
  50.6 46.9 %collective-permute-start.8 = (bf16[1536,512]{1,0:T(8,128)(2,1)}, bf16[1536,512]{1,0:T(8,128)(2,1)}, u32[]{:S(2)}, u32[]{:S(2)}) collective-permute-start(bf16[1536,512]{1,0:T(8,128)(2,1)} %collective-permute-done.near_k), channel_id=1, source_target_pairs={{0,2},{4,6},{8,10},{12,14},{16,18},{20,22},{24,26},{28,30},{1,3},{... | collective-permute-start | bytes 4718600 | tf_op jit(solution)/shard_map/ppermute | solution.py:462
  53.1 44.4 %collective-permute-start.9 = (bf16[1536,512]{1,0:T(8,128)(2,1)}, bf16[1536,512]{1,0:T(8,128)(2,1)}, u32[]{:S(2)}, u32[]{:S(2)}) collective-permute-start(bf16[1536,512]{1,0:T(8,128)(2,1)} %collective-permute-done.1.near_v), channel_id=1, source_target_pairs={{0,2},{4,6},{8,10},{12,14},{16,18},{20,22},{24,26},{28,30},{1,3},{... | collective-permute-start | bytes 4718600 | tf_op jit(solution)/shard_map/ppermute | solution.py:463
  78.9 7.4 %copy-start.5 = (bf16[1536,512]{1,0:T(8,128)(2,1)S(1)}, bf16[1536,512]{1,0:T(8,128)(2,1)}, u32[]{:S(2)}) copy-start(bf16[1536,512]{1,0:T(8,128)(2,1)} %q.11) | copy-start | bytes 4718596
  78.9 7.4 %copy-start.12 = (bf16[1536,128]{1,0:T(8,128)(2,1)S(1)}, bf16[1536,128]{1,0:T(8,128)(2,1)}, u32[]{:S(2)}) copy-start(bf16[1536,128]{1,0:T(8,128)(2,1)} %copy-done.11) | copy-start | bytes 1179652
  86.1 11.3 %collective-permute-start.7 = (bf16[768,512]{1,0:T(8,128)(2,1)S(1)}, bf16[768,512]{1,0:T(8,128)(2,1)S(1)}, u32[]{:S(2)}, u32[]{:S(2)}) collective-permute-start(bf16[768,512]{1,0:T(8,128)(2,1)S(1)} %broadcast_select_fusion.2.sink_a), channel_id=1, source_target_pairs={{0,2},{2,0},{4,6},{6,4},{8,10},{10,8},{12,14},{14,12},{16,18},{18,... | collective-permute-start | bytes 2359304 | tf_op jit(solution)/shard_map/ppermute | solution.py:460
  86.2 1.4 %copy-start.16 = (f32[1536,256]{1,0:T(8,128)S(1)}, f32[1536,256]{1,0:T(8,128)}, u32[]{:S(2)}) copy-start(f32[1536,256]{1,0:T(8,128)} %copy-done.15) | copy-start | bytes 4718596
  97.5 10.6 %copy-start.8 = (f32[1536,256]{1,0:T(8,128)S(1)}, f32[1536,256]{1,0:T(8,128)}, u32[]{:S(2)}) copy-start(f32[1536,256]{1,0:T(8,128)} %copy-done.7) | copy-start | bytes 4718596
  97.5 10.6 %copy-start.10 = (f32[1536,128]{1,0:T(8,128)S(1)}, f32[1536,128]{1,0:T(8,128)}, u32[]{:S(2)}) copy-start(f32[1536,128]{1,0:T(8,128)} %copy-done.9) | copy-start | bytes 2359300
  106.5 11.6 %collective-permute-start.11 = (bf16[768,256]{1,0:T(8,128)(2,1)S(1)}, bf16[768,256]{1,0:T(8,128)(2,1)S(1)}, u32[]{:S(2)}, u32[]{:S(2)}) collective-permute-start(bf16[768,256]{1,0:T(8,128)(2,1)S(1)} %get-tuple-element.40), channel_id=1, source_target_pairs={{0,1},{1,0},{2,3},{3,2},{4,5},{5,4},{6,7},{7,6},{8,9},{9,8},{10,11... | collective-permute-start | bytes 1179656 | tf_op jit(solution)/shard_map/ppermute | solution.py:485
  108.1 20.5 %copy-start.6 = (bf16[1024,1536]{1,0:T(8,128)(2,1)S(1)}, bf16[1024,1536]{1,0:T(8,128)(2,1)}, u32[]{:S(2)}) copy-start(bf16[1024,1536]{1,0:T(8,128)(2,1)} %refs_4_.1) | copy-start | bytes 9437188
  117.3 11.3 %collective-permute-start.10 = (bf16[768,256]{1,0:T(8,128)(2,1)S(1)}, bf16[768,256]{1,0:T(8,128)(2,1)S(1)}, u32[]{:S(2)}, u32[]{:S(2)}) collective-permute-start(bf16[768,256]{1,0:T(8,128)(2,1)S(1)} %get-tuple-element.39), channel_id=1, source_target_pairs={{0,1},{1,0},{2,3},{3,2},{4,5},{5,4},{6,7},{7,6},{8,9},{9,8},{10,11... | collective-permute-start | bytes 1179656 | tf_op jit(solution)/shard_map/ppermute | solution.py:485
  (12 other events, 13.3 us)

commit v2 on v1

--- a/solution.py
+++ b/solution.py
@@ -33,28 +33,22 @@
     return slice(slot * FT, (slot + 1) * FT)
 
 
-def extended_scores(q, kt, j):
-    return dot(q, kt[:, j * BK : (j + 1) * BK])
-
-
 def add_frame(lanes, kt, values):
     units = [(n, j) for n in range(len(lanes)) for j in range(FT // BK)]
 
-    def fetch(unit):
+    def scores(unit):
         n, j = unit
-        return extended_scores(lanes[n][0], kt, j)
-
-    ahead = fetch(units[0])
+        return dot(lanes[n][0], kt[:, j * BK : (j + 1) * BK])
+
+    ahead = scores(units[0])
     weights = []
     for at, (n, j) in enumerate(units):
         s = ahead
         if at + 1 < len(units):
-            ahead = fetch(units[at + 1])
-        _, shift, add = lanes[n]
-        for c in range(0, BK, HD):
-            weights.append(jnp.exp2(s[:, c : c + HD] * SCALE - shift).astype(jnp.bfloat16))
+            ahead = scores(units[at + 1])
+        weights.append(jnp.exp2(s * SCALE).astype(jnp.bfloat16))
         if j == FT // BK - 1:
-            add(dot(jnp.concatenate(weights, axis=1), values[...]))
+            lanes[n][1](dot(jnp.concatenate(weights, axis=1), values[...]))
             weights = []
 
 
@@ -71,13 +65,23 @@
 def spread(packed, h, heads):
     row = lax.broadcasted_iota(jnp.int32, (HD, HD), 0)
     chosen = jnp.where(row == h * (HD // heads), 1.0, 0.0).astype(jnp.bfloat16)
-    return dot(packed, chosen)
-
-
-def spread_sum(packed, h, heads):
     high = packed.astype(jnp.bfloat16)
     low = (packed - high.astype(jnp.float32)).astype(jnp.bfloat16)
-    return spread(high, h, heads) + spread(low, h, heads)
+    return dot(high, chosen) + dot(low, chosen)
+
+
+def more_columns(own, slot):
+    lane = lax.broadcasted_iota(jnp.int32, (1, HD), 1)
+    flag = jnp.where(lane == 1 + slot, 1.0, 0.0)
+    return jnp.where(lane == 0, -own, flag).astype(jnp.bfloat16)
+
+
+def set_more_rows(kt, seen):
+    row = lax.broadcasted_iota(jnp.int32, (HD, FT), 0)
+    more = jnp.where(row == 0, 1.0, 0.0)
+    for slot, shown in enumerate(seen):
+        more = jnp.where(row == 1 + slot, jnp.where(shown, 0.0, -HIDDEN), more)
+    kt[HD:, :] = more.astype(jnp.bfloat16)
 
 
 def sums_into(acc_from, acc, sums, rows, column, h, heads):
@@ -91,7 +95,7 @@
 
 
 def load_frame(kt, values, k, v, column):
-    kt[...] = k[:, column].T
+    kt[:HD, :] = k[:, column].T
     values[:, :HD] = v[:, column]
 
 
@@ -106,7 +110,7 @@
 
 
 def own_kernel(group, info, q, k, v, *refs):
-    m, acc, sums, token, kt, values = refs[-6:]
+    more, acc, sums, token, kt, values = refs[-6:]
     if len(refs) > 6:
         refs[0][...] = v[...]
     heads = group[1]
@@ -114,32 +118,32 @@
     token[...] = jnp.zeros_like(token)
     values[:, HD:] = jnp.ones((FT, HD), jnp.bfloat16)
     ones = jnp.ones((HD, HD), jnp.bfloat16)
-    m[...] = jnp.zeros_like(m)
     sums[...] = jnp.zeros_like(sums)
 
-    def turn(h, column, wide):
-        here = lanes_of(h, heads)
+    def shifts(h, column, wide):
         for slot in (0, 1):
             rows = rows_of(slot)
             product = q[rows, wide].astype(jnp.float32) * k[rows, wide].astype(jnp.float32)
-            own = (dot(product.astype(jnp.bfloat16), ones) * SCALE).astype(jnp.bfloat16)
-            m[rows, :] = jnp.where(here, own, m[rows, :])
-        for frame in (0, 1):
+            more[rows, column] = more_columns(dot(product.astype(jnp.bfloat16), ones), slot)
+
+    each_head(group, shifts)
+    for frame in (0, 1):
+        set_more_rows(kt, [visible(info, slot, first + frame) for slot in (0, 1)])
+
+        def turn(h, column, wide):
             load_frame(kt, values, k.at[rows_of(frame)], v.at[rows_of(frame)], wide)
             lanes = []
             for slot in (0, 1):
                 rows = rows_of(slot)
-                shift = spread(m[rows, :], h, heads)
-                shift = jnp.where(visible(info, slot, first + frame), shift, HIDDEN)
-                acc_from = acc if frame else None
-                add = sums_into(acc_from, acc, sums, rows, column, h, heads)
-                lanes.append((q[rows, wide], shift, add))
+                add = sums_into(acc if frame else None, acc, sums, rows, column, h, heads)
+                queries = jnp.concatenate([q[rows, wide], more[rows, column]], axis=1)
+                lanes.append((queries, add))
             add_frame(lanes, kt, values)
 
-    each_head(group, turn)
-
-
-def near_kernel(group, info, q, m, acc_in, sums_in, near_k, near_v, *refs):
+        each_head(group, turn)
+
+
+def near_kernel(group, info, q, more, acc_in, sums_in, near_k, near_v, *refs):
     acc, sums, token, kt, values, k_buf, v_buf, sem = refs
     offset, heads = group
     token[...] = jnp.zeros_like(token)
@@ -162,6 +166,7 @@
     values[:, HD:] = jnp.ones((FT, HD), jnp.bfloat16)
     sums[...] = sums_in[...]
     for frame in order:
+        set_more_rows(kt, [visible(info, slot, first - 2 + frame) for slot in (0, 1)])
         for copy in copies[frame]:
             copy.wait()
 
@@ -171,17 +176,16 @@
             lanes = []
             for slot in (0, 1):
                 rows = rows_of(slot)
-                shift = spread(m[rows, :], h, heads)
-                shift = jnp.where(visible(info, slot, first - 2 + frame), shift, HIDDEN)
                 add = sums_into(acc_from, acc, sums, rows, column, h, heads)
-                lanes.append((q[rows, wide], shift, add))
+                queries = jnp.concatenate([q[rows, wide], more[rows, column]], axis=1)
+                lanes.append((queries, add))
             add_frame(lanes, kt, values)
 
         each_head(group, turn)
 
 
 def final_kernel(
-    group, info, q, m, acc_in, sums_in,
+    group, info, q, more, acc_in, sums_in,
     sink_a, sink_b, far, relay_k, relay_v, key_any, value_any, near_k, near_v, *refs,
 ):
     outs = refs[:-8]
@@ -245,17 +249,19 @@
 
             return add
 
-        shifts = [spread(m[rows_of(slot), :], h, heads) for slot in (0, 1)]
+        queries = [
+            jnp.concatenate([q[rows_of(slot), wide], more[rows_of(slot), column]], axis=1)
+            for slot in (0, 1)
+        ]
         load_frame(kt, values, k_buf.at[0], v_buf.at[0], column)
-        add_frame(
-            [(q[rows_of(slot), wide], shifts[slot], keep(slot)) for slot in (1, 0)], kt, values
-        )
+        set_more_rows(kt, [True, True])
+        add_frame([(queries[slot], keep(slot)) for slot in (1, 0)], kt, values)
         load_frame(kt, values, k_buf.at[1], v_buf.at[1], column)
-        shown = jnp.where(far_seen, shifts[0], HIDDEN)
-        add_frame([(q[rows_of(0), wide], shown, keep(0))], kt, values)
+        set_more_rows(kt, [far_seen, False])
+        add_frame([(queries[0], keep(0))], kt, values)
         for slot in (0, 1):
             rows = rows_of(slot)
-            total = spread_sum(sums_in[rows, :], h, heads) + results[slot][:, HD:]
+            total = spread(sums_in[rows, :], h, heads) + results[slot][:, HD:]
             write(slot, h, acc_in[rows, column] + results[slot][:, :HD], total)
             too_large[h, slot] = jnp.max(jnp.where(total < LIMIT, 0.0, 1.0))
 
@@ -303,18 +309,26 @@
 
         queries = q[rows_of(slot), wide]
 
+        def scores(j):
+            return dot(queries, kt[:HD, j * BK : (j + 1) * BK]) * SCALE
+
         def peak():
             for j in range(FT // BK):
-                most = jnp.max(extended_scores(queries, kt, j), axis=1, keepdims=True) * SCALE
-                shift[...] = jnp.maximum(shift[...], most)
-
-        def more(added):
-            acc[...] = acc[...] + added
+                shift[...] = jnp.maximum(shift[...], jnp.max(scores(j), axis=1, keepdims=True))
+
+        def more_sums():
+            for j in range(FT // BK):
+                s = scores(j)
+                weights = jnp.concatenate(
+                    [jnp.exp2(s[:, c : c + HD] - shift[...]) for c in range(0, BK, HD)], axis=1
+                )
+                keys = values[j * BK : (j + 1) * BK, :]
+                acc[...] = acc[...] + dot(weights.astype(jnp.bfloat16), keys)
 
         shift[...] = jnp.full((FT, HD), -jnp.inf, jnp.float32)
         acc[...] = jnp.zeros((FT, 2 * HD), jnp.float32)
         sweep(peak)
-        sweep(lambda: add_frame([(queries, shift[...], more)], kt, values))
+        sweep(more_sums)
         write(slot, h, acc[:, :HD], acc[:, HD:])
 
     def check(h, column, wide):
@@ -328,22 +342,62 @@
 SMEM_SPEC = pl.BlockSpec(memory_space=pltpu.SMEM)
 
 
-def stage(kernel, arrays, in_any, outs, scratch, cost=None):
+def stage(kernel, arrays, in_any, outs, scratch, cost=None, tokens=()):
+    n = len(arrays)
+
+    def run(*refs):
+        kernel(*refs[:n], *refs[n + len(tokens) :])
+
     return pl.pallas_call(
-        kernel,
-        in_specs=[SMEM_SPEC] + [VMEM_SPEC] * (len(arrays) - in_any - 1) + [ANY_SPEC] * in_any,
+        run,
+        in_specs=[SMEM_SPEC] + [VMEM_SPEC] * (n - in_any - 1)
+        + [ANY_SPEC] * (in_any + len(tokens)),
         out_specs=[VMEM_SPEC] * len(outs),
         scratch_shapes=[
-            pltpu.VMEM((HD, FT), jnp.bfloat16), pltpu.VMEM((FT, 2 * HD), jnp.bfloat16)
+            pltpu.VMEM((2 * HD, FT), jnp.bfloat16), pltpu.VMEM((FT, 2 * HD), jnp.bfloat16)
         ] + list(scratch),
         out_shape=outs,
         compiler_params=PARAMS,
         cost_estimate=cost or COST,
-    )(*arrays)
-
-
-def last_frames(keys, values):
-    return jnp.concatenate([keys[FT:], values[FT:]], axis=0)
+    )(*arrays, *tokens)
+
+
+def small(kernel, scalars, arrays, tokens, rows):
+    width = arrays[0].shape[1]
+    n = len(arrays)
+
+    def run(scalars, *refs):
+        kernel(scalars, *refs[:n], refs[-1])
+
+    return pl.pallas_call(
+        run,
+        in_specs=[SMEM_SPEC] + [VMEM_SPEC] * n + [ANY_SPEC] * len(tokens),
+        out_specs=VMEM_SPEC,
+        out_shape=jax.ShapeDtypeStruct((rows, width), jnp.bfloat16),
+        compiler_params=PARAMS,
+        cost_estimate=COST,
+    )(jnp.reshape(scalars, (1,)).astype(jnp.int32), *arrays, *tokens)
+
+
+def pick(flag, taken, kept, tokens=()):
+    def kernel(flag, taken, kept, out):
+        @pl.when(flag[0] == 1)
+        def _():
+            out[...] = taken[:FT, :]
+
+        @pl.when(flag[0] == 0)
+        def _():
+            out[...] = kept[:FT, :]
+
+    return small(kernel, flag, [taken, kept], tokens, FT)
+
+
+def last_frames(keys, values, tokens=()):
+    def kernel(_, keys, values, out):
+        out[:FT, :] = keys[FT:, :]
+        out[FT:, :] = values[FT:, :]
+
+    return small(kernel, jnp.zeros((), jnp.int32), [keys, values], tokens, 2 * FT)
 
 
 def sink_steps(size):
@@ -410,7 +464,7 @@
     rows, width = query_states.shape
     q_like = jax.ShapeDtypeStruct((rows, width), jnp.bfloat16)
     group_width = groups[0][1] * HD
-    m_like = jax.ShapeDtypeStruct((rows, HD), jnp.bfloat16)
+    more_like = jax.ShapeDtypeStruct((rows, group_width), jnp.bfloat16)
     acc_like = jax.ShapeDtypeStruct((rows, group_width), jnp.float32)
     sums_like = jax.ShapeDtypeStruct((rows, HD), jnp.float32)
     frame_buffers = [pltpu.VMEM((2, FT, group_width), jnp.bfloat16)] * 2
@@ -419,10 +473,7 @@
     onward = [(i, i + 1) for i in range(size - 1)]
     near_k = lax.ppermute(key_states, axis, onward)
     moved = lax.ppermute(value_states, axis, [(0, 1)])
-    held = jnp.where(core == 0, key_states[:FT], moved[:FT])
-
-    def arrived(array):
-        return array[0, 0] == array[0, 0]
+    held = pick(core, moved, key_states)
 
     def near_stage(group, state):
         return stage(
@@ -436,27 +487,29 @@
     for step, pairs in enumerate(steps):
         moved = lax.ppermute(held, axis, pairs)
         takes = jnp.zeros((), bool)
+        tokens = []
         for _, target in pairs:
             takes = takes | (me == target)
         if step < len(groups):
-            *passed, m, acc, sums, token = stage(
+            *passed, more, acc, sums, token = stage(
                 functools.partial(own_kernel, groups[step]),
                 [info, query_states, key_states, value_states], 0,
-                [q_like] * (step == 0) + [m_like, acc_like, sums_like, TOKEN], [],
+                [q_like] * (step == 0) + [more_like, acc_like, sums_like, TOKEN], [],
+                tokens=[held] * (step > 0),
             )
-            states.append((m, acc, sums))
-            takes = takes & (token[0, 0] == 0)
+            states.append((more, acc, sums))
+            tokens.append(token)
             if step == 0:
                 near_v = lax.ppermute(passed[0], axis, onward)
-                takes = takes & arrived(near_k)
+                tokens.append(near_k)
             if step == len(groups) - 1:
-                own_last = jnp.where(token[0, 0] == 0, last_frames(key_states, value_states), 0)
+                own_last = last_frames(key_states, value_states, [token])
                 far = lax.ppermute(own_last, axis, [(i, i + 2) for i in range(0, size - 2, 2)])
         if step == len(steps) - 1:
             *sums_now, token = near_stage(groups[0], states[0])
             states[0] = states[0][0], *sums_now
-            takes = takes & (token[0, 0] == 0) & arrived(far)
-        held = jnp.where(takes, moved, held)
+            tokens += [token, far]
+        held = pick(takes, moved, held, tokens)
     other = lax.ppermute(held, axis, [(i, i ^ 1) for i in range(size)])
     on_chip = [(i, i + 1) for i in range(0, size, 2)]
     relay_k = lax.ppermute(near_k, axis, on_chip)

time: 136 us -> 130 us (0.956)
  other arithmetic: 10.2 us -> 0 us
  Pallas kernels: 54.3 us -> 63.8 us
  waiting for transfers between devices: 22.6 us -> 29 us
  between operations: 4.72 us -> 0.3 us
  local copies, waits for them, and re-layouts: 19.1 us -> 14.9 us
  starting transfers between devices: 22.8 us -> 21 us
    ppermute x3, waiting for transfers between devices: 6.06 us -> 19 us  [local(): moved = lax.ppermute(held, axis, pairs)]
    pallas_call x6 -> x11, Pallas kernels: 49.2 us -> 58.6 us  [the longest x6 49.7 us: stage(): pl.pallas_call(run, in_specs=[SMEM_SPEC] + [VMEM_SPEC] * (n - in_any - 1)...]
    select_n x4 -> x0, other arithmetic: 7.13 us -> none  [the longest x3 5.61 us: local(): held = jnp.where(takes, moved, held)]
    ppermute x1, waiting for transfers between devices: 5.82 us -> 0.01 us  [local(): lax.ppermute(own_last, axis, [(i, i + 2) for i in range(0, size - 2, 2)])]
    slice x6 -> x0, local copies, waits for them, and re-layouts: 4.15 us -> none  [the longest x2 2.43 us: arrived(): return array[0, 0] == array[0, 0]]
    slice x1 -> x0, other arithmetic: 3.09 us -> none  [last_frames(): return jnp.concatenate([keys[FT:], values[FT:]], axis=0)]
    unnamed x48 -> x50, local copies, waits for them, and re-layouts: 14.8 us -> 14.8 us
  transfers between devices with their start and end apart: 12 -> 12, of which waited for: 4 -> 2; matrix products, arithmetic and copies ran while one was open for 11% -> 0% of each run, Pallas kernels for 30% -> 39%
where the time goes in v2:
time: 130 us; the launch traced here: 129 us
  Pallas kernels  63.8 us (49%)
  waiting for transfers between devices  29 us (22%)
  starting transfers between devices  21 us (16%)
  local copies, waits for them, and re-layouts  14.9 us (11%)
    pallas_call x6, Pallas kernels, stage(): pl.pallas_call(run, in_specs=[SMEM_SPEC] + [VMEM_SPEC] * (n - in_any - 1)...  49.7 us
    ppermute x3, waiting for transfers between devices, local(): moved = lax.ppermute(held, axis, pairs)  19 us
    unnamed x50, local copies, waits for them, and re-layouts  14.8 us
    ppermute x2, waiting for transfers between devices, local(): theirs.append(lax.ppermute(results[1], 'head', [(0, 1), (1, 0)]))  10 us
    pallas_call x5, Pallas kernels, small(): pl.pallas_call(run, in_specs=[SMEM_SPEC] + [VMEM_SPEC] * n + [ANY_SPEC] *...  8.96 us
    pallas_call x1, Pallas kernels, project(): pl.pallas_call(kernel, grid=(turns,), in_specs=[SMEM_SPEC] + [VMEM_SPEC]...  5.15 us
    ppermute x3, starting transfers between devices, local(): moved = lax.ppermute(held, axis, pairs)  4.51 us
    ppermute x1, starting transfers between devices, local(): near_v = lax.ppermute(passed[0], axis, onward)  3.56 us
  transfers between devices with their start and end apart: 12, of which 2 were waited for; matrix products, arithmetic and copies ran while one was open for 0% of the time, Pallas kernels for 39%

profile of v2, /device:TPU:18, one launch (start us, length us, event | category | flops | bytes accessed | tf_op | source)
XLA Modules:
  0.0 129.1 jit_solution(844993783103542368)
XLA Ops:
  0.8 1.9 %collective-permute-start = (bf16[1536,512]{1,0:T(8,128)(2,1)}, bf16[1536,512]{1,0:T(8,128)(2,1)}, u32[]{:S(2)}, u32[]{:S(2)}) collective-permute-start(bf16[1536,512]{1,0:T(8,128)(2,1)} %refs_10_.3), channel_id=1, source_target_pairs={{0,2},{2,4},{4,6},{6,8},{8,10},{10,12},{12,14},{14,16},{16,18},{18... | collective-permute-start | bytes 4718600 | tf_op jit(solution)/shard_map/ppermute | solution.py:474
  3.9 1.4 %copy-done = bf16[1536,512]{1,0:T(8,128)(2,1)S(1)} copy-done((bf16[1536,512]{1,0:T(8,128)(2,1)S(1)}, bf16[1536,512]{1,0:T(8,128)(2,1)}, u32[]{:S(2)}) %copy-start) | copy-done | bytes 1572888
  5.3 1.4 %copy-done.9 = bf16[1536,512]{1,0:T(8,128)(2,1)S(1)} copy-done((bf16[1536,512]{1,0:T(8,128)(2,1)S(1)}, bf16[1536,512]{1,0:T(8,128)(2,1)}, u32[]{:S(2)}) %copy-start.9) | copy-done | bytes 1572888
  7.7 1.7 %collective-permute-start.3 = (bf16[768,512]{1,0:T(8,128)(2,1)}, bf16[768,512]{1,0:T(8,128)(2,1)}, u32[]{:S(2)}, u32[]{:S(2)}) collective-permute-start(bf16[768,512]{1,0:T(8,128)(2,1)} %shard_map.66.refs_1_), channel_id=1, source_target_pairs={{0,16},{2,18},{1,17},{3,19}} | collective-permute-start | bytes 2359304 | tf_op jit(solution)/shard_map/ppermute | solution.py:488
  10.9 8.4 %shard_map.64 = (bf16[1536,512]{1,0:T(8,128)(2,1)}, bf16[1536,256]{1,0:T(8,128)(2,1)S(1)}, f32[1536,256]{1,0:T(8,128)S(1)}, f32[1536,128]{1,0:T(8,128)S(1)}, f32[8,128]{1,0:T(8,128)S(1)}) custom-call(s32[7]{0:T(128)S(1)} %concatenate.3.refs_0_.info, bf16[1536,512]{1,0:T(8,128)(2,1)S(1)} %copy-done.3, bf16[1536,512]{1,0:T(8,128)(2,1)S(1)} %copy-done.1, ...), custom_call_target="tpu_custom_call" | custom-call | flops 1000 | bytes 1000 | tf_op jit(solution)/shard_map/pallas_call | solution.py:351
  22.2 3.6 %collective-permute-start.1 = (bf16[1536,512]{1,0:T(8,128)(2,1)}, bf16[1536,512]{1,0:T(8,128)(2,1)}, u32[]{:S(2)}, u32[]{:S(2)}) collective-permute-start(bf16[1536,512]{1,0:T(8,128)(2,1)} %get-tuple-element.26), channel_id=1, source_target_pairs={{0,2},{2,4},{4,6},{6,8},{8,10},{10,12},{12,14},{14,16},{16,18},{18... | collective-permute-start | bytes 4718600 | tf_op jit(solution)/shard_map/ppermute | solution.py:503
  25.8 2.5 %shard_map.67.refs_4_.refs_1_ = bf16[768,512]{1,0:T(8,128)(2,1)} custom-call(s32[1]{0:T(128)} %bitcast.5.scalars, bf16[768,512]{1,0:T(8,128)(2,1)} %collective-permute-done.3.refs_0_, bf16[768,512]{1,0:T(8,128)(2,1)} %shard_map.66.refs_1_, f32[8,128]{1,0:T(8,128)S(1)} %get-tuple-element.29.refs_2_, ...), custom_call_target="tpu_custom_call" | custom-call | flops 1000 | bytes 1000 | tf_op jit(solution)/shard_map/pallas_call | solution.py:372
  28.3 1.5 %collective-permute-start.4 = (bf16[768,512]{1,0:T(8,128)(2,1)}, bf16[768,512]{1,0:T(8,128)(2,1)}, u32[]{:S(2)}, u32[]{:S(2)}) collective-permute-start(bf16[768,512]{1,0:T(8,128)(2,1)} %shard_map.67.refs_4_.refs_1_), channel_id=1, source_target_pairs={{0,8},{16,24},{2,10},{18,26},{1,9},{17,25},{3,11},{19,27}} | collective-permute-start | bytes 2359304 | tf_op jit(solution)/shard_map/ppermute | solution.py:488
  29.9 7.2 %shard_map.68 = (bf16[1536,256]{1,0:T(8,128)(2,1)S(1)}, f32[1536,256]{1,0:T(8,128)S(1)}, f32[1536,128]{1,0:T(8,128)S(1)}, f32[8,128]{1,0:T(8,128)S(1)}) custom-call(s32[7]{0:T(128)S(1)} %concatenate.3.refs_0_.info, bf16[1536,512]{1,0:T(8,128)(2,1)S(1)} %copy-done.4, bf16[1536,512]{1,0:T(8,128)(2,1)S(1)} %copy-done.1, bf16[1536,512]{1,0:T(8,128)(2,1)S(1)} %copy-done.2, ...), custom_call_target="tpu_custom_call" | custom-call | flops 1000 | bytes 1000 | tf_op jit(solution)/shard_map/pallas_call | solution.py:351
  37.1 1.4 %shard_map.70 = bf16[1536,512]{1,0:T(8,128)(2,1)} custom-call(s32[1]{0:T(128)} %constant.48.clone.1.scalars, bf16[1536,512]{1,0:T(8,128)(2,1)S(1)} %copy-done.1, bf16[1536,512]{1,0:T(8,128)(2,1)S(1)} %copy-done.2, f32[8,128]{1,0:T(8,128)S(1)} %get-tuple-element.30.refs_2_), custom_call_target="tpu_custom_call" | custom-call | flops 1000 | bytes 1000 | tf_op jit(solution)/shard_map/pallas_call | solution.py:372
  39.2 3.1 %collective-permute-start.6 = (bf16[1536,512]{1,0:T(8,128)(2,1)}, bf16[1536,512]{1,0:T(8,128)(2,1)}, u32[]{:S(2)}, u32[]{:S(2)}) collective-permute-start(bf16[1536,512]{1,0:T(8,128)(2,1)} %shard_map.70), channel_id=1, source_target_pairs={{0,4},{4,8},{8,12},{12,16},{16,20},{20,24},{24,28},{1,5},{5,9},{9,... | collective-permute-start | bytes 4718600 | tf_op jit(solution)/shard_map/ppermute | solution.py:507
  42.4 2.3 %shard_map.69.refs_1_ = bf16[768,512]{1,0:T(8,128)(2,1)} custom-call(s32[1]{0:T(128)} %bitcast.4.scalars, bf16[768,512]{1,0:T(8,128)(2,1)} %collective-permute-done.4.refs_0_, bf16[768,512]{1,0:T(8,128)(2,1)} %shard_map.67.refs_4_.refs_1_, f32[8,128]{1,0:T(8,128)S(1)} %get-tuple-element.30.refs_2_), custom_call_target="tpu_custom_call" | custom-call | flops 1000 | bytes 1000 | tf_op jit(solution)/shard_map/pallas_call | solution.py:372
  46.0 2.4 %collective-permute-start.9 = (bf16[1536,512]{1,0:T(8,128)(2,1)}, bf16[1536,512]{1,0:T(8,128)(2,1)}, u32[]{:S(2)}, u32[]{:S(2)}) collective-permute-start(bf16[1536,512]{1,0:T(8,128)(2,1)} %collective-permute-done.1.refs_6_.refs_13_), channel_id=1, source_target_pairs={{0,2},{4,6},{8,10},{12,14},{16,18},{20,22},{24,26},{28,30},{1,3},{... | collective-permute-start | bytes 4718600 | tf_op jit(solution)/shard_map/ppermute | solution.py:516
  48.5 2.5 %collective-permute-start.8 = (bf16[1536,512]{1,0:T(8,128)(2,1)}, bf16[1536,512]{1,0:T(8,128)(2,1)}, u32[]{:S(2)}, u32[]{:S(2)}) collective-permute-start(bf16[1536,512]{1,0:T(8,128)(2,1)} %collective-permute-done.refs_5_.refs_3_.refs_12_), channel_id=1, source_target_pairs={{0,2},{4,6},{8,10},{12,14},{16,18},{20,22},{24,26},{28,30},{1,3},{... | collective-permute-start | bytes 4718600 | tf_op jit(solution)/shard_map/ppermute | solution.py:515
  51.0 1.4 %copy-done.5 = bf16[1536,512]{1,0:T(8,128)(2,1)S(1)} copy-done((bf16[1536,512]{1,0:T(8,128)(2,1)S(1)}, bf16[1536,512]{1,0:T(8,128)(2,1)}, u32[]{:S(2)}) %copy-start.5) | copy-done | bytes 1572888
  56.0 7.7 %shard_map.65 = (f32[1536,256]{1,0:T(8,128)S(1)}, f32[1536,128]{1,0:T(8,128)S(1)}, f32[8,128]{1,0:T(8,128)S(1)}) custom-call(s32[7]{0:T(128)S(1)} %concatenate.3.refs_0_.info, bf16[1536,512]{1,0:T(8,128)(2,1)S(1)} %copy-done.5, bf16[1536,256]{1,0:T(8,128)(2,1)S(1)} %copy-done.11, f32[1536,256]{1,0:T(8,128)S(1)} %copy-done.16, f32[1536,128]{1,0:T(8,128)S(1)} %copy-done.20, ...), custom_call_target="tpu_custom_call" | custom-call | flops 8000000000 | bytes 1000 | tf_op jit(solution)/shard_map/pallas_call | solution.py:351
  63.8 19.0 %collective-permute-done.5.refs_0_ = bf16[768,512]{1,0:T(8,128)(2,1)} collective-permute-done((bf16[768,512]{1,0:T(8,128)(2,1)}, bf16[768,512]{1,0:T(8,128)(2,1)}, u32[]{:S(2)}, u32[]{:S(2)}) %collective-permute-start.5) | collective-permute-done | bytes 786464 | tf_op jit(solution)/shard_map/ppermute | solution.py:488
  82.8 1.8 %shard_map.71.refs_5_ = bf16[768,512]{1,0:T(8,128)(2,1)S(1)} custom-call(s32[1]{0:T(128)} %bitcast.3.scalars, bf16[768,512]{1,0:T(8,128)(2,1)} %collective-permute-done.5.refs_0_, bf16[768,512]{1,0:T(8,128)(2,1)} %shard_map.69.refs_1_, f32[8,128]{1,0:T(8,128)S(1)} %get-tuple-element.31.refs_2_, bf16[1536,512]{1,0:T(8,128)(2,1)} %collective-permute-done.6.refs_3_.refs_7_), custom_call_target="tpu_custom_call" | custom-call | flops 1000 | bytes 1000 | tf_op jit(solution)/shard_map/pallas_call | solution.py:372
  85.4 8.3 %shard_map.73 = (f32[1536,256]{1,0:T(8,128)S(1)}, f32[1536,128]{1,0:T(8,128)S(1)}, f32[8,128]{1,0:T(8,128)}) custom-call(s32[7]{0:T(128)S(1)} %concatenate.3.refs_0_.info, bf16[1536,512]{1,0:T(8,128)(2,1)S(1)} %copy-done.6, bf16[1536,256]{1,0:T(8,128)(2,1)S(1)} %copy-done.14, f32[1536,256]{1,0:T(8,128)S(1)} %copy-done.18, f32[1536,128]{1,0:T(8,128)S(1)} %copy-done.22, ...), custom_call_target="tpu_custom_call" | custom-call | flops 8000000000 | bytes 1000 | tf_op jit(solution)/shard_map/pallas_call | solution.py:351
  93.8 8.8 %shard_map.74 = (bf16[768,256]{1,0:T(8,128)(2,1)S(1)}, bf16[768,256]{1,0:T(8,128)(2,1)S(1)}) custom-call(s32[7]{0:T(128)S(1)} %concatenate.3.refs_0_.info, bf16[1536,512]{1,0:T(8,128)(2,1)S(1)} %copy-done.6, bf16[1536,256]{1,0:T(8,128)(2,1)S(1)} %copy-done.14, f32[1536,256]{1,0:T(8,128)S(1)} %get-tuple-element.36.refs_3_, ...), custom_call_target="tpu_custom_call" | custom-call | flops 1000 | bytes 1000 | tf_op jit(solution)/shard_map/pallas_call | solution.py:351
  102.6 1.6 %collective-permute-start.11 = (bf16[768,256]{1,0:T(8,128)(2,1)S(1)}, bf16[768,256]{1,0:T(8,128)(2,1)S(1)}, u32[]{:S(2)}, u32[]{:S(2)}) collective-permute-start(bf16[768,256]{1,0:T(8,128)(2,1)S(1)} %get-tuple-element.40), channel_id=1, source_target_pairs={{0,1},{1,0},{2,3},{3,2},{4,5},{5,4},{6,7},{7,6},{8,9},{9,8},{10,11... | collective-permute-start | bytes 1179656 | tf_op jit(solution)/shard_map/ppermute | solution.py:538
  104.2 9.1 %shard_map.72 = (bf16[768,256]{1,0:T(8,128)(2,1)S(1)}, bf16[768,256]{1,0:T(8,128)(2,1)S(1)}) custom-call(s32[7]{0:T(128)S(1)} %concatenate.3.refs_0_.info, bf16[1536,512]{1,0:T(8,128)(2,1)S(1)} %copy-done.6, bf16[1536,256]{1,0:T(8,128)(2,1)S(1)} %copy-done.12, f32[1536,256]{1,0:T(8,128)S(1)} %get-tuple-element.27.refs_3_, ...), custom_call_target="tpu_custom_call" | custom-call | flops 1000 | bytes 1000 | tf_op jit(solution)/shard_map/pallas_call | solution.py:351
  113.9 10.0 %collective-permute-done.10.refs_2_ = bf16[768,256]{1,0:T(8,128)(2,1)S(1)} collective-permute-done((bf16[768,256]{1,0:T(8,128)(2,1)S(1)}, bf16[768,256]{1,0:T(8,128)(2,1)S(1)}, u32[]{:S(2)}, u32[]{:S(2)}) %collective-permute-start.10) | collective-permute-done | bytes 393248 | tf_op jit(solution)/shard_map/ppermute | solution.py:538
  123.9 5.2 %shard_map.75 = bf16[768,1536]{1,0:T(8,128)(2,1)} custom-call(s32[7]{0:T(128)S(1)} %concatenate.3.refs_0_.info, bf16[768,256]{1,0:T(8,128)(2,1)S(1)} %get-tuple-element.32.refs_0_, bf16[768,256]{1,0:T(8,128)(2,1)S(1)} %get-tuple-element.38.refs_1_, bf16[768,256]{1,0:T(8,128)(2,1)S(1)} %collective-permute-done.10.refs_2_, ...), custom_call_target="tpu_custom_call" | custom-call | flops 1000 | bytes 1000 | tf_op jit(solution)/shard_map/pallas_call | solution.py:437
  (63 shorter events, 14.4 us)
Async XLA Ops:
  0.0 2.7 %collective-permute-start.2 = (bf16[1536,512]{1,0:T(8,128)(2,1)}, bf16[1536,512]{1,0:T(8,128)(2,1)S(1)}, u32[]{:S(2)}, u32[]{:S(2)}) collective-permute-start(bf16[1536,512]{1,0:T(8,128)(2,1)} %refs_11_.3), channel_id=1, source_target_pairs={{0,2},{1,3}} | collective-permute-start | bytes 4718600 | tf_op jit(solution)/shard_map/ppermute | solution.py:475
  0.8 25.0 %collective-permute-start = (bf16[1536,512]{1,0:T(8,128)(2,1)}, bf16[1536,512]{1,0:T(8,128)(2,1)}, u32[]{:S(2)}, u32[]{:S(2)}) collective-permute-start(bf16[1536,512]{1,0:T(8,128)(2,1)} %refs_10_.3), channel_id=1, source_target_pairs={{0,2},{2,4},{4,6},{6,8},{8,10},{10,12},{12,14},{14,16},{16,18},{18... | collective-permute-start | bytes 4718600 | tf_op jit(solution)/shard_map/ppermute | solution.py:474
  6.7 2.7 %copy-start.23 = (s32[2]{0:T(128)S(1)}, s32[2]{0:T(128)}, u32[]{:S(2)}) copy-start(s32[2]{0:T(128)} %param.9) | copy-start | bytes 28
  6.7 2.7 %copy-start.24 = (s32[2]{0:T(128)S(1)}, s32[2]{0:T(128)}, u32[]{:S(2)}) copy-start(s32[2]{0:T(128)} %param.10) | copy-start | bytes 28
  6.7 2.8 %copy-start.1 = (bf16[1536,512]{1,0:T(8,128)(2,1)S(1)}, bf16[1536,512]{1,0:T(8,128)(2,1)}, u32[]{:S(2)}) copy-start(bf16[1536,512]{1,0:T(8,128)(2,1)} %refs_10_.3) | copy-start | bytes 4718596
  6.7 2.8 %copy-start.2 = (bf16[1536,512]{1,0:T(8,128)(2,1)S(1)}, bf16[1536,512]{1,0:T(8,128)(2,1)}, u32[]{:S(2)}) copy-start(bf16[1536,512]{1,0:T(8,128)(2,1)} %refs_11_.3) | copy-start | bytes 4718596
  7.7 18.1 %collective-permute-start.3 = (bf16[768,512]{1,0:T(8,128)(2,1)}, bf16[768,512]{1,0:T(8,128)(2,1)}, u32[]{:S(2)}, u32[]{:S(2)}) collective-permute-start(bf16[768,512]{1,0:T(8,128)(2,1)} %shard_map.66.refs_1_), channel_id=1, source_target_pairs={{0,16},{2,18},{1,17},{3,19}} | collective-permute-start | bytes 2359304 | tf_op jit(solution)/shard_map/ppermute | solution.py:488
  22.2 23.8 %collective-permute-start.1 = (bf16[1536,512]{1,0:T(8,128)(2,1)}, bf16[1536,512]{1,0:T(8,128)(2,1)}, u32[]{:S(2)}, u32[]{:S(2)}) collective-permute-start(bf16[1536,512]{1,0:T(8,128)(2,1)} %get-tuple-element.26), channel_id=1, source_target_pairs={{0,2},{2,4},{4,6},{6,8},{8,10},{10,12},{12,14},{14,16},{16,18},{18... | collective-permute-start | bytes 4718600 | tf_op jit(solution)/shard_map/ppermute | solution.py:503
  25.8 4.0 %copy-start.4 = (bf16[1536,512]{1,0:T(8,128)(2,1)S(1)}, bf16[1536,512]{1,0:T(8,128)(2,1)}, u32[]{:S(2)}) copy-start(bf16[1536,512]{1,0:T(8,128)(2,1)} %refs_1_.15) | copy-start | bytes 4718596
  28.3 14.1 %collective-permute-start.4 = (bf16[768,512]{1,0:T(8,128)(2,1)}, bf16[768,512]{1,0:T(8,128)(2,1)}, u32[]{:S(2)}, u32[]{:S(2)}) collective-permute-start(bf16[768,512]{1,0:T(8,128)(2,1)} %shard_map.67.refs_4_.refs_1_), channel_id=1, source_target_pairs={{0,8},{16,24},{2,10},{18,26},{1,9},{17,25},{3,11},{19,27}} | collective-permute-start | bytes 2359304 | tf_op jit(solution)/shard_map/ppermute | solution.py:488
  37.1 1.9 %copy-start.17 = (f32[1536,256]{1,0:T(8,128)}, f32[1536,256]{1,0:T(8,128)S(1)}, u32[]{:S(2)}) copy-start(f32[1536,256]{1,0:T(8,128)S(1)} %get-tuple-element.34.refs_3_) | copy-start | bytes 4718596
  37.1 2.1 %copy-start.21 = (f32[1536,128]{1,0:T(8,128)}, f32[1536,128]{1,0:T(8,128)S(1)}, u32[]{:S(2)}) copy-start(f32[1536,128]{1,0:T(8,128)S(1)} %get-tuple-element.35.refs_4_) | copy-start | bytes 2359300
  39.2 43.5 %collective-permute-start.6 = (bf16[1536,512]{1,0:T(8,128)(2,1)}, bf16[1536,512]{1,0:T(8,128)(2,1)}, u32[]{:S(2)}, u32[]{:S(2)}) collective-permute-start(bf16[1536,512]{1,0:T(8,128)(2,1)} %shard_map.70), channel_id=1, source_target_pairs={{0,4},{4,8},{8,12},{12,16},{16,20},{20,24},{24,28},{1,5},{5,9},{9,... | collective-permute-start | bytes 4718600 | tf_op jit(solution)/shard_map/ppermute | solution.py:507
  44.7 38.0 %collective-permute-start.5 = (bf16[768,512]{1,0:T(8,128)(2,1)}, bf16[768,512]{1,0:T(8,128)(2,1)}, u32[]{:S(2)}, u32[]{:S(2)}) collective-permute-start(bf16[768,512]{1,0:T(8,128)(2,1)} %shard_map.69.refs_1_), channel_id=1, source_target_pairs={{0,4},{8,12},{16,20},{24,28},{2,6},{10,14},{18,22},{26,30},{1,5},{... | collective-permute-start | bytes 2359304 | tf_op jit(solution)/shard_map/ppermute | solution.py:488
  46.0 47.7 %collective-permute-start.9 = (bf16[1536,512]{1,0:T(8,128)(2,1)}, bf16[1536,512]{1,0:T(8,128)(2,1)}, u32[]{:S(2)}, u32[]{:S(2)}) collective-permute-start(bf16[1536,512]{1,0:T(8,128)(2,1)} %collective-permute-done.1.refs_6_.refs_13_), channel_id=1, source_target_pairs={{0,2},{4,6},{8,10},{12,14},{16,18},{20,22},{24,26},{28,30},{1,3},{... | collective-permute-start | bytes 4718600 | tf_op jit(solution)/shard_map/ppermute | solution.py:516
  48.5 45.3 %collective-permute-start.8 = (bf16[1536,512]{1,0:T(8,128)(2,1)}, bf16[1536,512]{1,0:T(8,128)(2,1)}, u32[]{:S(2)}, u32[]{:S(2)}) collective-permute-start(bf16[1536,512]{1,0:T(8,128)(2,1)} %collective-permute-done.refs_5_.refs_3_.refs_12_), channel_id=1, source_target_pairs={{0,2},{4,6},{8,10},{12,14},{16,18},{20,22},{24,26},{28,30},{1,3},{... | collective-permute-start | bytes 4718600 | tf_op jit(solution)/shard_map/ppermute | solution.py:515
  56.0 28.6 %copy-start.22 = (f32[1536,128]{1,0:T(8,128)S(1)}, f32[1536,128]{1,0:T(8,128)}, u32[]{:S(2)}) copy-start(f32[1536,128]{1,0:T(8,128)} %copy-done.21) | copy-start | bytes 2359300
  82.8 2.1 %copy-start.14 = (bf16[1536,256]{1,0:T(8,128)(2,1)S(1)}, bf16[1536,256]{1,0:T(8,128)(2,1)}, u32[]{:S(2)}) copy-start(bf16[1536,256]{1,0:T(8,128)(2,1)} %copy-done.13) | copy-start | bytes 2359300
  82.8 2.6 %copy-start.18 = (f32[1536,256]{1,0:T(8,128)S(1)}, f32[1536,256]{1,0:T(8,128)}, u32[]{:S(2)}) copy-start(f32[1536,256]{1,0:T(8,128)} %copy-done.17) | copy-start | bytes 4718596
  84.6 9.2 %collective-permute-start.7 = (bf16[768,512]{1,0:T(8,128)(2,1)S(1)}, bf16[768,512]{1,0:T(8,128)(2,1)S(1)}, u32[]{:S(2)}, u32[]{:S(2)}) collective-permute-start(bf16[768,512]{1,0:T(8,128)(2,1)S(1)} %shard_map.71.refs_5_), channel_id=1, source_target_pairs={{0,2},{2,0},{4,6},{6,4},{8,10},{10,8},{12,14},{14,12},{16,18},{18,... | collective-permute-start | bytes 2359304 | tf_op jit(solution)/shard_map/ppermute | solution.py:513
  93.7 10.4 %copy-start.12 = (bf16[1536,256]{1,0:T(8,128)(2,1)S(1)}, bf16[1536,256]{1,0:T(8,128)(2,1)}, u32[]{:S(2)}) copy-start(bf16[1536,256]{1,0:T(8,128)(2,1)} %copy-done.10) | copy-start | bytes 2359300
  102.6 11.3 %collective-permute-start.11 = (bf16[768,256]{1,0:T(8,128)(2,1)S(1)}, bf16[768,256]{1,0:T(8,128)(2,1)S(1)}, u32[]{:S(2)}, u32[]{:S(2)}) collective-permute-start(bf16[768,256]{1,0:T(8,128)(2,1)S(1)} %get-tuple-element.40), channel_id=1, source_target_pairs={{0,1},{1,0},{2,3},{3,2},{4,5},{5,4},{6,7},{7,6},{8,9},{9,8},{10,11... | collective-permute-start | bytes 1179656 | tf_op jit(solution)/shard_map/ppermute | solution.py:538
  104.2 19.7 %copy-start.7 = (bf16[1024,1536]{1,0:T(8,128)(2,1)S(1)}, bf16[1024,1536]{1,0:T(8,128)(2,1)}, u32[]{:S(2)}) copy-start(bf16[1024,1536]{1,0:T(8,128)(2,1)} %refs_4_.1) | copy-start | bytes 9437188
  113.3 10.6 %collective-permute-start.10 = (bf16[768,256]{1,0:T(8,128)(2,1)S(1)}, bf16[768,256]{1,0:T(8,128)(2,1)S(1)}, u32[]{:S(2)}, u32[]{:S(2)}) collective-permute-start(bf16[768,256]{1,0:T(8,128)(2,1)S(1)} %get-tuple-element.39), channel_id=1, source_target_pairs={{0,1},{1,0},{2,3},{3,2},{4,5},{5,4},{6,7},{7,6},{8,9},{9,8},{10,11... | collective-permute-start | bytes 1179656 | tf_op jit(solution)/shard_map/ppermute | solution.py:538
  (13 other events, 16.7 us)

commit v3 on v2

--- a/solution.py
+++ b/solution.py
@@ -33,23 +33,20 @@
     return slice(slot * FT, (slot + 1) * FT)
 
 
-def add_frame(lanes, kt, values):
-    units = [(n, j) for n in range(len(lanes)) for j in range(FT // BK)]
+def add_frame(lanes, kt, values, block):
+    units = [(n, row) for n in range(len(lanes)) for row in range(0, FT, block)]
 
     def scores(unit):
-        n, j = unit
-        return dot(lanes[n][0], kt[:, j * BK : (j + 1) * BK])
+        n, row = unit
+        return dot(lanes[n][0][row : row + block, :], kt[...])
 
     ahead = scores(units[0])
-    weights = []
-    for at, (n, j) in enumerate(units):
+    for at, (n, row) in enumerate(units):
         s = ahead
         if at + 1 < len(units):
             ahead = scores(units[at + 1])
-        weights.append(jnp.exp2(s * SCALE).astype(jnp.bfloat16))
-        if j == FT // BK - 1:
-            lanes[n][1](dot(jnp.concatenate(weights, axis=1), values[...]))
-            weights = []
+        weights = jnp.exp2(s * SCALE).astype(jnp.bfloat16)
+        lanes[n][1](row, dot(weights, values[...]))
 
 
 def visible(info, slot, frame):
@@ -84,8 +81,9 @@
     kt[HD:, :] = more.astype(jnp.bfloat16)
 
 
-def sums_into(acc_from, acc, sums, rows, column, h, heads):
-    def add(added):
+def sums_into(acc_from, acc, sums, slot, column, h, heads):
+    def add(row, added):
+        rows = slice(slot * FT + row, slot * FT + row + added.shape[0])
         new = added[:, :HD]
         acc[rows, column] = new if acc_from is None else acc_from[rows, column] + new
         old = sums[rows, :]
@@ -110,9 +108,7 @@
 
 
 def own_kernel(group, info, q, k, v, *refs):
-    more, acc, sums, token, kt, values = refs[-6:]
-    if len(refs) > 6:
-        refs[0][...] = v[...]
+    more, acc, sums, token, kt, values = refs
     heads = group[1]
     first = info[0]
     token[...] = jnp.zeros_like(token)
@@ -135,10 +131,10 @@
             lanes = []
             for slot in (0, 1):
                 rows = rows_of(slot)
-                add = sums_into(acc if frame else None, acc, sums, rows, column, h, heads)
+                add = sums_into(acc if frame else None, acc, sums, slot, column, h, heads)
                 queries = jnp.concatenate([q[rows, wide], more[rows, column]], axis=1)
                 lanes.append((queries, add))
-            add_frame(lanes, kt, values)
+            add_frame(lanes, kt, values, 768)
 
         each_head(group, turn)
 
@@ -176,10 +172,10 @@
             lanes = []
             for slot in (0, 1):
                 rows = rows_of(slot)
-                add = sums_into(acc_from, acc, sums, rows, column, h, heads)
+                add = sums_into(acc_from, acc, sums, slot, column, h, heads)
                 queries = jnp.concatenate([q[rows, wide], more[rows, column]], axis=1)
                 lanes.append((queries, add))
-            add_frame(lanes, kt, values)
+            add_frame(lanes, kt, values, 384)
 
         each_head(group, turn)
 
@@ -188,8 +184,8 @@
     group, info, q, more, acc_in, sums_in,
     sink_a, sink_b, far, relay_k, relay_v, key_any, value_any, near_k, near_v, *refs,
 ):
-    outs = refs[:-8]
-    kt, values, k_buf, v_buf, acc, shift, too_large, sem = refs[-8:]
+    outs = refs[:-9]
+    kt, values, k_buf, v_buf, results, acc, shift, too_large, sem = refs[-9:]
     first = info[0]
     core = info[6]
     far_seen = visible(info, 0, first - 3)
@@ -241,11 +237,10 @@
                 outs[1][:, column] = attended
 
     def turn(h, column, wide):
-        results = {}
-
-        def keep(slot):
-            def add(added):
-                results[slot] = results[slot] + added if slot in results else added
+        def into(ref, slot, old=None):
+            def add(row, added):
+                rows = slice(slot * FT + row, slot * FT + row + added.shape[0])
+                ref[rows, :] = added if old is None else old[rows, :] + added
 
             return add
 
@@ -255,14 +250,14 @@
         ]
         load_frame(kt, values, k_buf.at[0], v_buf.at[0], column)
         set_more_rows(kt, [True, True])
-        add_frame([(queries[slot], keep(slot)) for slot in (1, 0)], kt, values)
+        add_frame([(queries[slot], into(results, slot)) for slot in (1, 0)], kt, values, 256)
         load_frame(kt, values, k_buf.at[1], v_buf.at[1], column)
         set_more_rows(kt, [far_seen, False])
-        add_frame([(queries[0], keep(0))], kt, values)
+        add_frame([(queries[0], into(results, 0, results))], kt, values, 256)
         for slot in (0, 1):
             rows = rows_of(slot)
-            total = spread(sums_in[rows, :], h, heads) + results[slot][:, HD:]
-            write(slot, h, acc_in[rows, column] + results[slot][:, :HD], total)
+            total = spread(sums_in[rows, :], h, heads) + results[rows, HD:]
+            write(slot, h, acc_in[rows, column] + results[rows, :HD], total)
             too_large[h, slot] = jnp.max(jnp.where(total < LIMIT, 0.0, 1.0))
 
     each_head(group, turn)
@@ -380,16 +375,27 @@
 
 
 def pick(flag, taken, kept, tokens=()):
-    def kernel(flag, taken, kept, out):
-        @pl.when(flag[0] == 1)
-        def _():
-            out[...] = taken[:FT, :]
-
-        @pl.when(flag[0] == 0)
-        def _():
-            out[...] = kept[:FT, :]
-
-    return small(kernel, flag, [taken, kept], tokens, FT)
+    width = kept.shape[1]
+
+    def kernel(flag, taken, kept, *refs):
+        out, sem = refs[-2:]
+        for value, source in ((1, taken), (0, kept)):
+
+            @pl.when(flag[0] == value)
+            def _():
+                copy = pltpu.make_async_copy(source.at[pl.ds(0, FT)], out, sem)
+                copy.start()
+                copy.wait()
+
+    return pl.pallas_call(
+        kernel,
+        in_specs=[SMEM_SPEC] + [ANY_SPEC] * (2 + len(tokens)),
+        out_specs=VMEM_SPEC,
+        out_shape=jax.ShapeDtypeStruct((FT, width), jnp.bfloat16),
+        scratch_shapes=[pltpu.SemaphoreType.DMA],
+        compiler_params=PARAMS,
+        cost_estimate=COST,
+    )(jnp.reshape(flag, (1,)).astype(jnp.int32), taken, kept, *tokens)
 
 
 def last_frames(keys, values, tokens=()):
@@ -461,8 +467,7 @@
         ]
     )
     groups = [(0, heads // 2), (heads // 2, heads // 2)] if heads % 2 == 0 else [(0, heads)]
-    rows, width = query_states.shape
-    q_like = jax.ShapeDtypeStruct((rows, width), jnp.bfloat16)
+    rows = query_states.shape[0]
     group_width = groups[0][1] * HD
     more_like = jax.ShapeDtypeStruct((rows, group_width), jnp.bfloat16)
     acc_like = jax.ShapeDtypeStruct((rows, group_width), jnp.float32)
@@ -472,6 +477,7 @@
 
     onward = [(i, i + 1) for i in range(size - 1)]
     near_k = lax.ppermute(key_states, axis, onward)
+    near_v = lax.ppermute(value_states, axis, onward)
     moved = lax.ppermute(value_states, axis, [(0, 1)])
     held = pick(core, moved, key_states)
 
@@ -491,17 +497,16 @@
         for _, target in pairs:
             takes = takes | (me == target)
         if step < len(groups):
-            *passed, more, acc, sums, token = stage(
+            more, acc, sums, token = stage(
                 functools.partial(own_kernel, groups[step]),
                 [info, query_states, key_states, value_states], 0,
-                [q_like] * (step == 0) + [more_like, acc_like, sums_like, TOKEN], [],
+                [more_like, acc_like, sums_like, TOKEN], [],
                 tokens=[held] * (step > 0),
             )
             states.append((more, acc, sums))
             tokens.append(token)
-            if step == 0:
-                near_v = lax.ppermute(passed[0], axis, onward)
-                tokens.append(near_k)
+            if step == 1:
+                tokens += [near_k, near_v]
             if step == len(groups) - 1:
                 own_last = last_frames(key_states, value_states, [token])
                 far = lax.ppermute(own_last, axis, [(i, i + 2) for i in range(0, size - 2, 2)])
@@ -527,6 +532,7 @@
              key_states, value_states, near_k, near_v], 9,
             [part] * (2 if paired else 1),
             frame_buffers + [
+                pltpu.VMEM((rows, 2 * HD), jnp.float32),
                 pltpu.VMEM((FT, 2 * HD), jnp.float32),
                 pltpu.VMEM((FT, HD), jnp.float32),
                 pltpu.SMEM((group[1], 2), jnp.float32),

time: 130 us -> 128 us (0.985)
  local copies, waits for them, and re-layouts: 14.9 us -> 12 us
  waiting for transfers between devices: 29 us -> 30.3 us
    pallas_call x0 -> x4, Pallas kernels: none -> 7.53 us  [pick(): pl.pallas_call(kernel, in_specs=[SMEM_SPEC] + [ANY_SPEC] * (2 + len(token...]
    pallas_call x5 -> x1, Pallas kernels: 8.96 us -> 2.93 us  [small(): pl.pallas_call(run, in_specs=[SMEM_SPEC] + [VMEM_SPEC] * n + [ANY_SPEC] *...]
    unnamed x50 -> x40, local copies, waits for them, and re-layouts: 14.8 us -> 12 us
    ppermute x1, waiting for transfers between devices: 0.01 us -> 2.38 us  [local(): near_v = lax.ppermute(value_states, axis, onward)]
    pallas_call x6, Pallas kernels: 49.7 us -> 47.8 us  [stage(): pl.pallas_call(run, in_specs=[SMEM_SPEC] + [VMEM_SPEC] * (n - in_any - 1)...]
    ppermute x3, waiting for transfers between devices: 19 us -> 17.4 us  [local(): moved = lax.ppermute(held, axis, pairs)]
  transfers between devices with their start and end apart: 12 -> 12, of which waited for: 2 -> 4; matrix products, arithmetic and copies ran while one was open for 0% -> 0% of each run, Pallas kernels for 39% -> 38%
where the time goes in v3:
time: 128 us; the launch traced here: 127 us
  Pallas kernels  63.4 us (50%)
  waiting for transfers between devices  30.3 us (24%)
  starting transfers between devices  21.3 us (17%)
  local copies, waits for them, and re-layouts  12 us (9%)
    pallas_call x6, Pallas kernels, stage(): pl.pallas_call(run, in_specs=[SMEM_SPEC] + [VMEM_SPEC] * (n - in_any - 1)...  47.8 us
    ppermute x3, waiting for transfers between devices, local(): moved = lax.ppermute(held, axis, pairs)  17.4 us
    unnamed x40, local copies, waits for them, and re-layouts  12 us
    ppermute x2, waiting for transfers between devices, local(): theirs.append(lax.ppermute(results[1], 'head', [(0, 1), (1, 0)]))  10.5 us
    pallas_call x4, Pallas kernels, pick(): pl.pallas_call(kernel, in_specs=[SMEM_SPEC] + [ANY_SPEC] * (2 + len(token...  7.53 us
    pallas_call x1, Pallas kernels, project(): pl.pallas_call(kernel, grid=(turns,), in_specs=[SMEM_SPEC] + [VMEM_SPEC]...  5.15 us
    ppermute x3, starting transfers between devices, local(): moved = lax.ppermute(held, axis, pairs)  4.45 us
    ppermute x1, starting transfers between devices, local(): near_v = lax.ppermute(value_states, axis, onward)  3.56 us
  transfers between devices with their start and end apart: 12, of which 4 were waited for; matrix products, arithmetic and copies ran while one was open for 0% of the time, Pallas kernels for 38%

profile of v3, /device:TPU:18, one launch (start us, length us, event | category | flops | bytes accessed | tf_op | source)
XLA Modules:
  0.0 127.4 jit_solution(13985348771916063131)
XLA Ops:
  1.9 1.4 %copy-done.4 = bf16[1536,512]{1,0:T(8,128)(2,1)S(1)} copy-done((bf16[1536,512]{1,0:T(8,128)(2,1)S(1)}, bf16[1536,512]{1,0:T(8,128)(2,1)}, u32[]{:S(2)}) %copy-start.4) | copy-done | bytes 1572888
  3.3 2.2 %shard_map.66.kept = bf16[768,512]{1,0:T(8,128)(2,1)} custom-call(s32[1]{0:T(128)} %bitcast.2.flag, bf16[1536,512]{1,0:T(8,128)(2,1)S(1)} %copy-done.4, bf16[1536,512]{1,0:T(8,128)(2,1)} %refs_10_.3), custom_call_target="tpu_custom_call" | custom-call | flops 1000 | bytes 1000 | tf_op jit(solution)/shard_map/pallas_call | solution.py:390
  5.5 1.6 %collective-permute-start.3 = (bf16[768,512]{1,0:T(8,128)(2,1)}, bf16[768,512]{1,0:T(8,128)(2,1)}, u32[]{:S(2)}, u32[]{:S(2)}) collective-permute-start(bf16[768,512]{1,0:T(8,128)(2,1)} %shard_map.66.kept), channel_id=1, source_target_pairs={{0,16},{2,18},{1,17},{3,19}} | collective-permute-start | bytes 2359304 | tf_op jit(solution)/shard_map/ppermute | solution.py:494
  7.1 1.9 %collective-permute-start = (bf16[1536,512]{1,0:T(8,128)(2,1)}, bf16[1536,512]{1,0:T(8,128)(2,1)}, u32[]{:S(2)}, u32[]{:S(2)}) collective-permute-start(bf16[1536,512]{1,0:T(8,128)(2,1)} %refs_10_.3), channel_id=1, source_target_pairs={{0,2},{2,4},{4,6},{6,8},{8,10},{10,12},{12,14},{14,16},{16,18},{18... | collective-permute-start | bytes 4718600 | tf_op jit(solution)/shard_map/ppermute | solution.py:479
  9.0 3.6 %collective-permute-start.1 = (bf16[1536,512]{1,0:T(8,128)(2,1)S(1)}, bf16[1536,512]{1,0:T(8,128)(2,1)}, u32[]{:S(2)}, u32[]{:S(2)}) collective-permute-start(bf16[1536,512]{1,0:T(8,128)(2,1)S(1)} %copy-done), channel_id=1, source_target_pairs={{0,2},{2,4},{4,6},{6,8},{8,10},{10,12},{12,14},{14,16},{16,18},{18... | collective-permute-start | bytes 4718600 | tf_op jit(solution)/shard_map/ppermute | solution.py:480
  12.7 8.1 %shard_map.64 = (bf16[1536,256]{1,0:T(8,128)(2,1)S(1)}, f32[1536,256]{1,0:T(8,128)S(1)}, f32[1536,128]{1,0:T(8,128)S(1)}, f32[8,128]{1,0:T(8,128)S(1)}) custom-call(s32[7]{0:T(128)S(1)} %concatenate.3.refs_0_.info, bf16[1536,512]{1,0:T(8,128)(2,1)S(1)} %copy-done.1, bf16[1536,512]{1,0:T(8,128)(2,1)} %refs_10_.3, bf16[1536,512]{1,0:T(8,128)(2,1)S(1)} %copy-done), custom_call_target="tpu_custom_call" | custom-call | flops 1000 | bytes 1000 | tf_op jit(solution)/shard_map/pallas_call | solution.py:346
  23.7 2.0 %shard_map.67.refs_4_.kept = bf16[768,512]{1,0:T(8,128)(2,1)} custom-call(s32[1]{0:T(128)} %bitcast.5.flag, bf16[768,512]{1,0:T(8,128)(2,1)} %collective-permute-done.3.taken, bf16[768,512]{1,0:T(8,128)(2,1)} %shard_map.66.kept, f32[8,128]{1,0:T(8,128)S(1)} %get-tuple-element.27.refs_0_), custom_call_target="tpu_custom_call" | custom-call | flops 1000 | bytes 1000 | tf_op jit(solution)/shard_map/pallas_call | solution.py:390
  25.7 1.6 %collective-permute-start.4 = (bf16[768,512]{1,0:T(8,128)(2,1)}, bf16[768,512]{1,0:T(8,128)(2,1)}, u32[]{:S(2)}, u32[]{:S(2)}) collective-permute-start(bf16[768,512]{1,0:T(8,128)(2,1)} %shard_map.67.refs_4_.kept), channel_id=1, source_target_pairs={{0,8},{16,24},{2,10},{18,26},{1,9},{17,25},{3,11},{19,27}} | collective-permute-start | bytes 2359304 | tf_op jit(solution)/shard_map/ppermute | solution.py:494
  27.3 8.1 %shard_map.68 = (bf16[1536,256]{1,0:T(8,128)(2,1)S(1)}, f32[1536,256]{1,0:T(8,128)S(1)}, f32[1536,128]{1,0:T(8,128)S(1)}, f32[8,128]{1,0:T(8,128)S(1)}) custom-call(s32[7]{0:T(128)S(1)} %concatenate.3.refs_0_.info, bf16[1536,512]{1,0:T(8,128)(2,1)S(1)} %copy-done.1, bf16[1536,512]{1,0:T(8,128)(2,1)} %refs_10_.3, bf16[1536,512]{1,0:T(8,128)(2,1)S(1)} %copy-done, ...), custom_call_target="tpu_custom_call" | custom-call | flops 1000 | bytes 1000 | tf_op jit(solution)/shard_map/pallas_call | solution.py:346
  37.6 2.9 %shard_map.70 = bf16[1536,512]{1,0:T(8,128)(2,1)} custom-call(s32[1]{0:T(128)} %constant.48.clone.1.scalars, bf16[1536,512]{1,0:T(8,128)(2,1)} %refs_10_.3, bf16[1536,512]{1,0:T(8,128)(2,1)S(1)} %copy-done, f32[8,128]{1,0:T(8,128)S(1)} %get-tuple-element.28.refs_0_.refs_2_), custom_call_target="tpu_custom_call" | custom-call | flops 1000 | bytes 1000 | tf_op jit(solution)/shard_map/pallas_call | solution.py:367
  40.5 3.1 %collective-permute-start.6 = (bf16[1536,512]{1,0:T(8,128)(2,1)}, bf16[1536,512]{1,0:T(8,128)(2,1)}, u32[]{:S(2)}, u32[]{:S(2)}) collective-permute-start(bf16[1536,512]{1,0:T(8,128)(2,1)} %shard_map.70), channel_id=1, source_target_pairs={{0,4},{4,8},{8,12},{12,16},{16,20},{20,24},{24,28},{1,5},{5,9},{9,... | collective-permute-start | bytes 4718600 | tf_op jit(solution)/shard_map/ppermute | solution.py:512
  43.6 2.4 %collective-permute-done.1.refs_6_.refs_2_.refs_13_ = bf16[1536,512]{1,0:T(8,128)(2,1)} collective-permute-done((bf16[1536,512]{1,0:T(8,128)(2,1)S(1)}, bf16[1536,512]{1,0:T(8,128)(2,1)}, u32[]{:S(2)}, u32[]{:S(2)}) %collective-permute-start.1) | collective-permute-done | bytes 1572896 | tf_op jit(solution)/shard_map/ppermute | solution.py:480
  46.0 2.0 %shard_map.69.kept = bf16[768,512]{1,0:T(8,128)(2,1)} custom-call(s32[1]{0:T(128)} %bitcast.4.flag, bf16[768,512]{1,0:T(8,128)(2,1)} %collective-permute-done.4.taken, bf16[768,512]{1,0:T(8,128)(2,1)} %shard_map.67.refs_4_.kept, f32[8,128]{1,0:T(8,128)S(1)} %get-tuple-element.28.refs_0_.refs_2_, ...), custom_call_target="tpu_custom_call" | custom-call | flops 1000 | bytes 1000 | tf_op jit(solution)/shard_map/pallas_call | solution.py:390
  49.3 2.5 %collective-permute-start.8 = (bf16[1536,512]{1,0:T(8,128)(2,1)}, bf16[1536,512]{1,0:T(8,128)(2,1)}, u32[]{:S(2)}, u32[]{:S(2)}) collective-permute-start(bf16[1536,512]{1,0:T(8,128)(2,1)} %collective-permute-done.refs_5_.refs_1_.refs_12_), channel_id=1, source_target_pairs={{0,2},{4,6},{8,10},{12,14},{16,18},{20,22},{24,26},{28,30},{1,3},{... | collective-permute-start | bytes 4718600 | tf_op jit(solution)/shard_map/ppermute | solution.py:520
  51.8 2.5 %collective-permute-start.9 = (bf16[1536,512]{1,0:T(8,128)(2,1)}, bf16[1536,512]{1,0:T(8,128)(2,1)}, u32[]{:S(2)}, u32[]{:S(2)}) collective-permute-start(bf16[1536,512]{1,0:T(8,128)(2,1)} %collective-permute-done.1.refs_6_.refs_2_.refs_13_), channel_id=1, source_target_pairs={{0,2},{4,6},{8,10},{12,14},{16,18},{20,22},{24,26},{28,30},{1,3},{... | collective-permute-start | bytes 4718600 | tf_op jit(solution)/shard_map/ppermute | solution.py:521
  55.4 1.4 %copy-done.11 = f32[1536,256]{1,0:T(8,128)S(1)} copy-done((f32[1536,256]{1,0:T(8,128)S(1)}, f32[1536,256]{1,0:T(8,128)}, u32[]{:S(2)}) %copy-start.11) | copy-done | bytes 1572888
  58.0 7.8 %shard_map.65 = (f32[1536,256]{1,0:T(8,128)S(1)}, f32[1536,128]{1,0:T(8,128)S(1)}, f32[8,128]{1,0:T(8,128)S(1)}) custom-call(s32[7]{0:T(128)S(1)} %concatenate.3.refs_0_.info, bf16[1536,512]{1,0:T(8,128)(2,1)S(1)} %copy-done.1, bf16[1536,256]{1,0:T(8,128)(2,1)S(1)} %copy-done.6, f32[1536,256]{1,0:T(8,128)S(1)} %copy-done.11, f32[1536,128]{1,0:T(8,128)S(1)} %copy-done.15, ...), custom_call_target="tpu_custom_call" | custom-call | flops 8000000000 | bytes 1000 | tf_op jit(solution)/shard_map/pallas_call | solution.py:346
  65.8 17.4 %collective-permute-done.5.taken = bf16[768,512]{1,0:T(8,128)(2,1)} collective-permute-done((bf16[768,512]{1,0:T(8,128)(2,1)}, bf16[768,512]{1,0:T(8,128)(2,1)}, u32[]{:S(2)}, u32[]{:S(2)}) %collective-permute-start.5) | collective-permute-done | bytes 786464 | tf_op jit(solution)/shard_map/ppermute | solution.py:494
  85.3 7.8 %shard_map.73 = (f32[1536,256]{1,0:T(8,128)S(1)}, f32[1536,128]{1,0:T(8,128)S(1)}, f32[8,128]{1,0:T(8,128)}) custom-call(s32[7]{0:T(128)S(1)} %concatenate.3.refs_0_.info, bf16[1536,512]{1,0:T(8,128)(2,1)S(1)} %copy-done.1, bf16[1536,256]{1,0:T(8,128)(2,1)S(1)} %copy-done.9, f32[1536,256]{1,0:T(8,128)S(1)} %copy-done.13, f32[1536,128]{1,0:T(8,128)S(1)} %copy-done.17, ...), custom_call_target="tpu_custom_call" | custom-call | flops 8000000000 | bytes 1000 | tf_op jit(solution)/shard_map/pallas_call | solution.py:346
  93.1 7.9 %shard_map.74 = (bf16[768,256]{1,0:T(8,128)(2,1)S(1)}, bf16[768,256]{1,0:T(8,128)(2,1)S(1)}) custom-call(s32[7]{0:T(128)S(1)} %concatenate.3.refs_0_.info, bf16[1536,512]{1,0:T(8,128)(2,1)S(1)} %copy-done.1, bf16[1536,256]{1,0:T(8,128)(2,1)S(1)} %copy-done.9, f32[1536,256]{1,0:T(8,128)S(1)} %get-tuple-element.34.refs_3_, ...), custom_call_target="tpu_custom_call" | custom-call | flops 1000 | bytes 1000 | tf_op jit(solution)/shard_map/pallas_call | solution.py:346
  101.1 2.4 %collective-permute-start.11 = (bf16[768,256]{1,0:T(8,128)(2,1)S(1)}, bf16[768,256]{1,0:T(8,128)(2,1)S(1)}, u32[]{:S(2)}, u32[]{:S(2)}) collective-permute-start(bf16[768,256]{1,0:T(8,128)(2,1)S(1)} %get-tuple-element.38), channel_id=1, source_target_pairs={{0,1},{1,0},{2,3},{3,2},{4,5},{5,4},{6,7},{7,6},{8,9},{9,8},{10,11... | collective-permute-start | bytes 1179656 | tf_op jit(solution)/shard_map/ppermute | solution.py:544
  103.5 8.1 %shard_map.72 = (bf16[768,256]{1,0:T(8,128)(2,1)S(1)}, bf16[768,256]{1,0:T(8,128)(2,1)S(1)}) custom-call(s32[7]{0:T(128)S(1)} %concatenate.3.refs_0_.info, bf16[1536,512]{1,0:T(8,128)(2,1)S(1)} %copy-done.1, bf16[1536,256]{1,0:T(8,128)(2,1)S(1)} %copy-done.7, f32[1536,256]{1,0:T(8,128)S(1)} %get-tuple-element.25.refs_3_, ...), custom_call_target="tpu_custom_call" | custom-call | flops 1000 | bytes 1000 | tf_op jit(solution)/shard_map/pallas_call | solution.py:346
  112.6 9.7 %collective-permute-done.10.refs_2_ = bf16[768,256]{1,0:T(8,128)(2,1)S(1)} collective-permute-done((bf16[768,256]{1,0:T(8,128)(2,1)S(1)}, bf16[768,256]{1,0:T(8,128)(2,1)S(1)}, u32[]{:S(2)}, u32[]{:S(2)}) %collective-permute-start.10) | collective-permute-done | bytes 393248 | tf_op jit(solution)/shard_map/ppermute | solution.py:544
  122.3 5.1 %shard_map.75 = bf16[768,1536]{1,0:T(8,128)(2,1)} custom-call(s32[7]{0:T(128)S(1)} %concatenate.3.refs_0_.info, bf16[768,256]{1,0:T(8,128)(2,1)S(1)} %get-tuple-element.30.refs_0_, bf16[768,256]{1,0:T(8,128)(2,1)S(1)} %get-tuple-element.36.refs_1_, bf16[768,256]{1,0:T(8,128)(2,1)S(1)} %collective-permute-done.10.refs_2_, ...), custom_call_target="tpu_custom_call" | custom-call | flops 1000 | bytes 1000 | tf_op jit(solution)/shard_map/pallas_call | solution.py:443
  (53 shorter events, 13.6 us)
Async XLA Ops:
  0.0 0.8 collective-permute-start.2
  1.9 1.4 %copy-start.4 = (bf16[1536,512]{1,0:T(8,128)(2,1)S(1)}, bf16[1536,512]{1,0:T(8,128)(2,1)}, u32[]{:S(2)}) copy-start(bf16[1536,512]{1,0:T(8,128)(2,1)} %copy-done.3) | copy-start | bytes 4718596
  3.3 5.7 %copy-start = (bf16[1536,512]{1,0:T(8,128)(2,1)S(1)}, bf16[1536,512]{1,0:T(8,128)(2,1)}, u32[]{:S(2)}) copy-start(bf16[1536,512]{1,0:T(8,128)(2,1)} %refs_11_.3) | copy-start | bytes 4718596
  3.3 9.3 %copy-start.18 = (s32[2]{0:T(128)S(1)}, s32[2]{0:T(128)}, u32[]{:S(2)}) copy-start(s32[2]{0:T(128)} %param.9) | copy-start | bytes 28
  3.3 9.3 %copy-start.19 = (s32[2]{0:T(128)S(1)}, s32[2]{0:T(128)}, u32[]{:S(2)}) copy-start(s32[2]{0:T(128)} %param.10) | copy-start | bytes 28
  3.3 9.4 %copy-start.1 = (bf16[1536,512]{1,0:T(8,128)(2,1)S(1)}, bf16[1536,512]{1,0:T(8,128)(2,1)}, u32[]{:S(2)}) copy-start(bf16[1536,512]{1,0:T(8,128)(2,1)} %refs_1_.13) | copy-start | bytes 4718596
  5.5 18.2 %collective-permute-start.3 = (bf16[768,512]{1,0:T(8,128)(2,1)}, bf16[768,512]{1,0:T(8,128)(2,1)}, u32[]{:S(2)}, u32[]{:S(2)}) collective-permute-start(bf16[768,512]{1,0:T(8,128)(2,1)} %shard_map.66.kept), channel_id=1, source_target_pairs={{0,16},{2,18},{1,17},{3,19}} | collective-permute-start | bytes 2359304 | tf_op jit(solution)/shard_map/ppermute | solution.py:494
  7.1 36.5 %collective-permute-start = (bf16[1536,512]{1,0:T(8,128)(2,1)}, bf16[1536,512]{1,0:T(8,128)(2,1)}, u32[]{:S(2)}, u32[]{:S(2)}) collective-permute-start(bf16[1536,512]{1,0:T(8,128)(2,1)} %refs_10_.3), channel_id=1, source_target_pairs={{0,2},{2,4},{4,6},{6,8},{8,10},{10,12},{12,14},{14,16},{16,18},{18... | collective-permute-start | bytes 4718600 | tf_op jit(solution)/shard_map/ppermute | solution.py:479
  9.0 37.0 %collective-permute-start.1 = (bf16[1536,512]{1,0:T(8,128)(2,1)S(1)}, bf16[1536,512]{1,0:T(8,128)(2,1)}, u32[]{:S(2)}, u32[]{:S(2)}) collective-permute-start(bf16[1536,512]{1,0:T(8,128)(2,1)S(1)} %copy-done), channel_id=1, source_target_pairs={{0,2},{2,4},{4,6},{6,8},{8,10},{10,12},{12,14},{14,16},{16,18},{18... | collective-permute-start | bytes 4718600 | tf_op jit(solution)/shard_map/ppermute | solution.py:480
  25.7 20.2 %collective-permute-start.4 = (bf16[768,512]{1,0:T(8,128)(2,1)}, bf16[768,512]{1,0:T(8,128)(2,1)}, u32[]{:S(2)}, u32[]{:S(2)}) collective-permute-start(bf16[768,512]{1,0:T(8,128)(2,1)} %shard_map.67.refs_4_.kept), channel_id=1, source_target_pairs={{0,8},{16,24},{2,10},{18,26},{1,9},{17,25},{3,11},{19,27}} | collective-permute-start | bytes 2359304 | tf_op jit(solution)/shard_map/ppermute | solution.py:494
  37.6 2.9 %copy-start.8 = (bf16[1536,256]{1,0:T(8,128)(2,1)}, bf16[1536,256]{1,0:T(8,128)(2,1)S(1)}, u32[]{:S(2)}) copy-start(bf16[1536,256]{1,0:T(8,128)(2,1)S(1)} %get-tuple-element.31.refs_2_) | copy-start | bytes 2359300
  40.5 42.7 %collective-permute-start.6 = (bf16[1536,512]{1,0:T(8,128)(2,1)}, bf16[1536,512]{1,0:T(8,128)(2,1)}, u32[]{:S(2)}, u32[]{:S(2)}) collective-permute-start(bf16[1536,512]{1,0:T(8,128)(2,1)} %shard_map.70), channel_id=1, source_target_pairs={{0,4},{4,8},{8,12},{12,16},{16,20},{20,24},{24,28},{1,5},{5,9},{9,... | collective-permute-start | bytes 4718600 | tf_op jit(solution)/shard_map/ppermute | solution.py:512
  48.0 35.2 %collective-permute-start.5 = (bf16[768,512]{1,0:T(8,128)(2,1)}, bf16[768,512]{1,0:T(8,128)(2,1)}, u32[]{:S(2)}, u32[]{:S(2)}) collective-permute-start(bf16[768,512]{1,0:T(8,128)(2,1)} %shard_map.69.kept), channel_id=1, source_target_pairs={{0,4},{8,12},{16,20},{24,28},{2,6},{10,14},{18,22},{26,30},{1,5},{... | collective-permute-start | bytes 2359304 | tf_op jit(solution)/shard_map/ppermute | solution.py:494
  49.3 43.8 %collective-permute-start.8 = (bf16[1536,512]{1,0:T(8,128)(2,1)}, bf16[1536,512]{1,0:T(8,128)(2,1)}, u32[]{:S(2)}, u32[]{:S(2)}) collective-permute-start(bf16[1536,512]{1,0:T(8,128)(2,1)} %collective-permute-done.refs_5_.refs_1_.refs_12_), channel_id=1, source_target_pairs={{0,2},{4,6},{8,10},{12,14},{16,18},{20,22},{24,26},{28,30},{1,3},{... | collective-permute-start | bytes 4718600 | tf_op jit(solution)/shard_map/ppermute | solution.py:520
  51.8 41.3 %collective-permute-start.9 = (bf16[1536,512]{1,0:T(8,128)(2,1)}, bf16[1536,512]{1,0:T(8,128)(2,1)}, u32[]{:S(2)}, u32[]{:S(2)}) collective-permute-start(bf16[1536,512]{1,0:T(8,128)(2,1)} %collective-permute-done.1.refs_6_.refs_2_.refs_13_), channel_id=1, source_target_pairs={{0,2},{4,6},{8,10},{12,14},{16,18},{20,22},{24,26},{28,30},{1,3},{... | collective-permute-start | bytes 4718600 | tf_op jit(solution)/shard_map/ppermute | solution.py:521
  55.4 1.4 %copy-start.11 = (f32[1536,256]{1,0:T(8,128)S(1)}, f32[1536,256]{1,0:T(8,128)}, u32[]{:S(2)}) copy-start(f32[1536,256]{1,0:T(8,128)} %copy-done.10) | copy-start | bytes 4718596
  83.2 1.4 %copy-start.9 = (bf16[1536,256]{1,0:T(8,128)(2,1)S(1)}, bf16[1536,256]{1,0:T(8,128)(2,1)}, u32[]{:S(2)}) copy-start(bf16[1536,256]{1,0:T(8,128)(2,1)} %copy-done.8) | copy-start | bytes 2359300
  83.2 1.9 %copy-start.13 = (f32[1536,256]{1,0:T(8,128)S(1)}, f32[1536,256]{1,0:T(8,128)}, u32[]{:S(2)}) copy-start(f32[1536,256]{1,0:T(8,128)} %copy-done.12) | copy-start | bytes 4718596
  83.2 2.1 %copy-start.17 = (f32[1536,128]{1,0:T(8,128)S(1)}, f32[1536,128]{1,0:T(8,128)}, u32[]{:S(2)}) copy-start(f32[1536,128]{1,0:T(8,128)} %copy-done.16) | copy-start | bytes 2359300
  84.5 8.6 %collective-permute-start.7 = (bf16[768,512]{1,0:T(8,128)(2,1)S(1)}, bf16[768,512]{1,0:T(8,128)(2,1)S(1)}, u32[]{:S(2)}, u32[]{:S(2)}) collective-permute-start(bf16[768,512]{1,0:T(8,128)(2,1)S(1)} %shard_map.71.refs_5_), channel_id=1, source_target_pairs={{0,2},{2,0},{4,6},{6,4},{8,10},{10,8},{12,14},{14,12},{16,18},{18,... | collective-permute-start | bytes 2359304 | tf_op jit(solution)/shard_map/ppermute | solution.py:518
  93.1 10.4 %copy-start.7 = (bf16[1536,256]{1,0:T(8,128)(2,1)S(1)}, bf16[1536,256]{1,0:T(8,128)(2,1)}, u32[]{:S(2)}) copy-start(bf16[1536,256]{1,0:T(8,128)(2,1)} %copy-done.5) | copy-start | bytes 2359300
  101.1 11.5 %collective-permute-start.11 = (bf16[768,256]{1,0:T(8,128)(2,1)S(1)}, bf16[768,256]{1,0:T(8,128)(2,1)S(1)}, u32[]{:S(2)}, u32[]{:S(2)}) collective-permute-start(bf16[768,256]{1,0:T(8,128)(2,1)S(1)} %get-tuple-element.38), channel_id=1, source_target_pairs={{0,1},{1,0},{2,3},{3,2},{4,5},{5,4},{6,7},{7,6},{8,9},{9,8},{10,11... | collective-permute-start | bytes 1179656 | tf_op jit(solution)/shard_map/ppermute | solution.py:544
  103.5 18.8 %copy-start.2 = (bf16[1024,1536]{1,0:T(8,128)(2,1)S(1)}, bf16[1024,1536]{1,0:T(8,128)(2,1)}, u32[]{:S(2)}) copy-start(bf16[1024,1536]{1,0:T(8,128)(2,1)} %refs_4_.1) | copy-start | bytes 9437188
  111.6 10.6 %collective-permute-start.10 = (bf16[768,256]{1,0:T(8,128)(2,1)S(1)}, bf16[768,256]{1,0:T(8,128)(2,1)S(1)}, u32[]{:S(2)}, u32[]{:S(2)}) collective-permute-start(bf16[768,256]{1,0:T(8,128)(2,1)S(1)} %get-tuple-element.37), channel_id=1, source_target_pairs={{0,1},{1,0},{2,3},{3,2},{4,5},{5,4},{6,7},{7,6},{8,9},{9,8},{10,11... | collective-permute-start | bytes 1179656 | tf_op jit(solution)/shard_map/ppermute | solution.py:544
  (8 other events, 8.5 us)

commit v4 on v3

--- a/solution.py
+++ b/solution.py
@@ -134,7 +134,7 @@
                 add = sums_into(acc if frame else None, acc, sums, slot, column, h, heads)
                 queries = jnp.concatenate([q[rows, wide], more[rows, column]], axis=1)
                 lanes.append((queries, add))
-            add_frame(lanes, kt, values, 768)
+            add_frame(lanes, kt, values, 256)
 
         each_head(group, turn)
 
@@ -175,7 +175,7 @@
                 add = sums_into(acc_from, acc, sums, slot, column, h, heads)
                 queries = jnp.concatenate([q[rows, wide], more[rows, column]], axis=1)
                 lanes.append((queries, add))
-            add_frame(lanes, kt, values, 384)
+            add_frame(lanes, kt, values, 256)
 
         each_head(group, turn)
 
@@ -193,6 +193,8 @@
     group_columns = pl.ds(offset * HD, heads * HD)
     values[:, HD:] = jnp.ones((FT, HD), jnp.bfloat16)
 
+    own_columns = pl.ds(0, heads * HD)
+
     def copies(frame, k, k_row, v, v_row, columns):
         return [
             pltpu.make_async_copy(
@@ -203,11 +205,11 @@
 
     arriving = {
         0: [
-            (0, sink_a, 0, sink_b, 0, group_columns),
-            (1, far, 0, far, FT, group_columns),
+            (0, sink_a, 0, sink_b, 0, own_columns),
+            (1, far, 0, far, FT, own_columns),
         ],
         1: [
-            (0, sink_b, 0, sink_a, 0, group_columns),
+            (0, sink_b, 0, sink_a, 0, own_columns),
             (1, relay_k, FT, relay_v, FT, group_columns),
         ],
     }
@@ -262,25 +264,28 @@
 
     each_head(group, turn)
 
-    def again(slot, h, wide):
+    def again(slot, h, column, wide):
         here, there = core == 0, core == 1
-        sources = [(here, sink_a, 0, sink_b, 0), (there, sink_b, 0, sink_a, 0)]
+        sources = [
+            (here, sink_a, 0, sink_b, 0, column), (there, sink_b, 0, sink_a, 0, column)
+        ]
         if slot == 0:
             sources += [
-                (far_seen & here, far, 0, far, FT), (far_seen & there, relay_k, FT, relay_v, FT)
+                (far_seen & here, far, 0, far, FT, column),
+                (far_seen & there, relay_k, FT, relay_v, FT, wide),
             ]
         for frame in (0, 1):
             row = frame * FT
             own = visible(info, slot, first + frame)
-            sources.append((own, key_any, row, value_any, row))
+            sources.append((own, key_any, row, value_any, row, wide))
             behind = visible(info, slot, first - 2 + frame)
-            sources.append((behind, near_k, row, near_v, row))
+            sources.append((behind, near_k, row, near_v, row, wide))
         one = (k_buf.at[0, :, :HD], v_buf.at[0, :, :HD])
 
         def sweep(step):
             def visit(t, carry):
                 seen = False
-                for n, (shown, k, k_row, v, v_row) in enumerate(sources):
+                for n, (shown, k, k_row, v, v_row, where) in enumerate(sources):
                     chosen = (t == n) & shown
                     seen = seen | chosen
 
@@ -288,7 +293,7 @@
                     def _():
                         for n, (ref, row) in enumerate(((k, k_row), (v, v_row))):
                             copy = pltpu.make_async_copy(
-                                ref.at[pl.ds(row, FT), wide], one[n], sem.at[0, n]
+                                ref.at[pl.ds(row, FT), where], one[n], sem.at[0, n]
                             )
                             copy.start()
                             copy.wait()
@@ -328,7 +333,7 @@
 
     def check(h, column, wide):
         for slot in (0, 1):
-            pl.when(too_large[h, slot] > 0.0)(lambda slot=slot: again(slot, h, wide))
+            pl.when(too_large[h, slot] > 0.0)(lambda slot=slot: again(slot, h, column, wide))
 
     each_head(group, check)
 
@@ -357,25 +362,8 @@
     )(*arrays, *tokens)
 
 
-def small(kernel, scalars, arrays, tokens, rows):
-    width = arrays[0].shape[1]
-    n = len(arrays)
-
-    def run(scalars, *refs):
-        kernel(scalars, *refs[:n], refs[-1])
-
-    return pl.pallas_call(
-        run,
-        in_specs=[SMEM_SPEC] + [VMEM_SPEC] * n + [ANY_SPEC] * len(tokens),
-        out_specs=VMEM_SPEC,
-        out_shape=jax.ShapeDtypeStruct((rows, width), jnp.bfloat16),
-        compiler_params=PARAMS,
-        cost_estimate=COST,
-    )(jnp.reshape(scalars, (1,)).astype(jnp.int32), *arrays, *tokens)
-
-
-def pick(flag, taken, kept, tokens=()):
-    width = kept.shape[1]
+def pick(flag, taken, kept, tokens=(), columns=None):
+    column, width = columns or (0, kept.shape[1])
 
     def kernel(flag, taken, kept, *refs):
         out, sem = refs[-2:]
@@ -383,7 +371,8 @@
 
             @pl.when(flag[0] == value)
             def _():
-                copy = pltpu.make_async_copy(source.at[pl.ds(0, FT)], out, sem)
+                rows = source.at[pl.ds(0, FT), pl.ds(column, width)]
+                copy = pltpu.make_async_copy(rows, out, sem)
                 copy.start()
                 copy.wait()
 
@@ -398,12 +387,32 @@
     )(jnp.reshape(flag, (1,)).astype(jnp.int32), taken, kept, *tokens)
 
 
-def last_frames(keys, values, tokens=()):
-    def kernel(_, keys, values, out):
-        out[:FT, :] = keys[FT:, :]
-        out[FT:, :] = values[FT:, :]
-
-    return small(kernel, jnp.zeros((), jnp.int32), [keys, values], tokens, 2 * FT)
+def last_frames(group, keys, values, tokens=()):
+    columns = pl.ds(group[0] * HD, group[1] * HD)
+    n = len(tokens)
+
+    def kernel(keys, values, *refs):
+        out, sem = refs[n:]
+        started = [
+            pltpu.make_async_copy(
+                source.at[pl.ds(FT, FT), columns], out.at[pl.ds(i * FT, FT)], sem.at[i]
+            )
+            for i, source in enumerate((keys, values))
+        ]
+        for copy in started:
+            copy.start()
+        for copy in started:
+            copy.wait()
+
+    return pl.pallas_call(
+        kernel,
+        in_specs=[ANY_SPEC] * (2 + n),
+        out_specs=VMEM_SPEC,
+        out_shape=jax.ShapeDtypeStruct((2 * FT, group[1] * HD), jnp.bfloat16),
+        scratch_shapes=[pltpu.SemaphoreType.DMA((2,))],
+        compiler_params=PARAMS,
+        cost_estimate=COST,
+    )(keys, values, *tokens)
 
 
 def sink_steps(size):
@@ -488,49 +497,51 @@
             frame_buffers + [dma_sems], NEAR_COST,
         )
 
+    def flag_of(pairs):
+        takes = jnp.zeros((), bool)
+        for _, target in pairs:
+            takes = takes | (me == target)
+        return takes
+
     states = []
-    steps = sink_steps(size)
+    *steps, last_step = sink_steps(size)
     for step, pairs in enumerate(steps):
         moved = lax.ppermute(held, axis, pairs)
-        takes = jnp.zeros((), bool)
         tokens = []
-        for _, target in pairs:
-            takes = takes | (me == target)
         if step < len(groups):
-            more, acc, sums, token = stage(
+            *state, token = stage(
                 functools.partial(own_kernel, groups[step]),
                 [info, query_states, key_states, value_states], 0,
-                [more_like, acc_like, sums_like, TOKEN], [],
-                tokens=[held] * (step > 0),
+                [more_like, acc_like, sums_like, TOKEN], [], tokens=[held] * (step > 0),
             )
-            states.append((more, acc, sums))
+            states.append(state)
             tokens.append(token)
-            if step == 1:
-                tokens += [near_k, near_v]
-            if step == len(groups) - 1:
-                own_last = last_frames(key_states, value_states, [token])
-                far = lax.ppermute(own_last, axis, [(i, i + 2) for i in range(0, size - 2, 2)])
-        if step == len(steps) - 1:
-            *sums_now, token = near_stage(groups[0], states[0])
-            states[0] = states[0][0], *sums_now
-            tokens += [token, far]
-        held = pick(takes, moved, held, tokens)
-    other = lax.ppermute(held, axis, [(i, i ^ 1) for i in range(size)])
+        if step < len(steps) - 1:
+            held = pick(flag_of(pairs), moved, held, tokens)
+
     on_chip = [(i, i + 1) for i in range(0, size, 2)]
     relay_k = lax.ppermute(near_k, axis, on_chip)
     relay_v = lax.ppermute(near_v, axis, on_chip)
-
-    for g, group in enumerate(groups[1:], 1):
-        *sums_now, _ = near_stage(group, states[g])
-        states[g] = states[g][0], *sums_now
+    own_done, arrivals = tokens, [near_k, near_v]
     mine, theirs = [], []
     for g, group in enumerate(groups):
-        part = jax.ShapeDtypeStruct((FT if paired else rows, group_width), jnp.bfloat16)
+        columns = group[0] * HD, group[1] * HD
+        own_last = last_frames(group, key_states, value_states, own_done)
+        far = lax.ppermute(own_last, axis, [(i, i + 2) for i in range(0, size - 2, 2)])
+        part = pick(flag_of(steps[-1]), moved, held, own_done + arrivals, columns)
+        arriving = lax.ppermute(part, axis, last_step)
+        more = states[g][0]
+        *sums_now, token = near_stage(group, states[g])
+        states[g] = more, *sums_now
+        part = pick(flag_of(last_step), arriving, part, [token, far] + mine)
+        own_done, arrivals = [part], []
+        other = lax.ppermute(part, axis, [(i, i ^ 1) for i in range(size)])
+        out = jax.ShapeDtypeStruct((FT if paired else rows, group_width), jnp.bfloat16)
         results = stage(
             functools.partial(final_kernel, group),
-            [info, query_states, *states[g], held, other, far, relay_k, relay_v,
+            [info, query_states, *states[g], part, other, far, relay_k, relay_v,
              key_states, value_states, near_k, near_v], 9,
-            [part] * (2 if paired else 1),
+            [out] * (2 if paired else 1),
             frame_buffers + [
                 pltpu.VMEM((rows, 2 * HD), jnp.float32),
                 pltpu.VMEM((FT, 2 * HD), jnp.float32),

time: 128 us -> 126 us (0.984)
  the two profiles are of different devices: /device:TPU:18 before, /device:TPU:0 now
where the time goes in v4:
time: 126 us
  Pallas kernels  58.2 us (46%)
  starting transfers between devices  38.9 us (31%)
  waiting for transfers between devices  18.9 us (15%)
  local copies, waits for them, and re-layouts  9.35 us (7%)
    pallas_call x6, Pallas kernels, stage(): pl.pallas_call(run, in_specs=[SMEM_SPEC] + [VMEM_SPEC] * (n - in_any - 1)...  46.4 us
    ppermute x2, waiting for transfers between devices, local(): theirs.append(lax.ppermute(results[1], 'head', [(0, 1), (1, 0)]))  10.3 us
    unnamed x46, local copies, waits for them, and re-layouts  9.27 us
    ppermute x2, starting transfers between devices, local(): lax.ppermute(own_last, axis, [(i, i + 2) for i in range(0, size - 2, 2)])  8.92 us
    ppermute x2, starting transfers between devices, local(): moved = lax.ppermute(held, axis, pairs)  6.57 us
    ppermute x2, starting transfers between devices, local(): arriving = lax.ppermute(part, axis, last_step)  6.29 us
    pallas_call x6, Pallas kernels, pick(): pl.pallas_call(kernel, in_specs=[SMEM_SPEC] + [ANY_SPEC] * (2 + len(token...  5.58 us
    pallas_call x1, Pallas kernels, project(): pl.pallas_call(kernel, grid=(turns,), in_specs=[SMEM_SPEC] + [VMEM_SPEC]...  5.15 us
  transfers between devices with their start and end apart: 15, of which 4 were waited for; matrix products, arithmetic and copies ran while one was open for 0% of the time, Pallas kernels for 42%

profile of v4, /device:TPU:0, one launch (start us, length us, event | category | flops | bytes accessed | tf_op | source)
XLA Modules:
  0.0 125.8 jit_solution(16415937471076918637)
XLA Ops:
  0.0 2.4 %collective-permute-start.2 = (bf16[1536,512]{1,0:T(8,128)(2,1)}, bf16[1536,512]{1,0:T(8,128)(2,1)S(1)}, u32[]{:S(2)}, u32[]{:S(2)}) collective-permute-start(bf16[1536,512]{1,0:T(8,128)(2,1)} %refs_11_.3), channel_id=1, source_target_pairs={{0,2},{1,3}} | collective-permute-start | bytes 4718600 | tf_op jit(solution)/shard_map/ppermute | solution.py:490
  2.5 2.5 %collective-permute-start = (bf16[1536,512]{1,0:T(8,128)(2,1)}, bf16[1536,512]{1,0:T(8,128)(2,1)}, u32[]{:S(2)}, u32[]{:S(2)}) collective-permute-start(bf16[1536,512]{1,0:T(8,128)(2,1)} %refs_10_.3), channel_id=1, source_target_pairs={{0,2},{2,4},{4,6},{6,8},{8,10},{10,12},{12,14},{14,16},{16,18},{18... | collective-permute-start | bytes 4718600 | tf_op jit(solution)/shard_map/ppermute | solution.py:488
  4.9 3.9 %collective-permute-start.1 = (bf16[1536,512]{1,0:T(8,128)(2,1)}, bf16[1536,512]{1,0:T(8,128)(2,1)}, u32[]{:S(2)}, u32[]{:S(2)}) collective-permute-start(bf16[1536,512]{1,0:T(8,128)(2,1)} %refs_11_.3), channel_id=1, source_target_pairs={{0,2},{2,4},{4,6},{6,8},{8,10},{10,12},{12,14},{14,16},{16,18},{18... | collective-permute-start | bytes 4718600 | tf_op jit(solution)/shard_map/ppermute | solution.py:489
  13.7 4.4 %collective-permute-start.3 = (bf16[768,512]{1,0:T(8,128)(2,1)}, bf16[768,512]{1,0:T(8,128)(2,1)}, u32[]{:S(2)}, u32[]{:S(2)}) collective-permute-start(bf16[768,512]{1,0:T(8,128)(2,1)} %shard_map.66.kept), channel_id=1, source_target_pairs={{0,16},{2,18},{1,17},{3,19}} | collective-permute-start | bytes 2359304 | tf_op jit(solution)/shard_map/ppermute | solution.py:509
  19.6 7.4 %shard_map.64 = (bf16[1536,256]{1,0:T(8,128)(2,1)S(1)}, f32[1536,256]{1,0:T(8,128)S(1)}, f32[1536,128]{1,0:T(8,128)S(1)}, f32[8,128]{1,0:T(8,128)S(1)}) custom-call(s32[7]{0:T(128)S(1)} %concatenate.3.refs_0_.info, bf16[1536,512]{1,0:T(8,128)(2,1)S(1)} %copy-done.3, bf16[1536,512]{1,0:T(8,128)(2,1)S(1)} %copy-done.1, bf16[1536,512]{1,0:T(8,128)(2,1)S(1)} %copy-done.2), custom_call_target="tpu_custom_call" | custom-call | flops 1000 | bytes 1000 | tf_op jit(solution)/shard_map/pallas_call | solution.py:351
  30.0 4.5 %collective-permute-done.3.taken = bf16[768,512]{1,0:T(8,128)(2,1)} collective-permute-done((bf16[768,512]{1,0:T(8,128)(2,1)}, bf16[768,512]{1,0:T(8,128)(2,1)}, u32[]{:S(2)}, u32[]{:S(2)}) %collective-permute-start.3) | collective-permute-done | bytes 786464 | tf_op jit(solution)/shard_map/ppermute | solution.py:509
  34.5 2.0 %shard_map.67.refs_4_.kept = bf16[768,512]{1,0:T(8,128)(2,1)} custom-call(s32[1]{0:T(128)} %bitcast.5.flag, bf16[768,512]{1,0:T(8,128)(2,1)} %collective-permute-done.3.taken, bf16[768,512]{1,0:T(8,128)(2,1)} %shard_map.66.kept, f32[8,128]{1,0:T(8,128)S(1)} %get-tuple-element.28.refs_0_), custom_call_target="tpu_custom_call" | custom-call | flops 1000 | bytes 1000 | tf_op jit(solution)/shard_map/pallas_call | solution.py:379
  36.6 2.2 %collective-permute-start.4 = (bf16[768,512]{1,0:T(8,128)(2,1)}, bf16[768,512]{1,0:T(8,128)(2,1)}, u32[]{:S(2)}, u32[]{:S(2)}) collective-permute-start(bf16[768,512]{1,0:T(8,128)(2,1)} %shard_map.67.refs_4_.kept), channel_id=1, source_target_pairs={{0,8},{16,24},{2,10},{18,26},{1,9},{17,25},{3,11},{19,27}} | collective-permute-start | bytes 2359304 | tf_op jit(solution)/shard_map/ppermute | solution.py:509
  38.8 2.4 %collective-permute-start.8 = (bf16[1536,512]{1,0:T(8,128)(2,1)}, bf16[1536,512]{1,0:T(8,128)(2,1)}, u32[]{:S(2)}, u32[]{:S(2)}) collective-permute-start(bf16[1536,512]{1,0:T(8,128)(2,1)} %collective-permute-done.refs_5_.refs_1_.refs_12_), channel_id=1, source_target_pairs={{0,2},{4,6},{8,10},{12,14},{16,18},{20,22},{24,26},{28,30},{1,3},{... | collective-permute-start | bytes 4718600 | tf_op jit(solution)/shard_map/ppermute | solution.py:523
  41.2 2.5 %collective-permute-start.9 = (bf16[1536,512]{1,0:T(8,128)(2,1)}, bf16[1536,512]{1,0:T(8,128)(2,1)}, u32[]{:S(2)}, u32[]{:S(2)}) collective-permute-start(bf16[1536,512]{1,0:T(8,128)(2,1)} %collective-permute-done.1.refs_6_.refs_2_.refs_13_), channel_id=1, source_target_pairs={{0,2},{4,6},{8,10},{12,14},{16,18},{20,22},{24,26},{28,30},{1,3},{... | collective-permute-start | bytes 4718600 | tf_op jit(solution)/shard_map/ppermute | solution.py:524
  43.7 7.4 %shard_map.68 = (bf16[1536,256]{1,0:T(8,128)(2,1)S(1)}, f32[1536,256]{1,0:T(8,128)S(1)}, f32[1536,128]{1,0:T(8,128)S(1)}, f32[8,128]{1,0:T(8,128)S(1)}) custom-call(s32[7]{0:T(128)S(1)} %concatenate.3.refs_0_.info, bf16[1536,512]{1,0:T(8,128)(2,1)S(1)} %copy-done.4, bf16[1536,512]{1,0:T(8,128)(2,1)S(1)} %copy-done.1, bf16[1536,512]{1,0:T(8,128)(2,1)S(1)} %copy-done.2, ...), custom_call_target="tpu_custom_call" | custom-call | flops 1000 | bytes 1000 | tf_op jit(solution)/shard_map/pallas_call | solution.py:351
  53.0 4.2 %collective-permute-start.6 = (bf16[1536,256]{1,0:T(8,128)(2,1)}, bf16[1536,256]{1,0:T(8,128)(2,1)}, u32[]{:S(2)}, u32[]{:S(2)}) collective-permute-start(bf16[1536,256]{1,0:T(8,128)(2,1)} %shard_map.70), channel_id=1, source_target_pairs={{0,4},{4,8},{8,12},{12,16},{16,20},{20,24},{24,28},{1,5},{5,9},{9,... | collective-permute-start | bytes 2359304 | tf_op jit(solution)/shard_map/ppermute | solution.py:530
  58.4 3.7 %collective-permute-start.5 = (bf16[768,256]{1,0:T(8,128)(2,1)S(1)}, bf16[768,256]{1,0:T(8,128)(2,1)S(1)}, u32[]{:S(2)}, u32[]{:S(2)}) collective-permute-start(bf16[768,256]{1,0:T(8,128)(2,1)S(1)} %shard_map.69.kept), channel_id=1, source_target_pairs={{0,4},{8,12},{16,20},{24,28},{2,6},{10,14},{18,22},{26,30},{1,5},{... | collective-permute-start | bytes 1179656 | tf_op jit(solution)/shard_map/ppermute | solution.py:532
  62.1 7.9 %shard_map.65 = (f32[1536,256]{1,0:T(8,128)S(1)}, f32[1536,128]{1,0:T(8,128)S(1)}, f32[8,128]{1,0:T(8,128)S(1)}) custom-call(s32[7]{0:T(128)S(1)} %concatenate.3.refs_0_.info, bf16[1536,512]{1,0:T(8,128)(2,1)S(1)} %copy-done.5, bf16[1536,256]{1,0:T(8,128)(2,1)S(1)} %copy-done.10, f32[1536,256]{1,0:T(8,128)S(1)} %copy-done.14, f32[1536,128]{1,0:T(8,128)S(1)} %copy-done.18, ...), custom_call_target="tpu_custom_call" | custom-call | flops 8000000000 | bytes 1000 | tf_op jit(solution)/shard_map/pallas_call | solution.py:351
  70.1 4.1 %collective-permute-done.5.taken = bf16[768,256]{1,0:T(8,128)(2,1)S(1)} collective-permute-done((bf16[768,256]{1,0:T(8,128)(2,1)S(1)}, bf16[768,256]{1,0:T(8,128)(2,1)S(1)}, u32[]{:S(2)}, u32[]{:S(2)}) %collective-permute-start.5) | collective-permute-done | bytes 393248 | tf_op jit(solution)/shard_map/ppermute | solution.py:532
  74.5 4.7 %collective-permute-start.11 = (bf16[1536,256]{1,0:T(8,128)(2,1)S(1)}, bf16[1536,256]{1,0:T(8,128)(2,1)S(1)}, u32[]{:S(2)}, u32[]{:S(2)}) collective-permute-start(bf16[1536,256]{1,0:T(8,128)(2,1)S(1)} %shard_map.75), channel_id=1, source_target_pairs={{0,4},{4,8},{8,12},{12,16},{16,20},{20,24},{24,28},{1,5},{5,9},{9,... | collective-permute-start | bytes 2359304 | tf_op jit(solution)/shard_map/ppermute | solution.py:530
  80.3 2.6 %collective-permute-start.10 = (bf16[768,256]{1,0:T(8,128)(2,1)S(1)}, bf16[768,256]{1,0:T(8,128)(2,1)S(1)}, u32[]{:S(2)}, u32[]{:S(2)}) collective-permute-start(bf16[768,256]{1,0:T(8,128)(2,1)S(1)} %shard_map.74.kept), channel_id=1, source_target_pairs={{0,4},{8,12},{16,20},{24,28},{2,6},{10,14},{18,22},{26,30},{1,5},{... | collective-permute-start | bytes 1179656 | tf_op jit(solution)/shard_map/ppermute | solution.py:532
  82.9 7.9 %shard_map.73 = (f32[1536,256]{1,0:T(8,128)S(1)}, f32[1536,128]{1,0:T(8,128)S(1)}, f32[8,128]{1,0:T(8,128)S(1)}) custom-call(s32[7]{0:T(128)S(1)} %concatenate.3.refs_0_.info, bf16[1536,512]{1,0:T(8,128)(2,1)S(1)} %copy-done.5, bf16[1536,256]{1,0:T(8,128)(2,1)S(1)} %copy-done.12, f32[1536,256]{1,0:T(8,128)S(1)} %copy-done.16, f32[1536,128]{1,0:T(8,128)S(1)} %copy-done.20, ...), custom_call_target="tpu_custom_call" | custom-call | flops 8000000000 | bytes 1000 | tf_op jit(solution)/shard_map/pallas_call | solution.py:351
  90.9 8.2 %shard_map.72 = (bf16[768,256]{1,0:T(8,128)(2,1)S(1)}, bf16[768,256]{1,0:T(8,128)(2,1)S(1)}) custom-call(s32[7]{0:T(128)S(1)} %concatenate.3.refs_0_.info, bf16[1536,512]{1,0:T(8,128)(2,1)S(1)} %copy-done.5, bf16[1536,256]{1,0:T(8,128)(2,1)S(1)} %copy-done.10, f32[1536,256]{1,0:T(8,128)S(1)} %get-tuple-element.26.refs_3_, ...), custom_call_target="tpu_custom_call" | custom-call | flops 1000 | bytes 1000 | tf_op jit(solution)/shard_map/pallas_call | solution.py:351
  99.6 1.5 %collective-permute-start.13 = (bf16[768,256]{1,0:T(8,128)(2,1)S(1)}, bf16[768,256]{1,0:T(8,128)(2,1)S(1)}, u32[]{:S(2)}, u32[]{:S(2)}) collective-permute-start(bf16[768,256]{1,0:T(8,128)(2,1)S(1)} %get-tuple-element.39), channel_id=1, source_target_pairs={{0,1},{1,0},{2,3},{3,2},{4,5},{5,4},{6,7},{7,6},{8,9},{9,8},{10,11... | collective-permute-start | bytes 1179656 | tf_op jit(solution)/shard_map/ppermute | solution.py:555
  101.2 7.6 %shard_map.77 = (bf16[768,256]{1,0:T(8,128)(2,1)S(1)}, bf16[768,256]{1,0:T(8,128)(2,1)S(1)}) custom-call(s32[7]{0:T(128)S(1)} %concatenate.3.refs_0_.info, bf16[1536,512]{1,0:T(8,128)(2,1)S(1)} %copy-done.5, bf16[1536,256]{1,0:T(8,128)(2,1)S(1)} %copy-done.12, f32[1536,256]{1,0:T(8,128)S(1)} %get-tuple-element.35.refs_3_, ...), custom_call_target="tpu_custom_call" | custom-call | flops 1000 | bytes 1000 | tf_op jit(solution)/shard_map/pallas_call | solution.py:351
  108.8 1.6 %collective-permute-start.14 = (bf16[768,256]{1,0:T(8,128)(2,1)S(1)}, bf16[768,256]{1,0:T(8,128)(2,1)S(1)}, u32[]{:S(2)}, u32[]{:S(2)}) collective-permute-start(bf16[768,256]{1,0:T(8,128)(2,1)S(1)} %get-tuple-element.40), channel_id=1, source_target_pairs={{0,1},{1,0},{2,3},{3,2},{4,5},{5,4},{6,7},{7,6},{8,9},{9,8},{10,11... | collective-permute-start | bytes 1179656 | tf_op jit(solution)/shard_map/ppermute | solution.py:555
  110.9 9.7 %collective-permute-done.14.refs_3_ = bf16[768,256]{1,0:T(8,128)(2,1)S(1)} collective-permute-done((bf16[768,256]{1,0:T(8,128)(2,1)S(1)}, bf16[768,256]{1,0:T(8,128)(2,1)S(1)}, u32[]{:S(2)}, u32[]{:S(2)}) %collective-permute-start.14) | collective-permute-done | bytes 393248 | tf_op jit(solution)/shard_map/ppermute | solution.py:555
  120.6 5.1 %shard_map.78 = bf16[768,1536]{1,0:T(8,128)(2,1)} custom-call(s32[7]{0:T(128)S(1)} %concatenate.3.refs_0_.info, bf16[768,256]{1,0:T(8,128)(2,1)S(1)} %get-tuple-element.31.refs_2_.refs_0_, bf16[768,256]{1,0:T(8,128)(2,1)S(1)} %get-tuple-element.38.refs_1_, bf16[768,256]{1,0:T(8,128)(2,1)S(1)} %collective-permute-done.13.refs_2_, ...), custom_call_target="tpu_custom_call" | custom-call | flops 1000 | bytes 1000 | tf_op jit(solution)/shard_map/pallas_call | solution.py:452
  (68 shorter events, 15.0 us)
Async XLA Ops:
  0.0 8.8 %collective-permute-start.2 = (bf16[1536,512]{1,0:T(8,128)(2,1)}, bf16[1536,512]{1,0:T(8,128)(2,1)S(1)}, u32[]{:S(2)}, u32[]{:S(2)}) collective-permute-start(bf16[1536,512]{1,0:T(8,128)(2,1)} %refs_11_.3), channel_id=1, source_target_pairs={{0,2},{1,3}} | collective-permute-start | bytes 4718600 | tf_op jit(solution)/shard_map/ppermute | solution.py:490
  2.5 36.3 %collective-permute-start = (bf16[1536,512]{1,0:T(8,128)(2,1)}, bf16[1536,512]{1,0:T(8,128)(2,1)}, u32[]{:S(2)}, u32[]{:S(2)}) collective-permute-start(bf16[1536,512]{1,0:T(8,128)(2,1)} %refs_10_.3), channel_id=1, source_target_pairs={{0,2},{2,4},{4,6},{6,8},{8,10},{10,12},{12,14},{14,16},{16,18},{18... | collective-permute-start | bytes 4718600 | tf_op jit(solution)/shard_map/ppermute | solution.py:488
  4.9 36.3 %collective-permute-start.1 = (bf16[1536,512]{1,0:T(8,128)(2,1)}, bf16[1536,512]{1,0:T(8,128)(2,1)}, u32[]{:S(2)}, u32[]{:S(2)}) collective-permute-start(bf16[1536,512]{1,0:T(8,128)(2,1)} %refs_11_.3), channel_id=1, source_target_pairs={{0,2},{2,4},{4,6},{6,8},{8,10},{10,12},{12,14},{14,16},{16,18},{18... | collective-permute-start | bytes 4718600 | tf_op jit(solution)/shard_map/ppermute | solution.py:489
  12.8 5.4 %copy-start.21 = (s32[2]{0:T(128)S(1)}, s32[2]{0:T(128)}, u32[]{:S(2)}) copy-start(s32[2]{0:T(128)} %param.9) | copy-start | bytes 28
  12.8 5.4 %copy-start.22 = (s32[2]{0:T(128)S(1)}, s32[2]{0:T(128)}, u32[]{:S(2)}) copy-start(s32[2]{0:T(128)} %param.10) | copy-start | bytes 28
  12.8 5.4 %copy-start.1 = (bf16[1536,512]{1,0:T(8,128)(2,1)S(1)}, bf16[1536,512]{1,0:T(8,128)(2,1)}, u32[]{:S(2)}) copy-start(bf16[1536,512]{1,0:T(8,128)(2,1)} %refs_10_.3) | copy-start | bytes 4718596
  12.8 5.4 %copy-start.2 = (bf16[1536,512]{1,0:T(8,128)(2,1)S(1)}, bf16[1536,512]{1,0:T(8,128)(2,1)}, u32[]{:S(2)}) copy-start(bf16[1536,512]{1,0:T(8,128)(2,1)} %refs_11_.3) | copy-start | bytes 4718596
  13.7 20.8 %collective-permute-start.3 = (bf16[768,512]{1,0:T(8,128)(2,1)}, bf16[768,512]{1,0:T(8,128)(2,1)}, u32[]{:S(2)}, u32[]{:S(2)}) collective-permute-start(bf16[768,512]{1,0:T(8,128)(2,1)} %shard_map.66.kept), channel_id=1, source_target_pairs={{0,16},{2,18},{1,17},{3,19}} | collective-permute-start | bytes 2359304 | tf_op jit(solution)/shard_map/ppermute | solution.py:509
  30.0 13.7 %copy-start.4 = (bf16[1536,512]{1,0:T(8,128)(2,1)S(1)}, bf16[1536,512]{1,0:T(8,128)(2,1)}, u32[]{:S(2)}) copy-start(bf16[1536,512]{1,0:T(8,128)(2,1)} %refs_1_.11) | copy-start | bytes 4718596
  36.6 20.6 %collective-permute-start.4 = (bf16[768,512]{1,0:T(8,128)(2,1)}, bf16[768,512]{1,0:T(8,128)(2,1)}, u32[]{:S(2)}, u32[]{:S(2)}) collective-permute-start(bf16[768,512]{1,0:T(8,128)(2,1)} %shard_map.67.refs_4_.kept), channel_id=1, source_target_pairs={{0,8},{16,24},{2,10},{18,26},{1,9},{17,25},{3,11},{19,27}} | collective-permute-start | bytes 2359304 | tf_op jit(solution)/shard_map/ppermute | solution.py:509
  38.8 52.1 %collective-permute-start.8 = (bf16[1536,512]{1,0:T(8,128)(2,1)}, bf16[1536,512]{1,0:T(8,128)(2,1)}, u32[]{:S(2)}, u32[]{:S(2)}) collective-permute-start(bf16[1536,512]{1,0:T(8,128)(2,1)} %collective-permute-done.refs_5_.refs_1_.refs_12_), channel_id=1, source_target_pairs={{0,2},{4,6},{8,10},{12,14},{16,18},{20,22},{24,26},{28,30},{1,3},{... | collective-permute-start | bytes 4718600 | tf_op jit(solution)/shard_map/ppermute | solution.py:523
  41.2 49.7 %collective-permute-start.9 = (bf16[1536,512]{1,0:T(8,128)(2,1)}, bf16[1536,512]{1,0:T(8,128)(2,1)}, u32[]{:S(2)}, u32[]{:S(2)}) collective-permute-start(bf16[1536,512]{1,0:T(8,128)(2,1)} %collective-permute-done.1.refs_6_.refs_2_.refs_13_), channel_id=1, source_target_pairs={{0,2},{4,6},{8,10},{12,14},{16,18},{20,22},{24,26},{28,30},{1,3},{... | collective-permute-start | bytes 4718600 | tf_op jit(solution)/shard_map/ppermute | solution.py:524
  53.0 17.1 %collective-permute-start.6 = (bf16[1536,256]{1,0:T(8,128)(2,1)}, bf16[1536,256]{1,0:T(8,128)(2,1)}, u32[]{:S(2)}, u32[]{:S(2)}) collective-permute-start(bf16[1536,256]{1,0:T(8,128)(2,1)} %shard_map.70), channel_id=1, source_target_pairs={{0,4},{4,8},{8,12},{12,16},{16,20},{20,24},{24,28},{1,5},{5,9},{9,... | collective-permute-start | bytes 2359304 | tf_op jit(solution)/shard_map/ppermute | solution.py:530
  58.4 15.7 %collective-permute-start.5 = (bf16[768,256]{1,0:T(8,128)(2,1)S(1)}, bf16[768,256]{1,0:T(8,128)(2,1)S(1)}, u32[]{:S(2)}, u32[]{:S(2)}) collective-permute-start(bf16[768,256]{1,0:T(8,128)(2,1)S(1)} %shard_map.69.kept), channel_id=1, source_target_pairs={{0,4},{8,12},{16,20},{24,28},{2,6},{10,14},{18,22},{26,30},{1,5},{... | collective-permute-start | bytes 1179656 | tf_op jit(solution)/shard_map/ppermute | solution.py:532
  74.4 8.6 %copy-start.20 = (f32[1536,128]{1,0:T(8,128)S(1)}, f32[1536,128]{1,0:T(8,128)}, u32[]{:S(2)}) copy-start(f32[1536,128]{1,0:T(8,128)} %copy-done.19) | copy-start | bytes 2359300
  74.4 8.5 %copy-start.12 = (bf16[1536,256]{1,0:T(8,128)(2,1)S(1)}, bf16[1536,256]{1,0:T(8,128)(2,1)}, u32[]{:S(2)}) copy-start(bf16[1536,256]{1,0:T(8,128)(2,1)} %copy-done.11) | copy-start | bytes 2359300
  74.5 8.5 %copy-start.16 = (f32[1536,256]{1,0:T(8,128)S(1)}, f32[1536,256]{1,0:T(8,128)}, u32[]{:S(2)}) copy-start(f32[1536,256]{1,0:T(8,128)} %copy-done.15) | copy-start | bytes 4718596
  74.5 24.7 %collective-permute-start.11 = (bf16[1536,256]{1,0:T(8,128)(2,1)S(1)}, bf16[1536,256]{1,0:T(8,128)(2,1)S(1)}, u32[]{:S(2)}, u32[]{:S(2)}) collective-permute-start(bf16[1536,256]{1,0:T(8,128)(2,1)S(1)} %shard_map.75), channel_id=1, source_target_pairs={{0,4},{4,8},{8,12},{12,16},{16,20},{20,24},{24,28},{1,5},{5,9},{9,... | collective-permute-start | bytes 2359304 | tf_op jit(solution)/shard_map/ppermute | solution.py:530
  79.2 11.7 %collective-permute-start.7 = (bf16[768,256]{1,0:T(8,128)(2,1)S(1)}, bf16[768,256]{1,0:T(8,128)(2,1)S(1)}, u32[]{:S(2)}, u32[]{:S(2)}) collective-permute-start(bf16[768,256]{1,0:T(8,128)(2,1)S(1)} %shard_map.71.refs_5_.refs_0_), channel_id=1, source_target_pairs={{0,2},{2,0},{4,6},{6,4},{8,10},{10,8},{12,14},{14,12},{16,18},{18,... | collective-permute-start | bytes 1179656 | tf_op jit(solution)/shard_map/ppermute | solution.py:538
  80.3 18.8 %collective-permute-start.10 = (bf16[768,256]{1,0:T(8,128)(2,1)S(1)}, bf16[768,256]{1,0:T(8,128)(2,1)S(1)}, u32[]{:S(2)}, u32[]{:S(2)}) collective-permute-start(bf16[768,256]{1,0:T(8,128)(2,1)S(1)} %shard_map.74.kept), channel_id=1, source_target_pairs={{0,4},{8,12},{16,20},{24,28},{2,6},{10,14},{18,22},{26,30},{1,5},{... | collective-permute-start | bytes 1179656 | tf_op jit(solution)/shard_map/ppermute | solution.py:532
  99.4 1.8 %collective-permute-start.12 = (bf16[768,256]{1,0:T(8,128)(2,1)S(1)}, bf16[768,256]{1,0:T(8,128)(2,1)S(1)}, u32[]{:S(2)}, u32[]{:S(2)}) collective-permute-start(bf16[768,256]{1,0:T(8,128)(2,1)S(1)} %shard_map.76.refs_5_), channel_id=1, source_target_pairs={{0,2},{2,0},{4,6},{6,4},{8,10},{10,8},{12,14},{14,12},{16,18},{18,... | collective-permute-start | bytes 1179656 | tf_op jit(solution)/shard_map/ppermute | solution.py:538
  99.6 11.3 %collective-permute-start.13 = (bf16[768,256]{1,0:T(8,128)(2,1)S(1)}, bf16[768,256]{1,0:T(8,128)(2,1)S(1)}, u32[]{:S(2)}, u32[]{:S(2)}) collective-permute-start(bf16[768,256]{1,0:T(8,128)(2,1)S(1)} %get-tuple-element.39), channel_id=1, source_target_pairs={{0,1},{1,0},{2,3},{3,2},{4,5},{5,4},{6,7},{7,6},{8,9},{9,8},{10,11... | collective-permute-start | bytes 1179656 | tf_op jit(solution)/shard_map/ppermute | solution.py:555
  101.2 19.5 %copy-start.6 = (bf16[1024,1536]{1,0:T(8,128)(2,1)S(1)}, bf16[1024,1536]{1,0:T(8,128)(2,1)}, u32[]{:S(2)}) copy-start(bf16[1024,1536]{1,0:T(8,128)(2,1)} %refs_4_.1) | copy-start | bytes 9437188
  108.8 11.8 %collective-permute-start.14 = (bf16[768,256]{1,0:T(8,128)(2,1)S(1)}, bf16[768,256]{1,0:T(8,128)(2,1)S(1)}, u32[]{:S(2)}, u32[]{:S(2)}) collective-permute-start(bf16[768,256]{1,0:T(8,128)(2,1)S(1)} %get-tuple-element.40), channel_id=1, source_target_pairs={{0,1},{1,0},{2,3},{3,2},{4,5},{5,4},{6,7},{7,6},{8,9},{9,8},{10,11... | collective-permute-start | bytes 1179656 | tf_op jit(solution)/shard_map/ppermute | solution.py:555
  (14 other events, 32.6 us)
